TPU v7x, 32 devices: a whole 2x2x4 slice. The times are simulated.
32 devices in a mesh: dp: 16 (over z, y, core), tensor: 2 (over x).
Axes of the slice: x: 2, y: 2, z: 4, core: 2. Of those that a mesh axis runs over, the one named last changes fastest.
Arguments:
- tokens: bfloat16 [2048, 2048], P('dp'), may hold values from -6 to 6
- cotangent: bfloat16 [2048, 2048], P('dp'), may hold values from -6 to 6
- lengths: int32 [16, 8], P('dp'), may hold values from 1 to 96, 128 in all within a row
- route: int32 [16, 128], P('dp'), may hold values from 0 to 127, each once within a row
- place: int32 [16, 128], P('dp'), may hold values from 0 to 127, each once within a row
- gain_one: bfloat16 [2048], P('dp'), may hold values from 0.5 to 1.5
- w_in: bfloat16 [2048, 2, 4096], P(None, None, ('dp', 'tensor')), may hold values from -0.125 to 0.125
- conv_w: bfloat16 [4, 4096], P(None, ('dp', 'tensor')), may hold values from -3 to 3
- conv_bias: bfloat16 [4096], P(('dp', 'tensor')), may hold values from -3 to 3
- w_x: bfloat16 [4096, 160], P(('dp', 'tensor')), may hold values from -0.09375 to 0.09375
- w_dt: bfloat16 [128, 4096], P(None, ('dp', 'tensor')), may hold values from -0.5 to 0.5
- dt_bias: bfloat16 [4096], P(('dp', 'tensor')), may hold values from -6 to -1
- a_log: bfloat16 [16, 4096], P(None, ('dp', 'tensor')), may hold values from -2 to 2.765625
- skip: bfloat16 [4096], P(('dp', 'tensor')), may hold values from 0.5 to 1.5
- w_out: bfloat16 [4096, 2048], P(('dp', 'tensor')), may hold values from -0.09375 to 0.09375
- gain_three: bfloat16 [2048], P('dp'), may hold values from 0.5 to 1.5
- mlp_one_in: bfloat16 [2048, 2, 8192], P('dp', None, 'tensor'), may hold values from -0.125 to 0.125
- mlp_one_out: bfloat16 [8192, 2048], P('tensor', 'dp'), may hold values from -0.0625 to 0.0625
- gain_two: bfloat16 [2048], P('dp'), may hold values from 0.5 to 1.5
- w_qkv: bfloat16 [2048, 3, 2048], P('dp', None, 'tensor'), may hold values from -0.125 to 0.125
- w_o: bfloat16 [2048, 2048], P('tensor', 'dp'), may hold values from -0.25 to 0.25
- gain_four: bfloat16 [2048], P('dp'), may hold values from 0.5 to 1.5
- mlp_two_in: bfloat16 [2048, 2, 8192], P('dp', None, 'tensor'), may hold values from -0.125 to 0.125
- mlp_two_out: bfloat16 [8192, 2048], P('tensor', 'dp'), may hold values from -0.0625 to 0.0625
Outputs:
- output: float32 [2048, 2048], P('dp')
- input_grad: float32 [2048, 2048], P('dp')
- grad_gain_one: float32 [2048], P('dp')
- grad_w_in: float32 [2048, 2, 4096], P(None, None, ('dp', 'tensor'))
- grad_conv_w: float32 [4, 4096], P(None, ('dp', 'tensor'))
- grad_conv_bias: float32 [4096], P(('dp', 'tensor'))
- grad_w_x: float32 [4096, 160], P(('dp', 'tensor'))
- grad_w_dt: float32 [128, 4096], P(None, ('dp', 'tensor'))
- grad_dt_bias: float32 [4096], P(('dp', 'tensor'))
- grad_a_log: float32 [16, 4096], P(None, ('dp', 'tensor'))
- grad_skip: float32 [4096], P(('dp', 'tensor'))
- grad_w_out: float32 [4096, 2048], P(('dp', 'tensor'))
- grad_gain_three: float32 [2048], P('dp')
- grad_mlp_one_in: float32 [2048, 2, 8192], P('dp', None, 'tensor')
- grad_mlp_one_out: float32 [8192, 2048], P('tensor', 'dp')
- grad_gain_two: float32 [2048], P('dp')
- grad_w_qkv: float32 [2048, 3, 2048], P('dp', None, 'tensor')
- grad_w_o: float32 [2048, 2048], P('tensor', 'dp')
- grad_gain_four: float32 [2048], P('dp')
- grad_mlp_two_in: float32 [2048, 2, 8192], P('dp', None, 'tensor')
- grad_mlp_two_out: float32 [8192, 2048], P('tensor', 'dp')
Inputs may be any that keep to these rules, and one draw needn't show every extreme that they name: `route`: each device's row is a permutation of its local rows; entries k * 8 to k * 8 + 7 name the rows it sends to index k of dp. Each device's row is a permutation of the rows it receives, numbered by sending index of dp and then by their place in the sender's slot. Each device's 8 lengths sum to 128.
All inputs are finite; a program needn't handle non-finite values.
Results may differ from a plain program's by a relative error of at most 0.02.
Values may be sent and summed in bfloat16 or wider, within the bound.
No kernel may reach another device: no remote copies, remote signals or barrier semaphores. Data moves between devices by JAX's collectives and lax.ppermute only.
A program may use at most 512 MiB of HBM per device.

v0:
```python
import jax
import jax.numpy as jnp
from jax import lax
from jax.sharding import PartitionSpec as P

N = 16
R = 128
K = 4
HD = 64
BLOCK = 16


eps = 1e-05


def silu_slope(operand):
    sig_value = jax.nn.sigmoid(operand)
    return sig_value * (1.0 + operand * (1.0 - sig_value))


def seq_layout(lens_row, row_count):
    seq_ends = jnp.cumsum(lens_row)
    begins = seq_ends - lens_row
    row_index = jnp.arange(row_count, dtype=jnp.int32)
    segment = jnp.sum((row_index[:, None] >= seq_ends[None, :]).astype(jnp.int32), axis=1)
    one_hot = (segment[:, None] == jnp.arange(lens_row.shape[0], dtype=jnp.int32)[None, :]).astype(
        jnp.int32
    )
    return (segment, row_index - jnp.sum(one_hot * begins[None, :], axis=1))


def norm_scale(stream):
    return lax.rsqrt(jnp.mean(stream * stream, axis=-1, keepdims=True) + eps)


def norm_backward(stream, rms_scale, gain_vec, grad_normed):
    weighted = grad_normed * gain_vec[None, :]
    inner_mean = jnp.mean(weighted * stream, axis=-1, keepdims=True)
    grad_stream = rms_scale * weighted - stream * rms_scale * rms_scale * rms_scale * inner_mean
    return (grad_stream, jnp.sum(grad_normed * stream * rms_scale, axis=0))


def branch_total(partial_value):
    return lax.psum(partial_value, "tensor")


def norm_grad_total(partial_value):
    return lax.psum(partial_value, "tensor")


def feed_weights(gain_vec, gate_up, down_proj):
    return (
        lax.all_gather(gain_vec, "dp", axis=0, tiled=True),
        lax.all_gather(gate_up, "dp", axis=0, tiled=True),
        lax.all_gather(down_proj, "dp", axis=1, tiled=True),
    )


def feed_forward(stream_in, gain_vec, gate_up, down_proj):
    row_count = stream_in.shape[0]
    model_width = stream_in.shape[1]
    hidden_width = gate_up.shape[2]
    scale_here = norm_scale(stream_in)
    normed = (stream_in * scale_here * gain_vec[None, :]).astype(jnp.bfloat16)
    pair = jnp.dot(
        normed, gate_up.reshape(model_width, 2 * hidden_width), preferred_element_type=jnp.float32
    ).reshape(row_count, 2, hidden_width)
    gate_part = pair[:, 0]
    up_part = pair[:, 1]
    hidden_low = (jax.nn.silu(gate_part) * up_part).astype(jnp.bfloat16)
    branch = branch_total(jnp.dot(hidden_low, down_proj, preferred_element_type=jnp.float32))
    return (stream_in + branch, (scale_here, normed, gate_part, up_part, hidden_low))


def feed_backward(grad_stream, stream_in, kept, gain_vec, gate_up, down_proj):
    scale_here, normed, gate_part, up_part, hidden_low = kept
    row_count = stream_in.shape[0]
    model_width = stream_in.shape[1]
    hidden_width = gate_up.shape[2]
    grad_low = grad_stream.astype(jnp.bfloat16)
    grad_down = jnp.einsum("tf,td->fd", hidden_low, grad_low, preferred_element_type=jnp.float32)
    grad_hidden = jnp.einsum("td,fd->tf", grad_low, down_proj, preferred_element_type=jnp.float32)
    grad_pair = jnp.stack(
        [grad_hidden * up_part * silu_slope(gate_part), grad_hidden * jax.nn.silu(gate_part)],
        axis=1,
    )
    grad_pair_low = grad_pair.astype(jnp.bfloat16).reshape(row_count, 2 * hidden_width)
    grad_gate_up = jnp.einsum(
        "td,tf->df", normed, grad_pair_low, preferred_element_type=jnp.float32
    ).reshape(model_width, 2, hidden_width)
    grad_normed = norm_grad_total(
        jnp.einsum(
            "tf,df->td",
            grad_pair_low,
            gate_up.reshape(model_width, 2 * hidden_width),
            preferred_element_type=jnp.float32,
        )
    )
    grad_norm_part, grad_gain = norm_backward(stream_in, scale_here, gain_vec, grad_normed)
    summed = (
        lax.psum_scatter(grad_gain, "dp", scatter_dimension=0, tiled=True),
        lax.psum_scatter(grad_gate_up, "dp", scatter_dimension=0, tiled=True),
        lax.psum_scatter(grad_down, "dp", scatter_dimension=1, tiled=True),
    )
    return (grad_stream + grad_norm_part, summed)


def delayed(values, places):
    return jnp.concatenate(
        [jnp.zeros((places,) + values.shape[1:], values.dtype), values[:-places]], axis=0
    )


def advanced(values, places):
    return jnp.concatenate(
        [values[places:], jnp.zeros((places,) + values.shape[1:], values.dtype)], axis=0
    )


def rotated(heads_in, cosine, sine_part):
    half_width = heads_in.shape[-1] // 2
    first_half = heads_in[..., :half_width]
    second_half = heads_in[..., half_width:]
    return jnp.concatenate(
        [
            first_half * cosine - second_half * sine_part,
            second_half * cosine + first_half * sine_part,
        ],
        axis=-1,
    )


def rotary(offset, head_dim):
    half_width = head_dim // 2
    inverse = 10000.0 ** (-jnp.arange(half_width, dtype=jnp.float32) / half_width)
    angle_table = offset.astype(jnp.float32)[:, None] * inverse[None, :]
    return (jnp.cos(angle_table)[:, None, :], jnp.sin(angle_table)[:, None, :])


def combine(earlier, latter):
    return (earlier[0] * latter[0], latter[0] * earlier[1] + latter[1])


def block_states(builder, inputs, state_shape, backwards):

    def local_step(carried, slices):
        decays, source = builder(slices)
        return ((decays * carried[0], decays * carried[1] + source), None)

    initial = (jnp.ones(state_shape, jnp.float32), jnp.zeros(state_shape, jnp.float32))
    block_ends, unused = lax.scan(local_step, initial, inputs, reverse=backwards)
    totals, reached = lax.associative_scan(combine, block_ends, reverse=backwards, axis=0)
    padding = jnp.zeros((1,) + tuple(state_shape[1:]), jnp.float32)
    if backwards:
        return jnp.concatenate([reached[1:], padding], axis=0)
    return jnp.concatenate([padding, reached[:-1]], axis=0)


def state_walk(builder, emitter, initial, inputs, side_inputs, backwards):

    def walk_step(carried, slices):
        decays, source = builder(slices[0])
        updated = decays * carried + source
        return (updated, emitter(carried, updated, decays, slices[0], slices[1]))

    unused, emitted = lax.scan(walk_step, initial, (inputs, side_inputs), reverse=backwards)
    return emitted


def shards(
    tokens,
    cotangent,
    lengths,
    route,
    place,
    gain_one,
    w_in,
    conv_w,
    conv_bias,
    w_x,
    w_dt,
    dt_bias,
    a_log,
    skip,
    w_out,
    gain_three,
    mlp_one_in,
    mlp_one_out,
    gain_two,
    w_qkv,
    w_o,
    gain_four,
    mlp_two_in,
    mlp_two_out,
):
    row_count = tokens.shape[0]
    model_width = tokens.shape[1]
    send_order = route[0]
    arrival = place[0]
    inbound, cot_packed = (
        lax.all_to_all(tokens[send_order], "dp", split_axis=0, concat_axis=0, tiled=True),
        lax.all_to_all(cotangent[send_order], "dp", split_axis=0, concat_axis=0, tiled=True),
    )
    stream = inbound[arrival].astype(jnp.float32)
    back_grad = cot_packed[arrival].astype(jnp.float32)
    segment, offset = seq_layout(lengths[0], row_count)
    keep_mask = (offset > 0).astype(jnp.float32)
    mamba_parts = (
        lax.all_gather(gain_one, "dp", axis=0, tiled=True),
        lax.all_gather(w_in, "dp", axis=2, tiled=True),
        lax.all_gather(conv_w, "dp", axis=1, tiled=True),
        lax.all_gather(conv_bias, "dp", axis=0, tiled=True),
        lax.all_gather(w_x, "dp", axis=0, tiled=True),
        lax.all_gather(w_dt, "dp", axis=1, tiled=True),
        lax.all_gather(dt_bias, "dp", axis=0, tiled=True),
        lax.all_gather(a_log, "dp", axis=1, tiled=True),
        lax.all_gather(skip, "dp", axis=0, tiled=True),
        lax.all_gather(w_out, "dp", axis=0, tiled=True),
    )
    gain_mamba = mamba_parts[0].astype(jnp.float32)
    channels = mamba_parts[1].shape[2]
    in_flat = mamba_parts[1].reshape(model_width, 2 * channels)
    conv_taps = mamba_parts[2].astype(jnp.float32)
    conv_shift = mamba_parts[3].astype(jnp.float32)
    select_proj = mamba_parts[4]
    step_proj = mamba_parts[5]
    step_bias = mamba_parts[6].astype(jnp.float32)
    decay_rate = -jnp.exp(mamba_parts[7].astype(jnp.float32))
    skip_gain = mamba_parts[8].astype(jnp.float32)
    out_proj = mamba_parts[9]
    scale_mamba = norm_scale(stream)
    normed_one = (stream * scale_mamba * gain_mamba[None, :]).astype(jnp.bfloat16)
    inner_pair = jnp.dot(normed_one, in_flat, preferred_element_type=jnp.float32).reshape(
        row_count, 2, channels
    )
    conv_input = inner_pair[:, 0]
    gate_input = inner_pair[:, 1]
    tap_valid = [(offset >= tap_index).astype(jnp.float32)[:, None] for tap_index in range(K)]
    conv_sum = conv_shift[None, :] + conv_taps[0][None, :] * conv_input
    for tap_index in range(1, K):
        conv_sum = (
            conv_sum
            + conv_taps[tap_index][None, :] * delayed(conv_input, tap_index) * tap_valid[tap_index]
        )
    mixer_low = jax.nn.silu(conv_sum).astype(jnp.bfloat16)
    mixer_val = mixer_low.astype(jnp.float32)
    selected = lax.psum(
        jnp.dot(mixer_low, select_proj, preferred_element_type=jnp.float32), "tensor"
    )
    step_low = selected[:, :R].astype(jnp.bfloat16)
    input_mat = selected[:, R : R + N]
    output_mat = selected[:, R + N :]
    step_pre = jnp.dot(step_low, step_proj, preferred_element_type=jnp.float32) + step_bias[None, :]
    stepsize = jax.nn.softplus(step_pre)
    block_count = row_count // BLOCK

    def by_step(values):
        return jnp.swapaxes(values.reshape((block_count, BLOCK) + values.shape[1:]), 0, 1)

    def by_token(values):
        return jnp.swapaxes(values, 0, 1).reshape((row_count,) + values.shape[2:])

    state_shape = (block_count, N, channels)
    scan_inputs = (by_step(stepsize), by_step(mixer_val), by_step(input_mat), by_step(keep_mask))

    def forward_terms(slices):
        step_now, mixer_now, input_now, keep_now = slices
        decays = jnp.exp(step_now[:, None, :] * decay_rate[None]) * keep_now[:, None, None]
        source = (step_now * mixer_now)[:, None, :] * input_now[:, :, None]
        return (decays, source)

    def emit_output(carried, updated, decays, slices, side_now):
        return jnp.sum(side_now[:, :, None] * updated, axis=1)

    block_init = block_states(forward_terms, scan_inputs, state_shape, False)
    scanned = by_token(
        state_walk(forward_terms, emit_output, block_init, scan_inputs, by_step(output_mat), False)
    )
    mixer_out = scanned + skip_gain[None, :] * mixer_val
    gate_value = jax.nn.silu(gate_input)
    gated_low = (mixer_out * gate_value).astype(jnp.bfloat16)
    mixer_branch = branch_total(jnp.dot(gated_low, out_proj, preferred_element_type=jnp.float32))
    stream_mid = stream + mixer_branch
    first_parts = feed_weights(gain_three, mlp_one_in, mlp_one_out)
    gain_first = first_parts[0].astype(jnp.float32)
    first_in = first_parts[1]
    first_out = first_parts[2]
    stream_ffn, kept_first = feed_forward(stream_mid, gain_first, first_in, first_out)
    attn_parts = (
        lax.all_gather(gain_two, "dp", axis=0, tiled=True),
        lax.all_gather(w_qkv, "dp", axis=0, tiled=True),
        lax.all_gather(w_o, "dp", axis=1, tiled=True),
    )
    gain_attn = attn_parts[0].astype(jnp.float32)
    inner_width = attn_parts[1].shape[2]
    head_count = inner_width // HD
    proj_flat = attn_parts[1].reshape(model_width, 3 * inner_width)
    attn_out = attn_parts[2]
    scale_attn = norm_scale(stream_ffn)
    normed_two = (stream_ffn * scale_attn * gain_attn[None, :]).astype(jnp.bfloat16)
    projected = jnp.dot(normed_two, proj_flat, preferred_element_type=jnp.float32).reshape(
        row_count, 3, head_count, HD
    )
    cosine, sine_part = rotary(offset, HD)
    factor = float(HD) ** (-0.5)
    query_low = (rotated(projected[:, 0], cosine, sine_part) * factor).astype(jnp.bfloat16)
    key_low = rotated(projected[:, 1], cosine, sine_part).astype(jnp.bfloat16)
    value_low = projected[:, 2].astype(jnp.bfloat16)
    row_index = jnp.arange(row_count, dtype=jnp.int32)
    allowed = (segment[:, None] == segment[None, :]) & (row_index[:, None] >= row_index[None, :])

    def masked_scores():
        raw_scores = jnp.einsum(
            "thd,shd->hts", query_low, key_low, preferred_element_type=jnp.float32
        )
        return jnp.where(allowed[None], raw_scores, -1e30)

    scores = masked_scores()
    row_top = jnp.max(scores, axis=-1, keepdims=True)
    log_total = row_top + jnp.log(jnp.sum(jnp.exp(scores - row_top), axis=-1, keepdims=True))
    attn_probs = jnp.exp(scores - log_total)
    context = jnp.einsum(
        "hts,shd->thd",
        attn_probs.astype(jnp.bfloat16),
        value_low,
        preferred_element_type=jnp.float32,
    )
    context_low = context.astype(jnp.bfloat16).reshape(row_count, inner_width)
    attn_branch = branch_total(jnp.dot(context_low, attn_out, preferred_element_type=jnp.float32))
    stream_attn = stream_ffn + attn_branch
    second_parts = feed_weights(gain_four, mlp_two_in, mlp_two_out)
    gain_second = second_parts[0].astype(jnp.float32)
    second_in = second_parts[1]
    second_out = second_parts[2]
    result, kept_second = feed_forward(stream_attn, gain_second, second_in, second_out)
    grad_attn_stream, second_sums = feed_backward(
        back_grad, stream_attn, kept_second, gain_second, second_in, second_out
    )
    grad_branch = grad_attn_stream.astype(jnp.bfloat16)
    grad_attn_out = jnp.einsum(
        "tf,td->fd", context_low, grad_branch, preferred_element_type=jnp.float32
    )
    grad_context = (
        jnp.einsum("td,fd->tf", grad_branch, attn_out, preferred_element_type=jnp.float32)
        .astype(jnp.bfloat16)
        .reshape(row_count, head_count, HD)
    )
    attn_probs = jnp.exp(masked_scores() - log_total)
    grad_probs = jnp.einsum(
        "thd,shd->hts", grad_context, value_low, preferred_element_type=jnp.float32
    )
    grad_values = jnp.einsum(
        "hts,thd->shd",
        attn_probs.astype(jnp.bfloat16),
        grad_context,
        preferred_element_type=jnp.float32,
    )
    grad_scores = (
        attn_probs * (grad_probs - jnp.sum(attn_probs * grad_probs, axis=-1, keepdims=True))
    ).astype(jnp.bfloat16)
    grad_query = (
        jnp.einsum("hts,shd->thd", grad_scores, key_low, preferred_element_type=jnp.float32)
        * factor
    )
    grad_key = jnp.einsum(
        "hts,thd->shd", grad_scores, query_low, preferred_element_type=jnp.float32
    )
    grad_proj = jnp.stack(
        [
            rotated(grad_query, cosine, -sine_part),
            rotated(grad_key, cosine, -sine_part),
            grad_values,
        ],
        axis=1,
    )
    grad_proj_low = grad_proj.astype(jnp.bfloat16).reshape(row_count, 3 * inner_width)
    grad_w_qkv = jnp.einsum(
        "td,tf->df", normed_two, grad_proj_low, preferred_element_type=jnp.float32
    ).reshape(model_width, 3, inner_width)
    grad_normed_two = norm_grad_total(
        jnp.einsum("tf,df->td", grad_proj_low, proj_flat, preferred_element_type=jnp.float32)
    )
    grad_norm_ffn, grad_gain_two = norm_backward(stream_ffn, scale_attn, gain_attn, grad_normed_two)
    grad_ffn_stream = grad_attn_stream + grad_norm_ffn
    attn_sums = (
        lax.psum_scatter(grad_gain_two, "dp", scatter_dimension=0, tiled=True),
        lax.psum_scatter(grad_w_qkv, "dp", scatter_dimension=0, tiled=True),
        lax.psum_scatter(grad_attn_out, "dp", scatter_dimension=1, tiled=True),
    )
    grad_mid, first_sums = feed_backward(
        grad_ffn_stream, stream_mid, kept_first, gain_first, first_in, first_out
    )
    grad_mixed = grad_mid.astype(jnp.bfloat16)
    grad_out_proj = jnp.einsum(
        "te,td->ed", gated_low, grad_mixed, preferred_element_type=jnp.float32
    )
    grad_gated = jnp.einsum("td,ed->te", grad_mixed, out_proj, preferred_element_type=jnp.float32)
    grad_scan_out = grad_gated * gate_value
    grad_gate_input = grad_gated * mixer_out * silu_slope(gate_input)

    def emit_previous(carried, updated, decays, slices, side_now):
        return carried

    prior_states = state_walk(forward_terms, emit_previous, block_init, scan_inputs, (), False)
    adjoint_inputs = (
        by_step(advanced(stepsize, 1)),
        by_step(advanced(keep_mask, 1)),
        by_step(grad_scan_out),
        by_step(output_mat),
    )

    def adjoint_terms(slices):
        step_next, keep_next, grad_now, output_now = slices
        decays = jnp.exp(step_next[:, None, :] * decay_rate[None]) * keep_next[:, None, None]
        return (decays, grad_now[:, None, :] * output_now[:, :, None])

    def emit_grads(carried, updated, decays, slices, side_now):
        grad_now = slices[2]
        step_now, mixer_now, input_now, keep_now = side_now[0]
        prior_state = side_now[1]
        own_decay = jnp.exp(step_now[:, None, :] * decay_rate[None]) * keep_now[:, None, None]
        drive_term = step_now * mixer_now
        current = own_decay * prior_state + drive_term[:, None, :] * input_now[:, :, None]
        through = updated * prior_state * own_decay
        along_input = jnp.sum(updated * input_now[:, :, None], axis=1)
        grad_step = jnp.sum(through * decay_rate[None], axis=1) + mixer_now * along_input
        return (
            grad_step,
            step_now * along_input,
            jnp.sum(updated * drive_term[:, None, :], axis=2),
            jnp.sum(grad_now[:, None, :] * current, axis=2),
            jnp.sum(through * step_now[:, None, :], axis=0),
        )

    adjoint_init = block_states(adjoint_terms, adjoint_inputs, state_shape, True)
    grad_parts = state_walk(
        adjoint_terms, emit_grads, adjoint_init, adjoint_inputs, (scan_inputs, prior_states), True
    )
    grad_stepsize = by_token(grad_parts[0])
    grad_mixer = by_token(grad_parts[1]) + skip_gain[None, :] * grad_scan_out
    grad_input_mat = by_token(grad_parts[2])
    grad_output_mat = by_token(grad_parts[3])
    grad_a_log = jnp.sum(grad_parts[4], axis=0) * decay_rate
    grad_skip = jnp.sum(grad_scan_out * mixer_val, axis=0)
    grad_step_low = (grad_stepsize * jax.nn.sigmoid(step_pre)).astype(jnp.bfloat16)
    grad_dt_bias = jnp.sum(grad_step_low.astype(jnp.float32), axis=0)
    grad_w_dt = jnp.einsum("tr,te->re", step_low, grad_step_low, preferred_element_type=jnp.float32)
    grad_step_in = jnp.einsum(
        "te,re->tr", grad_step_low, step_proj, preferred_element_type=jnp.float32
    )
    grad_selected = lax.psum(
        jnp.concatenate([grad_step_in, grad_input_mat, grad_output_mat], axis=1), "tensor"
    ).astype(jnp.bfloat16)
    grad_w_x = jnp.einsum("te,tp->ep", mixer_low, grad_selected, preferred_element_type=jnp.float32)
    grad_mixer = grad_mixer + jnp.einsum(
        "tp,ep->te", grad_selected, select_proj, preferred_element_type=jnp.float32
    )
    grad_conv = grad_mixer * silu_slope(conv_sum)
    grad_conv_bias = jnp.sum(grad_conv, axis=0)
    tap_grads = [jnp.sum(grad_conv * conv_input, axis=0)]
    grad_conv_input = conv_taps[0][None, :] * grad_conv
    for tap_index in range(1, K):
        masked_grad = grad_conv * tap_valid[tap_index]
        tap_grads.append(jnp.sum(masked_grad * delayed(conv_input, tap_index), axis=0))
        grad_conv_input = grad_conv_input + conv_taps[tap_index][None, :] * advanced(
            masked_grad, tap_index
        )
    grad_conv_w = jnp.stack(tap_grads, axis=0)
    grad_inner = (
        jnp.stack([grad_conv_input, grad_gate_input], axis=1)
        .astype(jnp.bfloat16)
        .reshape(row_count, 2 * channels)
    )
    grad_w_in = jnp.einsum(
        "td,tf->df", normed_one, grad_inner, preferred_element_type=jnp.float32
    ).reshape(model_width, 2, channels)
    grad_normed_one = norm_grad_total(
        jnp.einsum("tf,df->td", grad_inner, in_flat, preferred_element_type=jnp.float32)
    )
    grad_norm_in, grad_gain_one = norm_backward(stream, scale_mamba, gain_mamba, grad_normed_one)
    input_grad = grad_mid + grad_norm_in
    mamba_sums = (
        lax.psum_scatter(grad_gain_one, "dp", scatter_dimension=0, tiled=True),
        lax.psum_scatter(grad_w_in, "dp", scatter_dimension=2, tiled=True),
        lax.psum_scatter(grad_conv_w, "dp", scatter_dimension=1, tiled=True),
        lax.psum_scatter(grad_conv_bias, "dp", scatter_dimension=0, tiled=True),
        lax.psum_scatter(grad_w_x, "dp", scatter_dimension=0, tiled=True),
        lax.psum_scatter(grad_w_dt, "dp", scatter_dimension=1, tiled=True),
        lax.psum_scatter(grad_dt_bias, "dp", scatter_dimension=0, tiled=True),
        lax.psum_scatter(grad_a_log, "dp", scatter_dimension=1, tiled=True),
        lax.psum_scatter(grad_skip, "dp", scatter_dimension=0, tiled=True),
        lax.psum_scatter(grad_out_proj, "dp", scatter_dimension=0, tiled=True),
    )
    packed_out = jnp.zeros((row_count, model_width), jnp.float32).at[arrival].set(result)
    packed_grad = jnp.zeros((row_count, model_width), jnp.float32).at[arrival].set(input_grad)
    home_out, home_grad = (
        lax.all_to_all(packed_out, "dp", split_axis=0, concat_axis=0, tiled=True),
        lax.all_to_all(packed_grad, "dp", split_axis=0, concat_axis=0, tiled=True),
    )
    final_out = jnp.zeros((row_count, model_width), jnp.float32).at[send_order].set(home_out)
    final_grad = jnp.zeros((row_count, model_width), jnp.float32).at[send_order].set(home_grad)
    return (
        final_out,
        final_grad,
        mamba_sums[0],
        mamba_sums[1],
        mamba_sums[2],
        mamba_sums[3],
        mamba_sums[4],
        mamba_sums[5],
        mamba_sums[6],
        mamba_sums[7],
        mamba_sums[8],
        mamba_sums[9],
        first_sums[0],
        first_sums[1],
        first_sums[2],
        attn_sums[0],
        attn_sums[1],
        attn_sums[2],
        second_sums[0],
        second_sums[1],
        second_sums[2],
    )


def solution(mesh):
    return jax.shard_map(
        shards,
        mesh=mesh,
        in_specs=(
            P("dp", None),
            P("dp", None),
            P("dp", None),
            P("dp", None),
            P("dp", None),
            P("dp"),
            P(None, None, ("dp", "tensor")),
            P(None, ("dp", "tensor")),
            P(("dp", "tensor")),
            P(("dp", "tensor"), None),
            P(None, ("dp", "tensor")),
            P(("dp", "tensor")),
            P(None, ("dp", "tensor")),
            P(("dp", "tensor")),
            P(("dp", "tensor"), None),
            P("dp"),
            P("dp", None, "tensor"),
            P("tensor", "dp"),
            P("dp"),
            P("dp", None, "tensor"),
            P("tensor", "dp"),
            P("dp"),
            P("dp", None, "tensor"),
            P("tensor", "dp"),
        ),
        out_specs=(
            P("dp", None),
            P("dp", None),
            P("dp"),
            P(None, None, ("dp", "tensor")),
            P(None, ("dp", "tensor")),
            P(("dp", "tensor")),
            P(("dp", "tensor"), None),
            P(None, ("dp", "tensor")),
            P(("dp", "tensor")),
            P(None, ("dp", "tensor")),
            P(("dp", "tensor")),
            P(("dp", "tensor"), None),
            P("dp"),
            P("dp", None, "tensor"),
            P("tensor", "dp"),
            P("dp"),
            P("dp", None, "tensor"),
            P("tensor", "dp"),
            P("dp"),
            P("dp", None, "tensor"),
            P("tensor", "dp"),
        ),
        check_vma=False,
    )
```

profile of v0, /device:TPU:0, one launch (start us, length us, event | category | flops | bytes accessed | tf_op | source)
XLA Modules:
  0.0 5063.2 jit_solution(2563430131805032028)
XLA Ops:
  19.6 30.7 all_gather.58
  51.5 30.0 all-gather.1
  81.5 17.6 all-gather
  99.6 32.4 all_gather.61
  133.2 28.1 all-gather.16.cloned.1.call-done
  161.3 22.5 copy.157
  183.8 11.5 fusion.19
  200.7 19.1 all-gather.3
  219.8 17.3 all-gather.2
  237.2 23.2 all_gather.62
  260.4 18.7 all_gather.64
  288.2 40.7 while.81
  340.1 71.5 %while.78 = (s32[]{:T(128)}, f32[8,16,2048]{2,1,0:T(8,128)S(1)}, f32[16,8,2048]{2,1,0:T(8,128)}, f32[16,8,2048]{2,1,0:T(8,128)}, f32[16,2048]{1,0:T(8,128)S(1)},...) while((s32[]{:T(128)}, f32[8,16,2048]{2,1,0:T(8,128)S(1)}, ...), condition=%wide.region_9.10_spmd, body=%wide.region_7.9_spmd.sunk | while | flops 1835010 | bytes 2886881 | solution.py:166
  427.0 18.5 all-gather.4
  445.5 14.0 all-reduce.41.cloned.1.call-done
  461.0 168.7 %all-gather.20.cloned.1.call-done = bf16[2048,2,4096]{2,0,1:T(8,128)(2,1)} async-done(((bf16[128,2,4096]{2,0,1:T(8,128)(2,1)}), bf16[2048,2,4096]{2,0,1:T(8,128)(2,1)}) %all-gather.20.cloned.1.call-update) | async-done | bytes 33554448 | tf_op jit(solution)/shard_map/all_gather | solution.py:54
  629.7 42.1 copy.166
  671.8 17.7 fusion.17
  693.3 68.9 %all-gather.22.cloned.1.call-done = bf16[4096,2048]{1,0:T(8,128)(2,1)} async-done(((bf16[4096,128]{1,0:T(8,128)(2,1)}), bf16[4096,2048]{1,0:T(8,128)(2,1)}) %all-gather.22.cloned.1.call-update) | async-done | bytes 16777232 | tf_op jit(solution)/shard_map/all_gather | solution.py:55
  762.3 9.4 fusion.139
  778.6 19.1 all-gather.5
  799.2 10.8 all-reduce.43.cloned.1.call-done
  812.4 104.4 %all-gather.24.cloned.1.call-done = bf16[2048,3,1024]{0,2,1:T(8,128)(2,1)} async-done(((bf16[128,3,1024]{0,2,1:T(8,128)(2,1)}), bf16[2048,3,1024]{0,2,1:T(8,128)(2,1)}) %all-gather.24.cloned.1.call-update) | async-done | bytes 12582928 | tf_op jit(solution)/shard_map/all_gather | solution.py:291
  926.8 43.5 all-gather.26.cloned.1.call-done
  980.9 33.1 all-gather.6
  1015.9 131.1 %all-gather.28.cloned.1.call-done = bf16[2048,2,4096]{2,0,1:T(8,128)(2,1)} async-done(((bf16[128,2,4096]{2,0,1:T(8,128)(2,1)}), bf16[2048,2,4096]{2,0,1:T(8,128)(2,1)}) %all-gather.28.cloned.1.call-update) | async-done | bytes 33554448 | tf_op jit(solution)/shard_map/all_gather | solution.py:54
  1147.1 42.0 copy.170
  1194.6 18.0 fusion.15
  1212.7 111.8 %all-gather.30.cloned.1.call-done = bf16[4096,2048]{1,0:T(8,128)(2,1)} async-done(((bf16[4096,128]{1,0:T(8,128)(2,1)}), bf16[4096,2048]{1,0:T(8,128)(2,1)}) %all-gather.30.cloned.1.call-update) | async-done | bytes 16777232 | tf_op jit(solution)/shard_map/all_gather | solution.py:55
  1324.5 14.1 multiply_bitcast_fusion.3
  1338.6 17.4 convolution_bitcast_fusion.2
  1357.0 37.4 all-reduce.47.cloned.1.call-done
  1415.1 74.5 %while.79 = (s32[]{:T(128)}, f32[8,16,2048]{2,1,0:T(8,128)S(1)}, f32[16,8,16,2048]{3,2,1,0:T(8,128)}, f32[16,8,2048]{2,1,0:T(8,128)}, f32[16,2048]{1,0:T(8,128)S...) while((s32[]{:T(128)}, f32[8,16,2048]{2,1,0:T(8,128)S(1)}, ...), condition=%wide.region_31.32_spmd, body=%wide.region_30.31_spmd.sunk | while | flops 1327106 | bytes 4785881 | solution.py:166
  1497.4 14.1 multiply_bitcast_fusion.1
  1511.5 17.5 convolution_bitcast_fusion.1
  1533.0 9.5 fusion.141
  1542.5 26.6 all-reduce.51.cloned.1.call-done
  1573.4 8.3 multiply_reduce_fusion.8
  1584.3 87.8 %while.82 = (s32[]{:T(128)}, f32[8,16,2048]{2,1,0:T(8,128)}, f32[8,16,2048]{2,1,0:T(8,128)}, f32[16,8,2048]{2,1,0:T(8,128)}, f32[16,2048]{1,0:T(8,128)S(1)}, /*i...) while((s32[]{:T(128)}, f32[8,16,2048]{2,1,0:T(8,128)}, ...), condition=%wide.region_29.30_spmd.clone, body=%wide.region_28.29_spmd.clone.sunk | while | flops 2097156 | bytes 4720375 | solution.py:151
  1708.0 155.8 %while.80 = (s32[]{:T(128)}, f32[8,16,2048]{2,1,0:T(8,128)}, f32[16,8,2048]{2,1,0:T(8,128)}, f32[16,8,2048]{2,1,0:T(8,128)}, f32[16,8,16]{2,1,0:T(8,128)S(1)}, /...) while((s32[]{:T(128)}, f32[8,16,2048]{2,1,0:T(8,128)}, ...), condition=%wide.region_38.39_spmd, body=%wide.region_32.38_spmd.sunk | while | flops 5766915 | bytes 5067177 | solution.py:166
  1870.5 8.3 psum.78
  1885.3 12.4 convolution_bitcast_fusion
  1900.1 15.9 fusion.42
  1923.2 25.9 fusion.22
  1957.3 25.3 fusion.24
  1994.2 8.2 fusion.75
  2003.9 11.9 fusion.61
  2017.1 13.2 fusion.144
  2031.5 21.1 fusion.79
  2065.4 19.8 all-to-all-done.1
  2085.2 8.5 all-to-all-start.3
  2096.5 90.6 %all-reduce.28 = (f32[2048]{0:T(1024)S(1)}, f32[2048]{0:T(1024)S(1)}, f32[2048]{0:T(1024)S(1)}, f32[2048]{0:T(1024)S(1)}, f32[2048]{0:T(1024)S(1)}, /*index=5*/f32[2048]{0:T(1024)S(1)}, f32[2048]{0:T(1024)S(1)}) all-reduce(f32[2048]{0:T(1024)S(1)} %get-tuple-element.1009, ...), channel_id=2, replica_groups=mesh['dp'=16,'tensor'=2] {'dp'}, use_global_device_ids=true, to_apply=%region_45.46.clone | all-reduce | flops 14336 | bytes 114688
  2196.6 186.6 %reduce-scatter.15.cloned.1.call-done = f32[2048,2,128]{2,0,1:T(8,128)} async-done(((f32[2048,2,2048]{2,0,1:T(8,128)}), f32[2048,2,128]{2,0,1:T(8,128)}) %reduce-scatter.15.cloned.1.call-update) | async-done | bytes 2097168 | tf_op jit(solution)/shard_map/reduce_scatter | solution.py:484
  2388.6 634.8 %reduce-scatter.33.cloned.1.call-done = f32[128,2,4096]{2,0,1:T(8,128)} async-done(((f32[2048,2,4096]{2,0,1:T(8,128)}), f32[128,2,4096]{2,0,1:T(8,128)}) %reduce-scatter.33.cloned.1.call-update) | async-done | bytes 4194320 | tf_op jit(solution)/shard_map/reduce_scatter | solution.py:102
  3030.8 632.5 %reduce-scatter.25.cloned.1.call-done = f32[128,2,4096]{2,0,1:T(8,128)} async-done(((f32[2048,2,4096]{2,0,1:T(8,128)}), f32[128,2,4096]{2,0,1:T(8,128)}) %reduce-scatter.25.cloned.1.call-update) | async-done | bytes 4194320 | tf_op jit(solution)/shard_map/reduce_scatter | solution.py:102
  3663.3 7.5 copy.193
  3670.8 47.8 reduce-scatter.21.cloned.1.call-done
  3718.6 61.2 %reduce-scatter.19.cloned.1.call-done = f32[128,128]{1,0:T(8,128)} async-done(((f32[128,2048]{1,0:T(8,128)}), f32[128,128]{1,0:T(8,128)}) %reduce-scatter.19.cloned.1.call-update) | async-done | bytes 65552 | tf_op jit(solution)/shard_map/reduce_scatter | solution.py:488
  3779.7 61.5 %reduce-scatter.17.cloned.1.call-done = f32[128,160]{0,1:T(8,128)} async-done(((f32[2048,160]{0,1:T(8,128)}), f32[128,160]{0,1:T(8,128)}) %reduce-scatter.17.cloned.1.call-update) | async-done | bytes 81936 | tf_op jit(solution)/shard_map/reduce_scatter | solution.py:487
  3841.2 109.0 %reduce-scatter.31.cloned.1.call-done = f32[1024,128]{1,0:T(8,128)} async-done(((f32[1024,2048]{1,0:T(8,128)}), f32[1024,128]{1,0:T(8,128)}) %reduce-scatter.31.cloned.1.call-update) | async-done | bytes 524304 | tf_op jit(solution)/shard_map/reduce_scatter | solution.py:388
  3950.1 183.5 %reduce-scatter.23.cloned.1.call-done = f32[128,2048]{1,0:T(8,128)} async-done(((f32[2048,2048]{1,0:T(8,128)}), f32[128,2048]{1,0:T(8,128)}) %reduce-scatter.23.cloned.1.call-update) | async-done | bytes 1048592 | tf_op jit(solution)/shard_map/reduce_scatter | solution.py:492
  4133.7 248.0 %reduce-scatter.29.cloned.1.call-done = f32[128,3,1024]{2,0,1:T(8,128)} async-done(((f32[2048,3,1024]{2,0,1:T(8,128)}), f32[128,3,1024]{2,0,1:T(8,128)}) %reduce-scatter.29.cloned.1.call-update) | async-done | bytes 1572880 | tf_op jit(solution)/shard_map/reduce_scatter | solution.py:387
  4381.7 337.1 %reduce-scatter.35.cloned.1.call-done = f32[4096,128]{1,0:T(8,128)} async-done(((f32[4096,2048]{1,0:T(8,128)}), f32[4096,128]{1,0:T(8,128)}) %reduce-scatter.35.cloned.1.call-update) | async-done | bytes 2097168 | tf_op jit(solution)/shard_map/reduce_scatter | solution.py:103
  4718.8 337.1 %reduce-scatter.27.cloned.1.call-done = f32[4096,128]{1,0:T(8,128)} async-done(((f32[4096,2048]{1,0:T(8,128)}), f32[4096,128]{1,0:T(8,128)}) %reduce-scatter.27.cloned.1.call-update) | async-done | bytes 2097168 | tf_op jit(solution)/shard_map/reduce_scatter | solution.py:103
  (1045 shorter events, 687.2 us)
Async XLA Ops:
  7.2 154.1 %all-gather.16.cloned.1.call-start = ((), (), s32[]{:S(2)}) async-start(), calls=%async_computation.16 | async-start | bytes 17825792 | tf_op jit(solution)/shard_map/all_gather | solution.py:210
  10.2 40.1 copy-start.142
  10.2 41.2 copy-start.131
  10.2 71.3 %copy-start.132 = (bf16[128]{0:T(256)(128)(2,1)S(1)}, bf16[128]{0:T(256)(128)(2,1)}, u32[]{:S(2)}) copy-start(bf16[128]{0:T(256)(128)(2,1)} %param.42) | copy-start | bytes 772
  10.3 89.4 %copy-start.97 = (bf16[128,160]{0,1:T(8,128)(2,1)S(1)}, bf16[128,160]{0,1:T(8,128)(2,1)}, u32[]{:S(2)}) copy-start(bf16[128,160]{0,1:T(8,128)(2,1)} %param.43) | copy-start | bytes 122884
  12.0 120.1 %all-to-all-start = ((bf16[16,8,2048]{2,1,0:T(8,128)(2,1)}), bf16[16,8,2048]{2,1,0:T(8,128)(2,1)S(1)}, u32[]{:S(2)}, u32[]{:S(2)}) async-start(bf16[16,8,2048]{2,1,0:T(8,128)(2,1)} %bitcast.29), calls=%async_computation | async-start | bytes 1048576 | tf_op jit(solution)/shard_map/all_to_all | solution.py:201
  19.4 262.5 %all-reduce.39.cloned.1.call-start = ((), (), s32[]{:S(2)}) async-start(), calls=%async_computation.17 | async-start | bytes 163840 | tf_op jit(solution)/shard_map/psum | solution.py:247
  50.9 82.1 %copy-start.117 = (s32[1024]{0:T(1024)}, s32[1024]{0:T(1024)S(1)}, u32[]{:S(2)}) copy-start(s32[1024]{0:T(1024)S(1)} %pad_clamp_fusion) | copy-start | bytes 12292
  51.4 149.2 %copy-start.128 = (s32[128]{0:T(128)}, s32[128]{0:T(128)S(1)}, u32[]{:S(2)}) copy-start(s32[128]{0:T(128)S(1)} %select_reduce_fusion) | copy-start | bytes 1540
  81.5 102.3 %copy-start.70 = (f32[16,1,128]{2,1,0:T(1,128)}, f32[16,1,128]{2,1,0:T(1,128)S(1)}, u32[]{:S(2)}) copy-start(f32[16,1,128]{2,1,0:T(1,128)S(1)} %convert_element_type.220) | copy-start | bytes 24580
  99.6 95.9 %copy-start.119 = (f32[128]{0:T(128)}, f32[128]{0:T(128)S(1)}, u32[]{:S(2)}) copy-start(f32[128]{0:T(128)S(1)} %get-tuple-element.1215) | copy-start | bytes 1540
  99.6 95.9 %copy-start.121 = (f32[128]{0:T(128)}, f32[128]{0:T(128)S(1)}, u32[]{:S(2)}) copy-start(f32[128]{0:T(128)S(1)} %get-tuple-element.1216) | copy-start | bytes 1540
  99.6 95.9 %copy-start.123 = (f32[128]{0:T(128)}, f32[128]{0:T(128)S(1)}, u32[]{:S(2)}) copy-start(f32[128]{0:T(128)S(1)} %get-tuple-element.1217) | copy-start | bytes 1540
  132.0 63.6 %copy-start.86 = (f32[1,2048]{1,0:T(1,128)}, f32[1,2048]{1,0:T(1,128)S(1)}, u32[]{:S(2)}) copy-start(f32[1,2048]{1,0:T(1,128)S(1)} %get-tuple-element.1207) | copy-start | bytes 24580
  132.0 63.6 %copy-start.88 = (f32[1,2048]{1,0:T(1,128)}, f32[1,2048]{1,0:T(1,128)S(1)}, u32[]{:S(2)}) copy-start(f32[1,2048]{1,0:T(1,128)S(1)} %get-tuple-element.1208) | copy-start | bytes 24580
  132.0 63.6 %copy-start.90 = (f32[1,2048]{1,0:T(1,128)}, f32[1,2048]{1,0:T(1,128)S(1)}, u32[]{:S(2)}) copy-start(f32[1,2048]{1,0:T(1,128)S(1)} %get-tuple-element.1209) | copy-start | bytes 24580
  132.0 63.6 %copy-start.92 = (f32[1,2048]{1,0:T(1,128)}, f32[1,2048]{1,0:T(1,128)S(1)}, u32[]{:S(2)}) copy-start(f32[1,2048]{1,0:T(1,128)S(1)} %get-tuple-element.1210) | copy-start | bytes 24580
  133.0 326.5 %copy-start.15 = (bf16[128,2048]{1,0:T(8,128)(2,1)}, bf16[128,2048]{1,0:T(8,128)(2,1)S(1)}, u32[]{:S(2)}) copy-start(bf16[128,2048]{1,0:T(8,128)(2,1)S(1)} %gather_fusion.1) | copy-start | bytes 1572868
  133.2 50.6 copy-start.110
  197.0 40.2 copy-start.102
  198.8 61.6 %copy-start.18 = (bf16[128,2048]{1,0:T(8,128)(2,1)}, bf16[128,2048]{1,0:T(8,128)(2,1)S(1)}, u32[]{:S(2)}) copy-start(bf16[128,2048]{1,0:T(8,128)(2,1)S(1)} %get-tuple-element.1141) | copy-start | bytes 1572868
  198.8 61.6 %copy-start.125 = (bf16[16,128]{1,0:T(8,128)(2,1)S(1)}, bf16[16,128]{1,0:T(8,128)(2,1)}, u32[]{:S(2)}) copy-start(bf16[16,128]{1,0:T(8,128)(2,1)} %param.46) | copy-start | bytes 12292
  199.8 216.4 %all-gather.18.cloned.1.call-start = ((), (), s32[]{:S(2)}) async-start(), calls=%async_computation.18 | async-start | bytes 8912896 | tf_op jit(solution)/shard_map/all_gather | solution.py:218
  200.5 259.0 %all-reduce.41.cloned.1.call-start = ((), (), s32[]{:S(2)}) async-start(), calls=%async_computation.19 | async-start | bytes 2097152 | tf_op jit(solution)/shard_map/psum | solution.py:44
  219.8 193.8 %copy-start.83 = (f32[16,1,128]{2,1,0:T(1,128)}, f32[16,1,128]{2,1,0:T(1,128)S(1)}, u32[]{:S(2)}) copy-start(f32[16,1,128]{2,1,0:T(1,128)S(1)} %convert_element_type.222) | copy-start | bytes 24580
  422.0 207.6 %all-gather.20.cloned.1.call-start = ((), (), s32[]{:S(2)}) async-start(), calls=%async_computation.20 | async-start | bytes 35651584 | tf_op jit(solution)/shard_map/all_gather | solution.py:54
  426.3 335.9 %all-gather.22.cloned.1.call-start = ((), (), s32[]{:S(2)}) async-start(), calls=%async_computation.21 | async-start | bytes 17825792 | tf_op jit(solution)/shard_map/all_gather | solution.py:55
  426.9 383.1 %all-reduce.43.cloned.1.call-start = ((), (), s32[]{:S(2)}) async-start(), calls=%async_computation.22 | async-start | bytes 2097152 | tf_op jit(solution)/shard_map/psum | solution.py:44
  461.0 1108.2 %copy-start.6 = (f32[128,2048]{1,0:T(8,128)}, f32[128,2048]{1,0:T(8,128)S(1)}, u32[]{:S(2)}) copy-start(f32[128,2048]{1,0:T(8,128)S(1)} %get-tuple-element.1140) | copy-start | bytes 3145732
  461.0 210.8 %copy-start.104 = (f32[128]{0:T(128)}, f32[128]{0:T(128)S(1)}, u32[]{:S(2)}) copy-start(f32[128]{0:T(128)S(1)} %add_rsqrt_fusion.2) | copy-start | bytes 1540
  693.3 78.4 %copy-start.65 = (bf16[128,3,1024]{2,0,1:T(8,128)(2,1)S(1)}, bf16[128,3,1024]{2,0,1:T(8,128)(2,1)}, u32[]{:S(2)}) copy-start(bf16[128,3,1024]{2,0,1:T(8,128)(2,1)} %param.53) | copy-start | bytes 2359300
  771.7 145.1 %all-gather.24.cloned.1.call-start = ((), (), s32[]{:S(2)}) async-start(), calls=%async_computation.23 | async-start | bytes 13369344 | tf_op jit(solution)/shard_map/all_gather | solution.py:291
  772.9 197.4 %all-gather.26.cloned.1.call-start = ((), (), s32[]{:S(2)}) async-start(), calls=%async_computation.24 | async-start | bytes 4456448 | tf_op jit(solution)/shard_map/all_gather | solution.py:292
  773.7 373.4 %all-gather.28.cloned.1.call-start = ((), (), s32[]{:S(2)}) async-start(), calls=%async_computation.26 | async-start | bytes 35651584 | tf_op jit(solution)/shard_map/all_gather | solution.py:54
  778.0 413.9 %all-reduce.45.cloned.1.call-start = ((), (), s32[]{:S(2)}) async-start(), calls=%async_computation.25 | async-start | bytes 2097152 | tf_op jit(solution)/shard_map/psum | solution.py:44
  797.7 126.5 %copy-start.76 = (f32[16,1,128]{2,1,0:T(1,128)}, f32[16,1,128]{2,1,0:T(1,128)S(1)}, u32[]{:S(2)}) copy-start(f32[16,1,128]{2,1,0:T(1,128)S(1)} %convert_element_type.224) | copy-start | bytes 24580
  812.4 111.8 %copy-start.113 = (f32[128]{0:T(128)}, f32[128]{0:T(128)S(1)}, u32[]{:S(2)}) copy-start(f32[128]{0:T(128)S(1)} %add_rsqrt_fusion.1) | copy-start | bytes 1540
  926.5 43.8 copy-start.79
  926.8 47.5 copy-start.60
  974.3 350.2 %all-gather.30.cloned.1.call-start = ((), (), s32[]{:S(2)}) async-start(), calls=%async_computation.27 | async-start | bytes 17825792 | tf_op jit(solution)/shard_map/all_gather | solution.py:55
  977.3 36.8 all-to-all-start.2
  980.9 413.6 %all-reduce.47.cloned.1.call-start = ((), (), s32[]{:S(2)}) async-start(), calls=%async_computation.28 | async-start | bytes 2097152 | tf_op jit(solution)/shard_map/psum | solution.py:48
  1193.7 203.4 %copy-start.107 = (f32[128]{0:T(128)}, f32[128]{0:T(128)S(1)}, u32[]{:S(2)}) copy-start(f32[128]{0:T(128)S(1)} %add_rsqrt_fusion) | copy-start | bytes 1540
  1194.6 129.9 %copy-start.41 = (bf16[128,2048]{1,0:T(8,128)(2,1)S(1)}, bf16[128,2048]{1,0:T(8,128)(2,1)}, u32[]{:S(2)}) copy-start(bf16[128,2048]{1,0:T(8,128)(2,1)} %gather_fusion.3) | copy-start | bytes 1572868
  1356.0 136.6 %all-reduce.49.cloned.1.call-start = ((), (), s32[]{:S(2)}) async-start(), calls=%async_computation.29 | async-start | bytes 2097152 | tf_op jit(solution)/shard_map/psum | solution.py:48
  1414.9 154.3 %all-reduce.51.cloned.1.call-start = ((), (), s32[]{:S(2)}) async-start(), calls=%async_computation.30 | async-start | bytes 2097152 | tf_op jit(solution)/shard_map/psum | solution.py:48
  1528.9 523.8 %all-reduce.53.cloned.1.call-start = ((), (), s32[]{:S(2)}) async-start(), calls=%async_computation.43 | async-start | bytes 4194304 | tf_op jit(solution)/shard_map/psum | solution.py:44
  1533.0 36.1 copy-start.105
  1897.7 197.2 %reduce-scatter.37.cloned.1.call-start = ((), (), s32[]{:S(2)}) async-start(), calls=%async_computation.42 | async-start | bytes 1114112
  1900.0 483.1 %reduce-scatter.15.cloned.1.call-start = ((), (), s32[]{:S(2)}) async-start(), calls=%async_computation.31 | async-start | bytes 35651584 | tf_op jit(solution)/shard_map/reduce_scatter | solution.py:484
  1916.0 1107.3 %reduce-scatter.33.cloned.1.call-start = ((), (), s32[]{:S(2)}) async-start(), calls=%async_computation.40 | async-start | bytes 71303168 | tf_op jit(solution)/shard_map/reduce_scatter | solution.py:102
  1949.2 1714.1 %reduce-scatter.25.cloned.1.call-start = ((), (), s32[]{:S(2)}) async-start(), calls=%async_computation.36 | async-start | bytes 71303168 | tf_op jit(solution)/shard_map/reduce_scatter | solution.py:102
  1982.6 1735.9 %reduce-scatter.21.cloned.1.call-start = ((), (), s32[]{:S(2)}) async-start(), calls=%async_computation.34 | async-start | bytes 139264 | tf_op jit(solution)/shard_map/reduce_scatter | solution.py:490
  1985.2 1794.5 %reduce-scatter.19.cloned.1.call-start = ((), (), s32[]{:S(2)}) async-start(), calls=%async_computation.33 | async-start | bytes 1114112 | tf_op jit(solution)/shard_map/reduce_scatter | solution.py:488
  1986.6 1854.6 %reduce-scatter.17.cloned.1.call-start = ((), (), s32[]{:S(2)}) async-start(), calls=%async_computation.32 | async-start | bytes 1392640 | tf_op jit(solution)/shard_map/reduce_scatter | solution.py:487
  1988.1 1962.1 %reduce-scatter.31.cloned.1.call-start = ((), (), s32[]{:S(2)}) async-start(), calls=%async_computation.39 | async-start | bytes 8912896 | tf_op jit(solution)/shard_map/reduce_scatter | solution.py:388
  1992.7 2140.9 %reduce-scatter.23.cloned.1.call-start = ((), (), s32[]{:S(2)}) async-start(), calls=%async_computation.35 | async-start | bytes 17825792 | tf_op jit(solution)/shard_map/reduce_scatter | solution.py:492
  2002.4 2379.2 %reduce-scatter.29.cloned.1.call-start = ((), (), s32[]{:S(2)}) async-start(), calls=%async_computation.38 | async-start | bytes 26738688 | tf_op jit(solution)/shard_map/reduce_scatter | solution.py:387
  2015.8 2703.0 %reduce-scatter.35.cloned.1.call-start = ((), (), s32[]{:S(2)}) async-start(), calls=%async_computation.41 | async-start | bytes 35651584 | tf_op jit(solution)/shard_map/reduce_scatter | solution.py:103
  2030.3 3025.5 %reduce-scatter.27.cloned.1.call-start = ((), (), s32[]{:S(2)}) async-start(), calls=%async_computation.37 | async-start | bytes 35651584 | tf_op jit(solution)/shard_map/reduce_scatter | solution.py:103
  2056.1 29.1 all-to-all-start.1
  2062.5 33.9 copy-start.98
  2085.2 109.0 %all-to-all-start.3 = ((f32[16,8,2048]{2,1,0:T(8,128)}), f32[16,8,2048]{2,1,0:T(8,128)S(1)}, u32[]{:S(2)}, u32[]{:S(2)}) async-start(f32[16,8,2048]{2,1,0:T(8,128)} %bitcast.478), calls=%async_computation.3 | async-start | bytes 2097152 | tf_op jit(solution)/shard_map/all_to_all | solution.py:498
  3663.3 1392.6 %copy-start.1 = (bf16[128,2048]{1,0:T(8,128)(2,1)S(1)}, bf16[128,2048]{1,0:T(8,128)(2,1)}, u32[]{:S(2)}) copy-start(bf16[128,2048]{1,0:T(8,128)(2,1)} %param.34) | copy-start | bytes 1572868
  (113 other events, 583.1 us)
Sparse Core Ops, SparseCore 0:
  10.8 150.5 all-gather.15
  199.9 19.6 all-reduce.38
  221.8 77.6 all-gather.17
  422.1 37.3 all-reduce.40
  461.5 168.0 all-gather.19
  631.9 130.3 all-gather.21
  771.8 38.1 all-reduce.42
  812.8 103.9 all-gather.23
  918.9 51.3 all-gather.25
  972.3 174.6 all-gather.27
  1149.9 41.9 all-reduce.44
  1194.2 130.2 all-gather.29
  1356.1 38.2 all-reduce.46
  1415.0 40.0 all-reduce.48
  1529.1 40.0 all-reduce.50
  1897.9 64.2 all-reduce.52
  1966.6 57.4 reduce-scatter.36
  2028.2 354.8 reduce-scatter.14
  2387.4 635.9 reduce-scatter.32
  3027.4 635.8 reduce-scatter.24
  3667.3 51.2 reduce-scatter.20
  3723.2 56.4 reduce-scatter.18
  3783.9 57.2 reduce-scatter.16
  3846.2 103.8 reduce-scatter.30
  3955.4 178.2 reduce-scatter.22
  4138.8 242.8 reduce-scatter.28
  4386.9 331.8 reduce-scatter.34
  4724.2 331.6 reduce-scatter.26
where the time goes:
time: 5090 us; the launch traced here: 5060 us
  waiting for transfers between devices  3610 us (71%)
  local copies, waits for them, and re-layouts  446 us (9%)
  blocking collectives  359 us (7%)
  matrix products  318 us (6%)
  other arithmetic  285 us (6%)
    reduce_scatter x2, waiting for transfers between devices, feed_backward(): lax.psum_scatter(grad_gate_up, 'dp', scatter_dimension=0, tiled=True)  1270 us
    reduce_scatter x2, waiting for transfers between devices, feed_backward(): lax.psum_scatter(grad_down, 'dp', scatter_dimension=1, tiled=True)  674 us
    all_gather x2, waiting for transfers between devices, feed_weights(): lax.all_gather(gate_up, 'dp', axis=0, tiled=True)  300 us
    reduce_scatter x1, waiting for transfers between devices, shards(): lax.psum_scatter(grad_w_qkv, 'dp', scatter_dimension=0, tiled=True)  248 us
    reduce_scatter x1, waiting for transfers between devices, shards(): lax.psum_scatter(grad_w_in, 'dp', scatter_dimension=2, tiled=True)  187 us
    reduce_scatter x1, waiting for transfers between devices, shards(): lax.psum_scatter(grad_out_proj, 'dp', scatter_dimension=0, tiled=True)  184 us
    all_gather x2, waiting for transfers between devices, feed_weights(): lax.all_gather(down_proj, 'dp', axis=1, tiled=True)  181 us
    reduce_scatter x1, waiting for transfers between devices, shards(): lax.psum_scatter(grad_attn_out, 'dp', scatter_dimension=1, tiled=True)  109 us
  transfers between devices with their start and end apart: 32, of which 24 were waited for; matrix products, arithmetic and copies ran while one was open for 11% of the time, Pallas kernels for 0%

commit v1 on v0

v1 whole, which is shorter than its diff:
```python
import functools

import jax
import jax.numpy as jnp
from jax import lax
from jax.experimental import pallas as pl
from jax.experimental.pallas import tpu as pltpu
from jax.sharding import PartitionSpec as P

N = 16
R = 128
K = 4
HD = 64
LANE = 128
GROUP = 8
LOG2E = 1.4426950408889634
LN2 = 0.6931471805599453

low = jnp.bfloat16
full = jnp.float32
eps = 1e-05


def block_rows(ref, start, count, stride):
    return ref[pl.ds(start, count, stride=stride), :]


def spread(ref, values):
    rows = values.shape[0]
    for part in range(values.shape[1] // LANE):
        ref[part * rows : (part + 1) * rows, :] = values[:, part * LANE : (part + 1) * LANE]


def gathered(ref, rows):
    return jnp.concatenate(
        [ref[part * rows : (part + 1) * rows, :] for part in range(ref.shape[0] // rows)], axis=1
    )


def scan_forward_kernel(
    packs, chunk, mixer_ref, gate_ref, low_ref, mats_ref, keep_ref, proj_ref, bias_ref, rate_ref, skip_ref,
    gated_ref, out_ref, prior_ref, step_s, drive_s, out_s, rate_s, state,
):
    rows, width = mixer_ref.shape
    span = rows // packs
    parts = width // LANE
    place = pl.program_id(0)

    @pl.when(place == 0)
    def _():
        state[...] = jnp.zeros_like(state)
        pre = jnp.dot(low_ref[...], proj_ref[...], preferred_element_type=jnp.float32) + bias_ref[...]
        step = jax.nn.softplus(pre)
        spread(drive_s, step * mixer_ref[...])
        spread(step_s, jnp.where(keep_ref[...] > 0.0, step, 1e30))
        for n in range(N):
            for part in range(parts):
                rate_s[n, part] = jnp.broadcast_to(
                    rate_ref[n : n + 1, part * LANE : (part + 1) * LANE] * LOG2E, (packs, LANE)
                )

    def one(k, held):
        t = place * chunk + k
        mats = block_rows(mats_ref, t, packs, span)
        step_now = [block_rows(step_s, part * rows + t, packs, span) for part in range(parts)]
        drive_now = [block_rows(drive_s, part * rows + t, packs, span) for part in range(parts)]
        total = [jnp.zeros((packs, LANE), jnp.float32)] * parts
        fresh = []
        for n in range(N):
            source = jnp.broadcast_to(mats[:, n : n + 1], (packs, LANE))
            reader = jnp.broadcast_to(mats[:, N + n : N + n + 1], (packs, LANE))
            for part in range(parts):
                before = held[n * parts + part]
                prior_ref[k, n, part] = before
                now = jnp.exp2(step_now[part] * rate_s[n, part]) * before + drive_now[part] * source
                total[part] = total[part] + reader * now
                fresh.append(now)
        for part in range(parts):
            out_s[pl.ds(part * rows + t, packs, stride=span), :] = total[part]
        return tuple(fresh)

    final = lax.fori_loop(
        0, chunk, one, tuple(state[n, part] for n in range(N) for part in range(parts))
    )
    for n in range(N):
        for part in range(parts):
            state[n, part] = final[n * parts + part]

    @pl.when(place == pl.num_programs(0) - 1)
    def _():
        mixed = gathered(out_s, rows) + skip_ref[...] * mixer_ref[...]
        out_ref[...] = mixed
        gate = gate_ref[...]
        gated_ref[...] = (mixed * gate * jax.nn.sigmoid(gate)).astype(jnp.bfloat16)


def whole_block(shape):
    return pl.BlockSpec(shape, lambda c: (0,) * len(shape))


def scan_forward(mixer, gate, low, mats, keep, proj, bias, rate, skip, packs, chunk=16):
    rows, width = mixer.shape
    span = rows // packs
    parts = width // LANE
    args = (mixer, gate, low, mats, keep, proj, bias, rate, skip)
    return pl.pallas_call(
        functools.partial(scan_forward_kernel, packs, chunk),
        grid=(span // chunk,),
        in_specs=[whole_block(value.shape) for value in args],
        out_specs=[
            whole_block((rows, width)),
            whole_block((rows, width)),
            pl.BlockSpec((chunk, N, parts, packs, LANE), lambda c: (c, 0, 0, 0, 0)),
        ],
        out_shape=[
            jax.ShapeDtypeStruct((rows, width), jnp.bfloat16),
            jax.ShapeDtypeStruct((rows, width), jnp.float32),
            jax.ShapeDtypeStruct((span, N, parts, packs, LANE), jnp.float32),
        ],
        scratch_shapes=[
            pltpu.VMEM((parts * rows, LANE), jnp.float32),
            pltpu.VMEM((parts * rows, LANE), jnp.float32),
            pltpu.VMEM((parts * rows, LANE), jnp.float32),
            pltpu.VMEM((N, parts, packs, LANE), jnp.float32),
            pltpu.VMEM((N, parts, packs, LANE), jnp.float32),
        ],
        compiler_params=pltpu.CompilerParams(vmem_limit_bytes=48 << 20),
        cost_estimate=pl.CostEstimate(
            flops=rows * width * N * 8, bytes_accessed=rows * width * N * 4, transcendentals=rows * width * N
        ),
    )(*args)


def scan_backward_kernel(
    packs, chunk, mixer_ref, gate_ref, mixed_ref, gated_ref, low_ref, mats_ref, keep_ref, proj_ref, bias_ref,
    rate_ref, skip_ref, prior_ref,
    step_grad_ref, mixer_grad_ref, gate_grad_ref, mats_grad_ref, log_grad_ref, skip_grad_ref,
    step_s, drive_s, mix_s, grad_s, rate_s, total_s, along_s, log_s, state,
):
    rows, width = mixer_ref.shape
    span = rows // packs
    parts = width // LANE
    place = pl.program_id(0)
    lane = lax.broadcasted_iota(jnp.int32, (packs, LANE), 1)

    def step_before():
        return (
            jnp.dot(low_ref[...], proj_ref[...], preferred_element_type=jnp.float32) + bias_ref[...]
        )

    @pl.when(place == 0)
    def _():
        state[...] = jnp.zeros_like(state)
        log_s[...] = jnp.zeros_like(log_s)
        step = jax.nn.softplus(step_before())
        mixer = mixer_ref[...]
        gate = gate_ref[...]
        sig = jax.nn.sigmoid(gate)
        grad = gated_ref[...]
        scan_grad = grad * gate * sig
        gate_grad_ref[...] = (grad * mixed_ref[...] * sig * (1.0 + gate * (1.0 - sig))).astype(jnp.bfloat16)
        skip_grad_ref[...] = jnp.sum(scan_grad * mixer, axis=0, keepdims=True)
        spread(grad_s, scan_grad)
        spread(mix_s, mixer)
        spread(drive_s, step * mixer)
        spread(step_s, jnp.where(keep_ref[...] > 0.0, step, 1e30))
        for n in range(N):
            for part in range(parts):
                rate_s[n, part] = jnp.broadcast_to(
                    rate_ref[n : n + 1, part * LANE : (part + 1) * LANE] * LOG2E, (packs, LANE)
                )

    def one(back, held):
        k = chunk - 1 - back
        t = (pl.num_programs(0) - 1 - place) * chunk + k
        mats = block_rows(mats_ref, t, packs, span)
        step_now = [block_rows(step_s, part * rows + t, packs, span) for part in range(parts)]
        drive_now = [block_rows(drive_s, part * rows + t, packs, span) for part in range(parts)]
        mix_now = [block_rows(mix_s, part * rows + t, packs, span) for part in range(parts)]
        grad_now = [block_rows(grad_s, part * rows + t, packs, span) for part in range(parts)]
        zero = jnp.zeros((packs, LANE), jnp.float32)
        along = [zero] * parts
        rated = [zero] * parts
        waiting = []
        fresh = []
        for n in range(N):
            source = jnp.broadcast_to(mats[:, n : n + 1], (packs, LANE))
            reader = jnp.broadcast_to(mats[:, N + n : N + n + 1], (packs, LANE))
            source_sum = zero
            reader_sum = zero
            for part in range(parts):
                rate = rate_s[n, part]
                decay = jnp.exp2(step_now[part] * rate)
                kept = decay * prior_ref[k, n, part]
                now = kept + drive_now[part] * source
                adjoint = grad_now[part] * reader + held[n * parts + part]
                fresh.append(decay * adjoint)
                through = adjoint * kept
                rated[part] = rated[part] + through * rate
                log_s[n, part] += through * step_now[part]
                along[part] = along[part] + adjoint * source
                source_sum = source_sum + adjoint * drive_now[part]
                reader_sum = reader_sum + grad_now[part] * now
            waiting.append(source_sum)
            waiting.append(reader_sum)
        for part in range(parts):
            total_s[pl.ds(part * rows + t, packs, stride=span), :] = rated[part] * LN2 + mix_now[part] * along[part]
            along_s[pl.ds(part * rows + t, packs, stride=span), :] = along[part]
        big = jnp.dot(jnp.concatenate(waiting, axis=0).astype(jnp.bfloat16), jnp.ones((LANE, LANE), jnp.bfloat16), preferred_element_type=jnp.float32)
        mats_grad = zero
        for q in range(2 * N):
            mats_grad = jnp.where(lane == q, big[q * packs : (q + 1) * packs], mats_grad)
        mats_grad_ref[pl.ds(t, packs, stride=span), :] = mats_grad
        return tuple(fresh)

    final = lax.fori_loop(
        0, chunk, one, tuple(state[n, part] for n in range(N) for part in range(parts))
    )
    for n in range(N):
        for part in range(parts):
            state[n, part] = final[n * parts + part]

    @pl.when(place == pl.num_programs(0) - 1)
    def _():
        pre = step_before()
        step_grad_ref[...] = (gathered(total_s, rows) * jax.nn.sigmoid(pre)).astype(jnp.bfloat16)
        mixer_grad_ref[...] = (
            gathered(along_s, rows) * jax.nn.softplus(pre) + skip_ref[...] * gathered(grad_s, rows)
        )
        for n in range(N):
            log_grad_ref[n : n + 1, :] = jnp.concatenate(
                [jnp.sum(log_s[n, part], axis=0, keepdims=True) for part in range(parts)], axis=1
            ) * rate_ref[n : n + 1, :]


def scan_backward(
    mixer, gate, mixed, gated_grad, low, mats, keep, proj, bias, rate, skip, prior, packs, chunk=16
):
    rows, width = mixer.shape
    span = rows // packs
    parts = width // LANE
    last = span // chunk - 1
    args = (mixer, gate, mixed, gated_grad, low, mats, keep, proj, bias, rate, skip)
    shapes = [
        ((rows, width), jnp.bfloat16),
        ((rows, width), jnp.float32),
        ((rows, width), jnp.bfloat16),
        ((rows, LANE), jnp.float32),
        ((N, width), jnp.float32),
        ((1, width), jnp.float32),
    ]
    long_row = pltpu.VMEM((parts * rows, LANE), jnp.float32)
    small = pltpu.VMEM((N, parts, packs, LANE), jnp.float32)
    return pl.pallas_call(
        functools.partial(scan_backward_kernel, packs, chunk),
        grid=(span // chunk,),
        in_specs=[whole_block(value.shape) for value in args]
        + [pl.BlockSpec((chunk, N, parts, packs, LANE), lambda c: (last - c, 0, 0, 0, 0))],
        out_specs=[whole_block(shape) for shape, kind in shapes],
        out_shape=[jax.ShapeDtypeStruct(shape, kind) for shape, kind in shapes],
        scratch_shapes=[long_row, long_row, long_row, long_row, small, long_row, long_row, small, small],
        compiler_params=pltpu.CompilerParams(vmem_limit_bytes=56 << 20),
        cost_estimate=pl.CostEstimate(
            flops=rows * width * N * 20, bytes_accessed=rows * width * N * 4, transcendentals=rows * width * N
        ),
    )(*args, prior)


def silu_slope(operand):
    sig_value = jax.nn.sigmoid(operand)
    return sig_value * (1.0 + operand * (1.0 - sig_value))


def matmul(left, right):
    return jnp.dot(left, right, preferred_element_type=full)


def matmul_rows(left, right):
    return lax.dot_general(left, right, (((0,), (0,)), ((), ())), preferred_element_type=full)


def matmul_lanes(left, right):
    return lax.dot_general(left, right, (((1,), (1,)), ((), ())), preferred_element_type=full)


def norm_scale(stream):
    return lax.rsqrt(jnp.mean(stream * stream, axis=-1, keepdims=True) + eps)


def normed_rows(stream, gain):
    scale = norm_scale(stream)
    return scale, (stream * scale * gain[None, :]).astype(low)


def norm_backward(stream, rms_scale, gain_vec, grad_normed):
    weighted = grad_normed * gain_vec[None, :]
    inner_mean = jnp.mean(weighted * stream, axis=-1, keepdims=True)
    grad_stream = rms_scale * weighted - stream * rms_scale * rms_scale * rms_scale * inner_mean
    return (grad_stream, jnp.sum(grad_normed * stream * rms_scale, axis=0))


def hop(values, link):
    if link == "x":
        return lax.ppermute(values, "tensor", [(0, 1), (1, 0)])
    bit = {"core": 1, "y": 2, "z": 4, "outer": GROUP}[link]
    return lax.ppermute(values, "dp", [(k, k ^ bit) for k in range(lax.axis_size("dp"))])


def ordered(mine, theirs, index):
    first = index == 0
    return jnp.where(first, mine, theirs), jnp.where(first, theirs, mine)


def cuts(rows):
    third = rows * 3 // 8
    return ((0, third), (third, 2 * third), (2 * third, rows))


def gather_rows(own):
    tensor_at = lax.axis_index("tensor")

    def grow(values, axis, link):
        got = hop(values, link)
        if link == "x":
            return jnp.stack(ordered(values, got, tensor_at), axis=axis)
        return jnp.stack([values, got], axis=axis)

    first, second, third = [own[start:stop] for start, stop in cuts(own.shape[0])]
    first = grow(grow(grow(first, 0, "x"), 0, "y"), 0, "z")
    second = grow(grow(grow(second, 0, "y"), 0, "z"), 2, "x")
    third = grow(grow(grow(third, 0, "z"), 1, "x"), 1, "y")
    local = jnp.concatenate([first, second, third], axis=3)
    both = jnp.stack([local, hop(local, "core")], axis=0)
    return both.reshape((2 * GROUP * own.shape[0], own.shape[1]))


def reduce_rows(partial):
    kind = partial.dtype
    tensor_at = lax.axis_index("tensor")
    width = partial.shape[1]
    rows = partial.shape[0] // (2 * GROUP)
    cube = partial.reshape((2, 2, 2, 2, rows, width))

    def fold(values, axis, link):
        low_half = lax.index_in_dim(values, 0, axis, keepdims=False)
        high_half = lax.index_in_dim(values, 1, axis, keepdims=False)
        if link == "x":
            low_half, high_half = ordered(low_half, high_half, tensor_at)
        return low_half.astype(full) + hop(high_half.astype(kind), link).astype(full)

    cube = fold(cube, 0, "core")
    first, second, third = [cube[:, :, :, start:stop] for start, stop in cuts(rows)]
    first = fold(fold(fold(first, 0, "z"), 0, "y"), 0, "x")
    second = fold(fold(fold(second, 2, "x"), 0, "z"), 0, "y")
    third = fold(fold(fold(third, 1, "y"), 1, "x"), 0, "z")
    return jnp.concatenate([first, second, third], axis=0)


def outer_count():
    return lax.axis_size("dp") // GROUP


def outer_groups():
    return [[k + GROUP * other for other in range(outer_count())] for k in range(GROUP)]


def outer_gather(values, axis):
    if outer_count() == 2:
        pieces = ordered(values, hop(values, "outer"), lax.axis_index("dp") // GROUP)
        return jnp.concatenate(pieces, axis=axis)
    return lax.all_gather(values, "dp", axis_index_groups=outer_groups(), axis=axis, tiled=True)


def channel_gather(values):
    if outer_count() == 2:
        return jnp.concatenate([values, hop(values, "outer")], axis=-1)
    return lax.all_gather(
        values, "dp", axis_index_groups=outer_groups(), axis=values.ndim - 1, tiled=True
    )


def channel_scatter(make, width, kind):
    if outer_count() == 2:
        half = width // 2
        got = hop(make(half, width).astype(kind), "outer")
        return make(0, half) + got.astype(full)
    values = make(0, width).astype(kind)
    return lax.psum_scatter(
        values, "dp", axis_index_groups=outer_groups(), scatter_dimension=values.ndim - 1, tiled=True
    ).astype(full)


def outer_sum(make):
    if outer_count() == 2:
        here = lax.axis_index("dp") // GROUP
        got = hop(make(1 - here).astype(low), "outer")
        return make(here) + got.astype(full)
    blocks = jnp.stack([make(k).astype(low) for k in range(outer_count())], axis=0)
    return lax.psum_scatter(
        blocks, "dp", axis_index_groups=outer_groups(), scatter_dimension=0, tiled=True
    )[0].astype(full)


def inner_swap(values):
    groups = [
        [GROUP * outer + k for k in range(GROUP)] for outer in range(outer_count())
    ]
    return lax.all_to_all(
        values, "dp", split_axis=0, concat_axis=0, axis_index_groups=groups, tiled=True
    )


def lanes_of(values, block, count):
    size = values.shape[1] // count
    return lax.dynamic_slice_in_dim(values, block * size, size, axis=1)


def take_in(weight):
    depth, pairs, width = weight.shape
    cut = weight.reshape((depth, pairs, GROUP, width // GROUP)).transpose((2, 0, 1, 3))
    swapped = inner_swap(cut.reshape((GROUP, depth, pairs * width // GROUP)))
    return outer_gather(swapped.reshape((GROUP * depth, -1)), 0)


def give_in(make, depth, pairs, width):
    total = outer_sum(make).astype(low).reshape((GROUP, depth, -1))
    swapped = inner_swap(total).reshape((GROUP, depth, pairs, width // GROUP))
    return swapped.transpose((1, 2, 0, 3)).reshape((depth, pairs, width)).astype(full)


def take_out(weight):
    height, depth = weight.shape
    swapped = inner_swap(weight.reshape((GROUP, height // GROUP, depth)))
    return outer_gather(swapped.transpose((1, 0, 2)).reshape((height // GROUP, GROUP * depth)), 1)


def give_out(make, height, depth):
    total = outer_sum(make).astype(low).reshape((height // GROUP, GROUP, depth))
    return inner_swap(total.transpose((1, 0, 2))).reshape((height, depth)).astype(full)


def feed_forward(stream, gain, gate_up, down):
    hidden_width = down.shape[0]
    scale, normed = normed_rows(stream, gain)
    every = gather_rows(normed)
    pair = matmul(every, gate_up)
    gate = pair[:, :hidden_width]
    up = pair[:, hidden_width:]
    hidden = (jax.nn.silu(gate) * up).astype(low)
    branch = reduce_rows(matmul(hidden, down).astype(low))
    return stream + branch, (scale, every, gate, up, hidden)


def feed_backward(grad, every_grad, stream, kept, gain, gate_up, down):
    scale, every, gate, up, hidden = kept
    count = outer_count()
    hidden_grad = matmul_lanes(every_grad, down)
    pair_grad = jnp.concatenate(
        [hidden_grad * up * silu_slope(gate), hidden_grad * jax.nn.silu(gate)], axis=1
    ).astype(low)
    normed_grad = reduce_rows(matmul_lanes(pair_grad, gate_up).astype(low))
    norm_part, gain_grad = norm_backward(stream, scale, gain, normed_grad)
    depth = gate_up.shape[0] // (count * GROUP)
    in_grad = give_in(
        lambda block: matmul_rows(lanes_of(every, block, count), pair_grad),
        depth, 2, gate_up.shape[1] * GROUP // 2,
    )
    out_grad = give_out(
        lambda block: matmul_rows(hidden, lanes_of(every_grad, block, count)),
        down.shape[0] * GROUP, depth,
    )
    return grad + norm_part, (gain_grad, in_grad, out_grad)


def shifted(values, places):
    if places >= 0:
        pad = jnp.zeros_like(values[:, :places])
        return jnp.concatenate([pad, values[:, : values.shape[1] - places]], axis=1)
    pad = jnp.zeros_like(values[:, :-places])
    return jnp.concatenate([values[:, -places:], pad], axis=1)


def rotated(heads_in, cosine, sine_part):
    half_width = heads_in.shape[-1] // 2
    first_half = heads_in[..., :half_width]
    second_half = heads_in[..., half_width:]
    return jnp.concatenate(
        [
            first_half * cosine - second_half * sine_part,
            second_half * cosine + first_half * sine_part,
        ],
        axis=-1,
    )


def picks(index, count):
    return (index[:, None] == jnp.arange(count, dtype=jnp.int32)[None, :]).astype(low)


def shards(
    tokens, cotangent, lengths, route, place, gain_one, w_in, conv_w, conv_bias, w_x, w_dt, dt_bias, a_log,
    skip, w_out, gain_three, mlp_one_in, mlp_one_out, gain_two, w_qkv, w_o, gain_four, mlp_two_in, mlp_two_out,
):
    dp_count = lax.axis_size("dp")
    dp_at = lax.axis_index("dp")
    tensor_at = lax.axis_index("tensor")
    row_count, model_width = tokens.shape
    own_count = row_count // lax.axis_size("tensor")
    slot = row_count // dp_count
    count = outer_count()
    seqs = lengths.shape[1]
    part = gain_one.shape[0]

    send_sel = picks(route[0], row_count)
    arrive_sel = picks(place[0], row_count)
    own_sel = lax.dynamic_slice_in_dim(arrive_sel, tensor_at * own_count, own_count, axis=0)
    side = jnp.concatenate([gain_one, gain_three, gain_two, gain_four, lengths[0].astype(low)])
    side_width = -(-side.shape[0] // (slot * LANE)) * LANE
    side_rows = jnp.pad(side, (0, slot * side_width - side.shape[0])).reshape((1, slot, side_width))
    outbound = matmul(send_sel, tokens).astype(low).reshape((dp_count, slot, model_width))
    inbound = lax.all_to_all(
        jnp.concatenate([outbound, jnp.broadcast_to(side_rows, (dp_count, slot, side_width))], axis=2),
        "dp", split_axis=0, concat_axis=0, tiled=True,
    )
    stream = matmul(own_sel, inbound[:, :, :model_width].reshape((row_count, model_width)))
    sides = inbound[:, :, model_width:].reshape((dp_count, slot * side_width))
    gains = [
        sides[:, k * part : (k + 1) * part].reshape((model_width,)).astype(full) for k in range(4)
    ]
    gain_mamba, gain_first, gain_attn, gain_second = gains
    all_lengths = sides[:, 4 * part : 4 * part + seqs].astype(full)

    pack_at = dp_at ^ jnp.array([0, 2, 4, 6, 1, 3, 5, 7], jnp.int32)
    pack_sel = (pack_at[:, None] == jnp.arange(dp_count, dtype=jnp.int32)[None, :]).astype(full)
    pack_lengths = jnp.sum(pack_sel[:, :, None] * all_lengths[None], axis=1).astype(jnp.int32)
    seq_ends = jnp.cumsum(pack_lengths, axis=1)
    row_index = jnp.arange(row_count, dtype=jnp.int32)
    segment = jnp.sum((row_index[None, :, None] >= seq_ends[:, None, :]).astype(jnp.int32), axis=2)
    one_hot = segment[:, :, None] == jnp.arange(seqs, dtype=jnp.int32)[None, None, :]
    offset = row_index[None, :] - jnp.sum(
        jnp.where(one_hot, (seq_ends - pack_lengths)[:, None, :], 0), axis=2
    )
    packs = GROUP
    every_count = packs * row_count
    taps = [(offset >= tap).astype(full)[:, :, None] for tap in range(K)]
    keep_mask = taps[1].reshape((every_count, 1))

    small = channel_gather(
        jnp.concatenate(
            [w_x.T, w_dt, conv_w, conv_bias[None], dt_bias[None], a_log, skip[None]], axis=0
        )
    )
    in_pair = channel_gather(w_in)
    channels = in_pair.shape[2]
    in_flat = in_pair.reshape((model_width, 2 * channels))
    select_rows = R + 2 * N
    select_proj = small[:select_rows]
    step_proj = small[select_rows : select_rows + R]
    rest = small[select_rows + R :].astype(full)
    conv_taps = rest[:K]
    conv_shift = rest[K]
    step_bias = rest[K + 1 : K + 2]
    decay_rate = -jnp.exp(rest[K + 2 : K + 2 + N])
    skip_gain = rest[K + 2 + N : K + 3 + N]
    if count == 2:
        out_proj = jnp.concatenate([w_out, hop(w_out, "outer")], axis=0)
    else:
        out_proj = lax.all_gather(w_out, "dp", axis_index_groups=outer_groups(), axis=0, tiled=True)

    scale_mamba, normed_one = normed_rows(stream, gain_mamba)
    every_one = gather_rows(normed_one)
    inner = matmul(every_one, in_flat)
    conv_input = inner[:, :channels].reshape((packs, row_count, channels))
    gate_input = inner[:, channels:]
    conv_sum = conv_shift + conv_taps[0] * conv_input
    for tap in range(1, K):
        conv_sum = conv_sum + conv_taps[tap] * shifted(conv_input, tap) * taps[tap]
    mixer_low = jax.nn.silu(conv_sum).astype(low).reshape((every_count, channels))
    mixer_val = mixer_low.astype(full)
    selected = gather_rows(reduce_rows(matmul_lanes(mixer_low, select_proj)))
    step_low = selected[:, :R].astype(low)
    mats = jnp.pad(selected[:, R:], ((0, 0), (0, LANE - 2 * N)))
    scan_args = (step_low, mats, keep_mask, step_proj, step_bias, decay_rate, skip_gain)
    gated_low, mixer_out, prior = scan_forward(mixer_val, gate_input, *scan_args, packs)
    stream_mid = stream + reduce_rows(matmul(gated_low, out_proj).astype(low))

    first_in = take_in(mlp_one_in)
    first_out = take_out(mlp_one_out)
    stream_ffn, kept_first = feed_forward(stream_mid, gain_first, first_in, first_out)

    proj_flat = take_in(w_qkv)
    attn_out = take_out(w_o)
    inner_width = attn_out.shape[0]
    head_count = inner_width // HD
    scale_attn, normed_two = normed_rows(stream_ffn, gain_attn)
    every_two = gather_rows(normed_two)
    projected = matmul(every_two, proj_flat).reshape((packs, row_count, 3, head_count, HD))
    half_width = HD // 2
    inverse = 10000.0 ** (-jnp.arange(half_width, dtype=full) / half_width)
    angle_table = offset.astype(full)[:, :, None, None] * inverse
    cosine, sine_part = jnp.cos(angle_table), jnp.sin(angle_table)
    factor = float(HD) ** (-0.5)
    query_low = (rotated(projected[:, :, 0], cosine, sine_part) * factor).astype(low)
    key_low = rotated(projected[:, :, 1], cosine, sine_part).astype(low)
    value_low = projected[:, :, 2].astype(low)
    allowed = (segment[:, :, None] == segment[:, None, :]) & (
        row_index[:, None] >= row_index[None, :]
    )
    scores = jnp.einsum("pthd,pshd->phts", query_low, key_low, preferred_element_type=full)
    attn_probs = jax.nn.softmax(jnp.where(allowed[:, None], scores, -1e30), axis=-1)
    probs_low = attn_probs.astype(low)
    context_low = (
        jnp.einsum("phts,pshd->pthd", probs_low, value_low, preferred_element_type=full)
        .astype(low)
        .reshape((every_count, inner_width))
    )
    stream_attn = stream_ffn + reduce_rows(matmul(context_low, attn_out).astype(low))

    second_in = take_in(mlp_two_in)
    second_out = take_out(mlp_two_out)
    result, kept_second = feed_forward(stream_attn, gain_second, second_in, second_out)

    cot_in = lax.all_to_all(
        matmul(send_sel, cotangent).astype(low), "dp", split_axis=0, concat_axis=0, tiled=True
    )
    back_grad = matmul(own_sel, cot_in)
    grad_attn_stream, second_sums = feed_backward(
        back_grad, gather_rows(back_grad.astype(low)), stream_attn, kept_second, gain_second, second_in, second_out
    )

    every_branch = gather_rows(grad_attn_stream.astype(low))
    attn_depth = part
    grad_w_o = give_out(
        lambda block: matmul_rows(context_low, lanes_of(every_branch, block, count)),
        inner_width * GROUP, attn_depth,
    )
    grad_context = (
        matmul_lanes(every_branch, attn_out)
        .astype(low)
        .reshape((packs, row_count, head_count, HD))
    )
    grad_probs = jnp.einsum("pthd,pshd->phts", grad_context, value_low, preferred_element_type=full)
    grad_values = jnp.einsum("phts,pthd->pshd", probs_low, grad_context, preferred_element_type=full)
    grad_scores = (
        attn_probs * (grad_probs - jnp.sum(attn_probs * grad_probs, axis=-1, keepdims=True))
    ).astype(low)
    grad_query = (
        jnp.einsum("phts,pshd->pthd", grad_scores, key_low, preferred_element_type=full) * factor
    )
    grad_key = jnp.einsum("phts,pthd->pshd", grad_scores, query_low, preferred_element_type=full)
    grad_proj = jnp.stack(
        [rotated(grad_query, cosine, -sine_part), rotated(grad_key, cosine, -sine_part), grad_values], axis=2
    )
    grad_proj_low = grad_proj.astype(low).reshape((every_count, 3 * inner_width))
    grad_w_qkv = give_in(
        lambda block: matmul_rows(lanes_of(every_two, block, count), grad_proj_low),
        attn_depth, 3, inner_width * GROUP,
    )
    grad_normed_two = reduce_rows(matmul_lanes(grad_proj_low, proj_flat).astype(low))
    norm_ffn, grad_gain_two = norm_backward(stream_ffn, scale_attn, gain_attn, grad_normed_two)
    grad_ffn_stream = grad_attn_stream + norm_ffn

    grad_mid, first_sums = feed_backward(
        grad_ffn_stream, gather_rows(grad_ffn_stream.astype(low)), stream_mid, kept_first, gain_first,
        first_in, first_out,
    )

    every_mixed = gather_rows(grad_mid.astype(low))
    grad_gated = matmul_lanes(every_mixed, out_proj)
    if count == 2:
        half = channels // 2
        got = hop(matmul_rows(gated_low[:, half:], every_mixed).astype(low), "outer")
        grad_w_out = matmul_rows(gated_low[:, :half], every_mixed) + got.astype(full)
    else:
        grad_w_out = lax.psum_scatter(
            matmul_rows(gated_low, every_mixed).astype(low), "dp", axis_index_groups=outer_groups(),
            scatter_dimension=0, tiled=True,
        ).astype(full)
    grad_step_low, grad_mixer, grad_gate, mats_grad, grad_a_log, grad_skip = scan_backward(
        mixer_val, gate_input, mixer_out, grad_gated, *scan_args, prior, packs
    )
    grad_dt_bias = jnp.sum(grad_step_low.astype(full), axis=0, keepdims=True)
    grad_w_dt = matmul_rows(step_low, grad_step_low)
    grad_selected = gather_rows(
        reduce_rows(
            jnp.concatenate(
                [matmul_lanes(grad_step_low, step_proj), mats_grad[:, 0 : 2 * N : 2], mats_grad[:, 1 : 2 * N : 2]],
                axis=1,
            )
        ).astype(low)
    )
    grad_w_x = matmul_rows(grad_selected, mixer_low)
    grad_mixer = grad_mixer + matmul(grad_selected, select_proj)
    grad_conv = grad_mixer.reshape((packs, row_count, channels)) * silu_slope(conv_sum)
    grad_conv_bias = jnp.sum(grad_conv, axis=(0, 1))[None]
    tap_grads = [jnp.sum(grad_conv * conv_input, axis=(0, 1))]
    grad_conv_input = conv_taps[0] * grad_conv
    for tap in range(1, K):
        masked_grad = grad_conv * taps[tap]
        tap_grads.append(jnp.sum(masked_grad * shifted(conv_input, tap), axis=(0, 1)))
        grad_conv_input = grad_conv_input + conv_taps[tap] * shifted(masked_grad, -tap)
    grad_conv_low = grad_conv_input.astype(low).reshape((every_count, channels))
    grad_inner = jnp.concatenate([grad_conv_low, grad_gate], axis=1)
    grad_normed_one = reduce_rows(matmul_lanes(grad_inner, in_flat).astype(low))

    def in_grads(start, stop):
        columns = jnp.concatenate([grad_conv_low[:, start:stop], grad_gate[:, start:stop]], axis=1)
        return matmul_rows(every_one, columns).reshape((model_width, 2, stop - start))

    grad_w_in = channel_scatter(in_grads, channels, low)
    small_grads = jnp.concatenate(
        [grad_w_x, grad_w_dt, jnp.stack(tap_grads), grad_conv_bias, grad_dt_bias, grad_a_log, grad_skip], axis=0
    )
    small_sums = channel_scatter(lambda start, stop: small_grads[:, start:stop], channels, full)
    norm_in, grad_gain_one = norm_backward(stream, scale_mamba, gain_mamba, grad_normed_one)
    input_grad = grad_mid + norm_in

    def homeward(own_rows):
        pieces = ordered(own_rows, hop(own_rows, "x"), tensor_at)
        packed = jnp.concatenate(pieces, axis=0)
        return matmul_rows(arrive_sel, packed).astype(low).reshape((dp_count, slot, model_width))

    def landed(home):
        return matmul_rows(send_sel, home.reshape((row_count, model_width)))

    final_out = landed(
        lax.all_to_all(homeward(result.astype(low)), "dp", split_axis=0, concat_axis=0, tiled=True)
    )
    gain_grads = jnp.stack([grad_gain_one, first_sums[0], grad_gain_two, second_sums[0]])
    gain_grads = gain_grads + hop(gain_grads, "x")
    gain_high = gain_grads.astype(low)
    gain_parts = jnp.stack([gain_high, (gain_grads - gain_high.astype(full)).astype(low)])
    gain_parts = gain_parts.reshape((8, dp_count, part)).transpose((1, 0, 2)).reshape((dp_count, 8 * part))
    gain_width = -(-8 * part // (slot * LANE)) * LANE
    gain_parts = jnp.pad(gain_parts, ((0, 0), (0, slot * gain_width - 8 * part)))
    gain_parts = gain_parts.reshape((dp_count, slot, gain_width))
    home_grad = lax.all_to_all(
        jnp.concatenate([homeward(input_grad.astype(low)), gain_parts], axis=2),
        "dp", split_axis=0, concat_axis=0, tiled=True,
    )
    final_grad = landed(home_grad[:, :, :model_width])
    gain_sums = jnp.sum(
        home_grad[:, :, model_width:].reshape((dp_count, slot * gain_width))[:, : 8 * part].astype(full), axis=0
    )
    gain_sums = gain_sums.reshape((2, 4, part))
    gain_sums = gain_sums[0] + gain_sums[1]
    sizes = [select_rows, R, K, 1, 1, N, 1]
    cut_at = [sum(sizes[:k]) for k in range(len(sizes) + 1)]
    pieces = [small_sums[cut_at[k] : cut_at[k + 1]] for k in range(len(sizes))]
    return (
        final_out, final_grad, gain_sums[0], grad_w_in, pieces[2], pieces[3][0], pieces[0].T, pieces[1],
        pieces[4][0], pieces[5], pieces[6][0], grad_w_out, gain_sums[1], first_sums[1], first_sums[2],
        gain_sums[2], grad_w_qkv, grad_w_o, gain_sums[3], second_sums[1], second_sums[2],
    )


def solution(mesh):
    return jax.shard_map(
        shards,
        mesh=mesh,
        in_specs=(
            P("dp", None),
            P("dp", None),
            P("dp", None),
            P("dp", None),
            P("dp", None),
            P("dp"),
            P(None, None, ("dp", "tensor")),
            P(None, ("dp", "tensor")),
            P(("dp", "tensor")),
            P(("dp", "tensor"), None),
            P(None, ("dp", "tensor")),
            P(("dp", "tensor")),
            P(None, ("dp", "tensor")),
            P(("dp", "tensor")),
            P(("dp", "tensor"), None),
            P("dp"),
            P("dp", None, "tensor"),
            P("tensor", "dp"),
            P("dp"),
            P("dp", None, "tensor"),
            P("tensor", "dp"),
            P("dp"),
            P("dp", None, "tensor"),
            P("tensor", "dp"),
        ),
        out_specs=(
            P("dp", None),
            P("dp", None),
            P("dp"),
            P(None, None, ("dp", "tensor")),
            P(None, ("dp", "tensor")),
            P(("dp", "tensor")),
            P(("dp", "tensor"), None),
            P(None, ("dp", "tensor")),
            P(("dp", "tensor")),
            P(None, ("dp", "tensor")),
            P(("dp", "tensor")),
            P(("dp", "tensor"), None),
            P("dp"),
            P("dp", None, "tensor"),
            P("tensor", "dp"),
            P("dp"),
            P("dp", None, "tensor"),
            P("tensor", "dp"),
            P("dp"),
            P("dp", None, "tensor"),
            P("tensor", "dp"),
        ),
        check_vma=False,
    )
```

time: 5090 us -> 1790 us (0.35)
  waiting for transfers between devices: 3610 us -> 973 us
  blocking collectives: 359 us -> 19.9 us
  starting transfers between devices: 27.4 us -> 333 us
  local copies, waits for them, and re-layouts: 446 us -> 150 us
  matrix products: 318 us -> 120 us
  other arithmetic: 285 us -> 112 us
  Pallas kernels: 0 us -> 63.8 us
    reduce_scatter x11 -> x0, waiting for transfers between devices: 2840 us -> none  [the longest x2 1270 us: feed_backward(): lax.psum_scatter(grad_gate_up, 'dp', scatter_dimension=0, tiled=True)]
    ppermute x0 -> x221, waiting for transfers between devices: none -> 950 us  [the longest x158 863 us: hop(): lax.ppermute(values, 'dp', [(k, k ^ bit) for k in range(lax.axis_size('dp...]
    all_gather x8 -> x0, waiting for transfers between devices: 657 us -> none  [the longest x2 300 us: feed_weights(): lax.all_gather(gate_up, 'dp', axis=0, tiled=True)]
    ppermute x0 -> x221, starting transfers between devices: none -> 270 us  [the longest x158 202 us: hop(): lax.ppermute(values, 'dp', [(k, k ^ bit) for k in range(lax.axis_size('dp...]
    all_gather x11 -> x0, blocking collectives: 260 us -> none  [the longest x2 51.6 us: feed_weights(): lax.all_gather(gain_vec, 'dp', axis=0, tiled=True)]
    dot_general x36 -> x50, matrix products: 318 us -> 119 us  [the longest x22 61.7 us: matmul_rows(): lax.dot_general(left, right, (((0,), (0,)), ((), ())), preferred_element_...]
    mul x256 -> x0, local copies, waits for them, and re-layouts: 172 us -> none  [the longest x48 40.6 us: forward_terms(): step_now[:, None, :] * decay_rate[None]]
    all_gather x3 -> x0, local copies, waits for them, and re-layouts: 107 us -> none  [the longest x2 84.1 us: feed_weights(): lax.all_gather(gate_up, 'dp', axis=0, tiled=True)]
  transfers between devices with their start and end apart: 32 -> 236, of which waited for: 24 -> 133; matrix products, arithmetic and copies ran while one was open for 11% -> 17% of each run, Pallas kernels for 0% -> 2%
where the time goes in v1:
time: 1790 us; the launch traced here: 1780 us
  waiting for transfers between devices  973 us (54%)
  starting transfers between devices  333 us (19%)
  local copies, waits for them, and re-layouts  150 us (8%)
  matrix products  120 us (7%)
  other arithmetic  112 us (6%)
  Pallas kernels  63.8 us (4%)
  blocking collectives  19.9 us (1%)
    ppermute x158, waiting for transfers between devices, hop(): lax.ppermute(values, 'dp', [(k, k ^ bit) for k in range(lax.axis_size('dp...  863 us
    ppermute x158, starting transfers between devices, hop(): lax.ppermute(values, 'dp', [(k, k ^ bit) for k in range(lax.axis_size('dp...  202 us
    ppermute x63, waiting for transfers between devices, hop(): return lax.ppermute(values, 'tensor', [(0, 1), (1, 0)])  87 us
    ppermute x63, starting transfers between devices, hop(): return lax.ppermute(values, 'tensor', [(0, 1), (1, 0)])  67.3 us
    dot_general x22, matrix products, matmul_rows(): lax.dot_general(left, right, (((0,), (0,)), ((), ())), preferred_element_...  61.7 us
    unnamed x409, local copies, waits for them, and re-layouts  46.7 us
    all_to_all x11, starting transfers between devices, inner_swap(): lax.all_to_all(values, 'dp', split_axis=0, concat_axis=0, axis_index_grou...  45.1 us
    pallas_call x1, Pallas kernels, scan_backward(): pl.pallas_call(functools.partial(scan_backward_kernel, packs, chunk), gri...  43.1 us
  transfers between devices with their start and end apart: 236, of which 133 were waited for; matrix products, arithmetic and copies ran while one was open for 17% of the time, Pallas kernels for 2%

profile of v1, /device:TPU:0, one launch (start us, length us, event | category | flops | bytes accessed | tf_op | source)
XLA Modules:
  0.0 1778.3 jit_solution(9273686261346488748)
XLA Ops:
  6.8 7.4 all-to-all-start
  20.4 9.3 all-to-all-done
  30.9 36.2 %collective-permute-start.7 = (bf16[16,2048]{1,0:T(8,128)(2,1)S(1)}, bf16[16,2048]{1,0:T(8,128)(2,1)S(1)}, u32[]{:S(2)}, u32[]{:S(2)}) collective-permute-start(bf16[16,2048]{1,0:T(8,128)(2,1)S(1)} %get-tuple-element.367), channel_id=1, source_target_pairs={{0,8},{2,10},{4,12},{6,14},{8,0},{10,2},{12,4},{14,6},{16,24},{18,... | collective-permute-start | bytes 196616 | tf_op jit(solution)/shard_map/ppermute | solution.py:306
  70.6 31.9 %collective-permute-done.7 = bf16[16,2048]{1,0:T(8,128)(2,1)S(1)} collective-permute-done((bf16[16,2048]{1,0:T(8,128)(2,1)S(1)}, bf16[16,2048]{1,0:T(8,128)(2,1)S(1)}, u32[]{:S(2)}, u32[]{:S(2)}) %collective-permute-start.7) | collective-permute-done | bytes 65568 | tf_op jit(solution)/shard_map/ppermute | solution.py:306
  110.4 5.6 collective-permute-done.5
  117.4 7.6 collective-permute-done.6
  125.4 7.5 collective-permute-done.3
  195.0 20.7 %shard_map.400 = (bf16[1024,256]{1,0:T(8,128)(2,1)S(1)}, f32[1024,256]{1,0:T(8,128)S(1)}, f32[128,16,2,8,128]{4,3,2,1,0:T(8,128)}) custom-call(f32[1024,256]{1,0:T(8,128)S(1)} %bitcast_convert_fusion.3.mixer_ref, f32[1024,256]{1,0:T(8,128)S(1)} %get-tuple-element.212.gate_ref, bf16[1024,128]{1,0:T(8,128)(2,1)S(1)} %slice.2264.low_ref, ...), custom_call_target="tpu_custom_call" | custom-call | flops 33554432 | bytes 16777216 | tf_op jit(solution)/shard_map/pallas_call | solution.py:106
  221.0 6.2 copy.569
  242.2 23.6 %collective-permute-done.40 = bf16[2,2,16,2048]{3,2,0,1:T(8,128)(2,1)S(1)} collective-permute-done((bf16[2,2,16,2048]{3,2,0,1:T(8,128)(2,1)S(1)}, bf16[2,2,16,2048]{3,2,0,1:T(8,128)(2,1)S(1)}, u32[]{:S(2)}, u32[]{:S(2)}) %collective-permute-start.40) | collective-permute-done | bytes 262176 | tf_op jit(solution)/shard_map/ppermute | solution.py:306
  307.5 42.9 %collective-permute-done.47 = bf16[2,24,2048]{2,1,0:T(8,128)(2,1)S(1)} collective-permute-done((bf16[2,24,2048]{2,1,0:T(8,128)(2,1)S(1)}, bf16[2,24,2048]{2,1,0:T(8,128)(2,1)S(1)}, u32[]{:S(2)}, u32[]{:S(2)}) %collective-permute-start.47) | collective-permute-done | bytes 196640 | tf_op jit(solution)/shard_map/ppermute | solution.py:306
  355.8 5.7 collective-permute-done.48
  361.6 32.6 %collective-permute-done.45 = bf16[2,2,24,2048]{3,2,0,1:T(8,128)(2,1)S(1)} collective-permute-done((bf16[2,2,24,2048]{3,2,0,1:T(8,128)(2,1)S(1)}, bf16[2,2,24,2048]{3,2,0,1:T(8,128)(2,1)S(1)}, u32[]{:S(2)}, u32[]{:S(2)}) %collective-permute-start.45) | collective-permute-done | bytes 393248 | tf_op jit(solution)/shard_map/ppermute | solution.py:306
  398.1 48.5 %collective-permute-done.54 = bf16[512,1024]{0,1:T(8,128)(2,1)} collective-permute-done((bf16[512,1024]{0,1:T(8,128)(2,1)}, bf16[512,1024]{0,1:T(8,128)(2,1)}, u32[]{:S(2)}, u32[]{:S(2)}) %collective-permute-start.54) | collective-permute-done | bytes 1048608 | tf_op jit(solution)/shard_map/ppermute | solution.py:306
  454.9 4.6 fusion.2
  465.2 19.9 %all_to_all.87 = bf16[8,128,128]{2,1,0:T(8,128)(2,1)S(1)} all-to-all(bf16[8,128,128]{2,1,0:T(8,128)(2,1)S(1)} %bitcast.1414), channel_id=1, replica_groups={{0,2,4,6,8,10,12,14},{16,18,20,22,24,26,28,30},{1,3,5,7,9,11,13,15},{17..., dimensions={0} | all-to-all | bytes 524288 | tf_op jit(solution)/shard_map/all_to_all | solution.py:408
  493.5 4.9 copy.601
  501.0 5.6 collective-permute-done.76
  512.6 5.6 collective-permute-done.62
  545.0 4.6 collective-permute-done.65
  588.4 29.8 %collective-permute-done.75 = bf16[1024,384]{1,0:T(8,128)(2,1)S(1)} collective-permute-done((bf16[1024,384]{1,0:T(8,128)(2,1)S(1)}, bf16[1024,384]{1,0:T(8,128)(2,1)S(1)}, u32[]{:S(2)}, u32[]{:S(2)}) %collective-permute-start.75) | collective-permute-done | bytes 786464 | tf_op jit(solution)/shard_map/ppermute | solution.py:306
  683.8 22.4 %collective-permute-done.83 = bf16[24,2048]{1,0:T(8,128)(2,1)S(1)} collective-permute-done((bf16[24,2048]{1,0:T(8,128)(2,1)S(1)}, bf16[24,2048]{1,0:T(8,128)(2,1)S(1)}, u32[]{:S(2)}, u32[]{:S(2)}) %collective-permute-start.83) | collective-permute-done | bytes 98336 | tf_op jit(solution)/shard_map/ppermute | solution.py:306
  734.5 56.0 %collective-permute-done.91 = bf16[2,24,2048]{2,1,0:T(8,128)(2,1)S(1)} collective-permute-done((bf16[2,24,2048]{2,1,0:T(8,128)(2,1)S(1)}, bf16[2,24,2048]{2,1,0:T(8,128)(2,1)S(1)}, u32[]{:S(2)}, u32[]{:S(2)}) %collective-permute-start.91) | collective-permute-done | bytes 196640 | tf_op jit(solution)/shard_map/ppermute | solution.py:306
  792.4 9.0 collective-permute-done.92
  803.9 58.9 %collective-permute-done.89 = bf16[2,2,24,2048]{3,2,0,1:T(8,128)(2,1)S(1)} collective-permute-done((bf16[2,2,24,2048]{3,2,0,1:T(8,128)(2,1)S(1)}, bf16[2,2,24,2048]{3,2,0,1:T(8,128)(2,1)S(1)}, u32[]{:S(2)}, u32[]{:S(2)}) %collective-permute-start.89) | collective-permute-done | bytes 393248 | tf_op jit(solution)/shard_map/ppermute | solution.py:306
  871.5 4.6 fusion.1
  883.6 6.3 convolution_convert_fusion.7
  900.0 4.7 collective-permute-done.106
  905.1 6.7 collective-permute-done.127
  953.0 6.7 collective-permute-done.134
  962.8 4.7 collective-permute-done.135
  996.2 5.6 collective-permute-done.147
  1032.5 6.6 collective-permute-done.154
  1042.2 4.8 collective-permute-done.155
  1057.2 6.0 fusion.36
  1063.3 85.7 %collective-permute-done.220 = bf16[512,1024]{1,0:T(8,128)(2,1)} collective-permute-done((bf16[512,1024]{1,0:T(8,128)(2,1)}, bf16[512,1024]{1,0:T(8,128)(2,1)}, u32[]{:S(2)}, u32[]{:S(2)}) %collective-permute-start.220) | collective-permute-done | bytes 1048608 | tf_op jit(solution)/shard_map/ppermute | solution.py:306
  1164.9 6.5 convolution_convert_fusion.6
  1173.6 20.1 %collective-permute-done.219 = bf16[1024,1024]{1,0:T(8,128)(2,1)} collective-permute-done((bf16[1024,1024]{1,0:T(8,128)(2,1)}, bf16[1024,1024]{1,0:T(8,128)(2,1)}, u32[]{:S(2)}, u32[]{:S(2)}) %collective-permute-start.219) | collective-permute-done | bytes 2097184 | tf_op jit(solution)/shard_map/ppermute | solution.py:306
  1193.7 5.3 add_convert_fusion
  1208.3 23.5 %collective-permute-done.218 = bf16[128,1024]{1,0:T(8,128)(2,1)S(1)} collective-permute-done((bf16[128,1024]{1,0:T(8,128)(2,1)S(1)}, bf16[128,1024]{1,0:T(8,128)(2,1)S(1)}, u32[]{:S(2)}, u32[]{:S(2)}) %collective-permute-start.218) | collective-permute-done | bytes 262176 | tf_op jit(solution)/shard_map/ppermute | solution.py:306
  1233.0 15.4 collective-permute-done.217
  1252.9 5.9 fusion.33
  1264.3 6.1 collective-permute-done.167
  1289.2 12.8 all-to-all-done.7
  1319.4 30.6 %collective-permute-done.176 = bf16[16,2048]{1,0:T(8,128)(2,1)S(1)} collective-permute-done((bf16[16,2048]{1,0:T(8,128)(2,1)S(1)}, bf16[16,2048]{1,0:T(8,128)(2,1)S(1)}, u32[]{:S(2)}, u32[]{:S(2)}) %collective-permute-start.176) | collective-permute-done | bytes 65568 | tf_op jit(solution)/shard_map/ppermute | solution.py:306
  1357.1 46.2 %collective-permute-done.174 = bf16[2,24,2048]{2,1,0:T(8,128)(2,1)S(1)} collective-permute-done((bf16[2,24,2048]{2,1,0:T(8,128)(2,1)S(1)}, bf16[2,24,2048]{2,1,0:T(8,128)(2,1)S(1)}, u32[]{:S(2)}, u32[]{:S(2)}) %collective-permute-start.174) | collective-permute-done | bytes 196640 | tf_op jit(solution)/shard_map/ppermute | solution.py:306
  1415.6 46.9 %collective-permute-done.172 = bf16[2,2,24,2048]{3,2,0,1:T(8,128)(2,1)} collective-permute-done((bf16[2,2,24,2048]{3,2,0,1:T(8,128)(2,1)}, bf16[2,2,24,2048]{3,2,0,1:T(8,128)(2,1)}, u32[]{:S(2)}, u32[]{:S(2)}) %collective-permute-start.172) | collective-permute-done | bytes 393248 | tf_op jit(solution)/shard_map/ppermute | solution.py:306
  1473.6 5.1 reshape.784
  1478.8 6.6 copy.856
  1485.3 6.6 reshape.780
  1501.4 4.5 all-to-all-start.11
  1505.9 6.6 add_convert_fusion.1
  1519.3 43.1 %shard_map.401 = (bf16[1024,256]{1,0:T(8,128)(2,1)}, f32[1024,256]{1,0:T(8,128)}, bf16[1024,256]{1,0:T(8,128)(2,1)}, f32[1024,128]{1,0:T(8,128)}, f32[16,256]{1,0:T(8,128)}, /*index=5*/f32[1,256]{1,0:T(1,128)}) custom-call(f32[1024,256]{1,0:T(8,128)} %copy-done.2, f32[1024,256]{1,0:T(8,128)} %copy-done.3, f32[1024,256]{1,0:T(8,128)} %copy-done.9, ...), custom_call_target="tpu_custom_call" | custom-call | flops 83886080 | bytes 16777216 | tf_op jit(solution)/shard_map/pallas_call | solution.py:254
  1566.8 4.4 slice.1288
  1584.9 20.8 %collective-permute-done.193 = f32[2,2,16,160]{3,2,0,1:T(8,128)S(1)} collective-permute-done((f32[2,2,16,160]{3,2,0,1:T(8,128)S(1)}, f32[2,2,16,160]{3,2,0,1:T(8,128)S(1)}, u32[]{:S(2)}, u32[]{:S(2)}) %collective-permute-start.193) | collective-permute-done | bytes 40992 | tf_op jit(solution)/shard_map/ppermute | solution.py:306
  1656.5 5.1 reshape.782
  1661.6 6.6 copy.857
  1668.2 6.8 reshape.776
  1681.9 4.7 convolution_convert_fusion.8
  1693.8 5.2 collective-permute-done.207
  1700.1 18.9 %collective-permute-done.201 = bf16[2,2,24,2048]{3,2,1,0:T(8,128)(2,1)S(1)} collective-permute-done((bf16[2,2,24,2048]{3,2,1,0:T(8,128)(2,1)S(1)}, bf16[2,2,24,2048]{3,2,1,0:T(8,128)(2,1)S(1)}, u32[]{:S(2)}, u32[]{:S(2)}) %collective-permute-start.201) | collective-permute-done | bytes 393248 | tf_op jit(solution)/shard_map/ppermute | solution.py:306
  1722.8 13.9 collective-permute-done.209
  1750.4 4.4 collective-permute-done.210
  1767.3 8.6 copy.681
  (1360 shorter events, 731.2 us)
Async XLA Ops:
  6.8 22.9 %all-to-all-start = ((bf16[16,8,2176]{2,1,0:T(8,128)(2,1)}), bf16[16,8,2176]{2,1,0:T(8,128)(2,1)S(1)}, u32[]{:S(2)}, u32[]{:S(2)}) async-start(bf16[16,8,2176]{2,1,0:T(8,128)(2,1)} %pad_maximum_fusion.42), calls=%async_computation | async-start | bytes 1114112 | tf_op jit(solution)/shard_map/all_to_all | solution.py:521
  14.2 120.9 %collective-permute-start.11 = (bf16[2048,2,128]{2,1,0:T(2,128)(2,1)}, bf16[2048,2,128]{2,1,0:T(2,128)(2,1)}, u32[]{:S(2)}, u32[]{:S(2)}) collective-permute-start(bf16[2048,2,128]{2,1,0:T(2,128)(2,1)} %param.31), channel_id=1, source_target_pairs={{0,16},{2,18},{4,20},{6,22},{8,24},{10,26},{12,28},{14,30},{16,0},... | collective-permute-start | bytes 3145736 | tf_op jit(solution)/shard_map/ppermute | solution.py:306
  17.3 117.1 %collective-permute-start = (bf16[311,128]{1,0:T(8,128)(2,1)S(1)}, bf16[311,128]{1,0:T(8,128)(2,1)S(1)}, u32[]{:S(2)}, u32[]{:S(2)}) collective-permute-start(bf16[311,128]{1,0:T(8,128)(2,1)S(1)} %concatenate.162), channel_id=1, source_target_pairs={{0,16},{2,18},{4,20},{6,22},{8,24},{10,26},{12,28},{14,30},{16,0},... | collective-permute-start | bytes 238856 | tf_op jit(solution)/shard_map/ppermute | solution.py:306
  17.6 172.1 %collective-permute-start.32 = (bf16[128,2048]{1,0:T(8,128)(2,1)}, bf16[128,2048]{1,0:T(8,128)(2,1)}, u32[]{:S(2)}, u32[]{:S(2)}) collective-permute-start(bf16[128,2048]{1,0:T(8,128)(2,1)} %param.39), channel_id=1, source_target_pairs={{0,16},{2,18},{4,20},{6,22},{8,24},{10,26},{12,28},{14,30},{16,0},... | collective-permute-start | bytes 1572872 | tf_op jit(solution)/shard_map/ppermute | solution.py:306
  30.9 71.5 %collective-permute-start.7 = (bf16[16,2048]{1,0:T(8,128)(2,1)S(1)}, bf16[16,2048]{1,0:T(8,128)(2,1)S(1)}, u32[]{:S(2)}, u32[]{:S(2)}) collective-permute-start(bf16[16,2048]{1,0:T(8,128)(2,1)S(1)} %get-tuple-element.367), channel_id=1, source_target_pairs={{0,8},{2,10},{4,12},{6,14},{8,0},{10,2},{12,4},{14,6},{16,24},{18,... | collective-permute-start | bytes 196616 | tf_op jit(solution)/shard_map/ppermute | solution.py:306
  69.1 35.0 %collective-permute-start.1 = (bf16[24,2048]{1,0:T(8,128)(2,1)S(1)}, bf16[24,2048]{1,0:T(8,128)(2,1)S(1)}, u32[]{:S(2)}, u32[]{:S(2)}) collective-permute-start(bf16[24,2048]{1,0:T(8,128)(2,1)S(1)} %slice.1361), channel_id=1, source_target_pairs={{0,1},{1,0},{2,3},{3,2},{4,5},{5,4},{6,7},{7,6},{8,9},{9,8},{10,11... | collective-permute-start | bytes 294920 | tf_op jit(solution)/shard_map/ppermute | solution.py:304
  230.3 54.5 %all-to-all-start.1 = ((bf16[8,128,1024]{1,2,0:T(8,128)(2,1)}), bf16[8,128,1024]{1,2,0:T(8,128)(2,1)}, u32[]{:S(2)}, u32[]{:S(2)}) async-start(bf16[8,128,1024]{1,2,0:T(8,128)(2,1)} %bitcast.1301), calls=%async_computation.1 | async-start | bytes 4194304 | tf_op jit(solution)/shard_map/all_to_all | solution.py:408
  237.7 30.9 %collective-permute-start.34 = (bf16[2,2,24,2048]{3,2,1,0:T(8,128)(2,1)S(1)}, bf16[2,2,24,2048]{3,2,1,0:T(8,128)(2,1)S(1)}, u32[]{:S(2)}, u32[]{:S(2)}) collective-permute-start(bf16[2,2,24,2048]{3,2,1,0:T(8,128)(2,1)S(1)} %slice_bitcast_fusion.44), channel_id=1, source_target_pairs={{0,8},{2,10},{4,12},{6,14},{8,0},{10,2},{12,4},{14,6},{16,24},{18,... | collective-permute-start | bytes 1179656 | tf_op jit(solution)/shard_map/ppermute | solution.py:306
  239.7 26.1 %collective-permute-start.40 = (bf16[2,2,16,2048]{3,2,0,1:T(8,128)(2,1)S(1)}, bf16[2,2,16,2048]{3,2,0,1:T(8,128)(2,1)S(1)}, u32[]{:S(2)}, u32[]{:S(2)}) collective-permute-start(bf16[2,2,16,2048]{3,2,0,1:T(8,128)(2,1)S(1)} %slice_bitcast_fusion.52), channel_id=1, source_target_pairs={{0,4},{2,6},{4,0},{6,2},{8,12},{10,14},{12,8},{14,10},{16,20},{18,... | collective-permute-start | bytes 786440 | tf_op jit(solution)/shard_map/ppermute | solution.py:306
  241.3 31.4 %collective-permute-start.37 = (bf16[2,2,24,2048]{3,2,1,0:T(8,128)(2,1)S(1)}, bf16[2,2,24,2048]{3,2,1,0:T(8,128)(2,1)S(1)}, u32[]{:S(2)}, u32[]{:S(2)}) collective-permute-start(bf16[2,2,24,2048]{3,2,1,0:T(8,128)(2,1)S(1)} %fusion.128), channel_id=1, source_target_pairs={{0,1},{1,0},{2,3},{3,2},{4,5},{5,4},{6,7},{7,6},{8,9},{9,8},{10,11... | collective-permute-start | bytes 1179656 | tf_op jit(solution)/shard_map/ppermute | solution.py:304
  284.8 111.0 %all-to-all-start.2 = ((bf16[8,512,128]{2,1,0:T(8,128)(2,1)}), bf16[8,512,128]{2,1,0:T(8,128)(2,1)}, u32[]{:S(2)}, u32[]{:S(2)}) async-start(bf16[8,512,128]{2,1,0:T(8,128)(2,1)} %bitcast.135), calls=%async_computation.2 | async-start | bytes 2097152 | tf_op jit(solution)/shard_map/all_to_all | solution.py:408
  291.9 156.4 %collective-permute-start.53 = (bf16[1024,1024]{1,0:T(8,128)(2,1)S(1)}, bf16[1024,1024]{1,0:T(8,128)(2,1)}, u32[]{:S(2)}, u32[]{:S(2)}) collective-permute-start(bf16[1024,1024]{1,0:T(8,128)(2,1)S(1)} %bitcast.1305), channel_id=1, source_target_pairs={{0,16},{2,18},{4,20},{6,22},{8,24},{10,26},{12,28},{14,30},{16,0},... | collective-permute-start | bytes 6291464 | tf_op jit(solution)/shard_map/ppermute | solution.py:306
  300.5 52.7 %collective-permute-start.44 = (bf16[2,24,2048]{2,1,0:T(8,128)(2,1)S(1)}, bf16[2,24,2048]{2,1,0:T(8,128)(2,1)S(1)}, u32[]{:S(2)}, u32[]{:S(2)}) collective-permute-start(bf16[2,24,2048]{2,1,0:T(8,128)(2,1)S(1)} %get-tuple-element.393), channel_id=1, source_target_pairs={{0,4},{2,6},{4,0},{6,2},{8,12},{10,14},{12,8},{14,10},{16,20},{18,... | collective-permute-start | bytes 589832 | tf_op jit(solution)/shard_map/ppermute | solution.py:306
  304.5 46.0 %collective-permute-start.47 = (bf16[2,24,2048]{2,1,0:T(8,128)(2,1)S(1)}, bf16[2,24,2048]{2,1,0:T(8,128)(2,1)S(1)}, u32[]{:S(2)}, u32[]{:S(2)}) collective-permute-start(bf16[2,24,2048]{2,1,0:T(8,128)(2,1)S(1)} %get-tuple-element.395), channel_id=1, source_target_pairs={{0,8},{2,10},{4,12},{6,14},{8,0},{10,2},{12,4},{14,6},{16,24},{18,... | collective-permute-start | bytes 589832 | tf_op jit(solution)/shard_map/ppermute | solution.py:306
  353.2 40.9 %collective-permute-start.45 = (bf16[2,2,24,2048]{3,2,0,1:T(8,128)(2,1)S(1)}, bf16[2,2,24,2048]{3,2,0,1:T(8,128)(2,1)S(1)}, u32[]{:S(2)}, u32[]{:S(2)}) collective-permute-start(bf16[2,2,24,2048]{3,2,0,1:T(8,128)(2,1)S(1)} %get-tuple-element.281), channel_id=1, source_target_pairs={{0,8},{2,10},{4,12},{6,14},{8,0},{10,2},{12,4},{14,6},{16,24},{18,... | collective-permute-start | bytes 1179656 | tf_op jit(solution)/shard_map/ppermute | solution.py:306
  395.7 55.6 %collective-permute-start.52 = (bf16[2,2,2,64,2048]{4,3,1,0,2:T(8,128)(2,1)}, bf16[2,2,2,64,2048]{4,3,1,0,2:T(8,128)(2,1)}, u32[]{:S(2)}, u32[]{:S(2)}) collective-permute-start(bf16[2,2,2,64,2048]{4,3,1,0,2:T(8,128)(2,1)} %pad_maximum_fusion.16), channel_id=1, source_target_pairs={{0,2},{2,0},{4,6},{6,4},{8,10},{10,8},{12,14},{14,12},{16,18},{18,... | collective-permute-start | bytes 6291464 | tf_op jit(solution)/shard_map/ppermute | solution.py:306
  398.1 48.5 %collective-permute-start.54 = (bf16[512,1024]{0,1:T(8,128)(2,1)}, bf16[512,1024]{0,1:T(8,128)(2,1)}, u32[]{:S(2)}, u32[]{:S(2)}) collective-permute-start(bf16[512,1024]{0,1:T(8,128)(2,1)} %bitcast.1329), channel_id=1, source_target_pairs={{0,16},{2,18},{4,20},{6,22},{8,24},{10,26},{12,28},{14,30},{16,0},... | collective-permute-start | bytes 3145736 | tf_op jit(solution)/shard_map/ppermute | solution.py:306
  465.1 43.3 %collective-permute-start.55 = (bf16[2,2,2,64,2048]{4,3,2,1,0:T(8,128)(2,1)}, bf16[2,2,2,64,2048]{4,3,2,1,0:T(8,128)(2,1)}, u32[]{:S(2)}, u32[]{:S(2)}) collective-permute-start(bf16[2,2,2,64,2048]{4,3,2,1,0:T(8,128)(2,1)} %bitcast.139), channel_id=1, source_target_pairs={{0,2},{2,0},{4,6},{6,4},{8,10},{10,8},{12,14},{14,12},{16,18},{18,... | collective-permute-start | bytes 6291464 | tf_op jit(solution)/shard_map/ppermute | solution.py:306
  488.6 47.9 %all-to-all-start.8 = ((bf16[16,8,2048]{2,1,0:T(8,128)(2,1)}), bf16[16,8,2048]{2,1,0:T(8,128)(2,1)S(1)}, u32[]{:S(2)}, u32[]{:S(2)}) async-start(bf16[16,8,2048]{2,1,0:T(8,128)(2,1)} %fusion.5), calls=%async_computation.8 | async-start | bytes 1048576 | tf_op jit(solution)/shard_map/all_to_all | solution.py:623
  536.4 39.4 %all-to-all-start.3 = ((bf16[8,128,384]{1,2,0:T(8,128)(2,1)}), bf16[8,128,384]{1,2,0:T(8,128)(2,1)S(1)}, u32[]{:S(2)}, u32[]{:S(2)}) async-start(bf16[8,128,384]{1,2,0:T(8,128)(2,1)} %bitcast.189), calls=%async_computation.3 | async-start | bytes 1572864 | tf_op jit(solution)/shard_map/all_to_all | solution.py:408
  541.7 92.1 %collective-permute-start.110 = (bf16[24,2048]{1,0:T(8,128)(2,1)}, bf16[24,2048]{1,0:T(8,128)(2,1)}, u32[]{:S(2)}, u32[]{:S(2)}) collective-permute-start(bf16[24,2048]{1,0:T(8,128)(2,1)} %slice.1498), channel_id=1, source_target_pairs={{0,1},{1,0},{2,3},{3,2},{4,5},{5,4},{6,7},{7,6},{8,9},{9,8},{10,11... | collective-permute-start | bytes 294920 | tf_op jit(solution)/shard_map/ppermute | solution.py:304
  573.7 49.0 %collective-permute-start.74 = (bf16[2,2,2,64,2048]{4,3,1,0,2:T(8,128)(2,1)}, bf16[2,2,2,64,2048]{4,3,1,0,2:T(8,128)(2,1)}, u32[]{:S(2)}, u32[]{:S(2)}) collective-permute-start(bf16[2,2,2,64,2048]{4,3,1,0,2:T(8,128)(2,1)} %pad_maximum_fusion.18), channel_id=1, source_target_pairs={{0,2},{2,0},{4,6},{6,4},{8,10},{10,8},{12,14},{14,12},{16,18},{18,... | collective-permute-start | bytes 6291464 | tf_op jit(solution)/shard_map/ppermute | solution.py:306
  575.9 98.8 %all-to-all-start.6 = ((bf16[8,512,128]{2,1,0:T(8,128)(2,1)}), bf16[8,512,128]{2,1,0:T(8,128)(2,1)}, u32[]{:S(2)}, u32[]{:S(2)}) async-start(bf16[8,512,128]{2,1,0:T(8,128)(2,1)} %bitcast.1388), calls=%async_computation.6 | async-start | bytes 2097152 | tf_op jit(solution)/shard_map/all_to_all | solution.py:408
  580.5 37.7 %collective-permute-start.75 = (bf16[1024,384]{1,0:T(8,128)(2,1)S(1)}, bf16[1024,384]{1,0:T(8,128)(2,1)S(1)}, u32[]{:S(2)}, u32[]{:S(2)}) collective-permute-start(bf16[1024,384]{1,0:T(8,128)(2,1)S(1)} %bitcast.1349), channel_id=1, source_target_pairs={{0,16},{2,18},{4,20},{6,22},{8,24},{10,26},{12,28},{14,30},{16,0},... | collective-permute-start | bytes 2359304 | tf_op jit(solution)/shard_map/ppermute | solution.py:306
  587.4 54.4 %collective-permute-start.117 = (bf16[2,16,2048]{2,1,0:T(8,128)(2,1)}, bf16[2,16,2048]{2,1,0:T(8,128)(2,1)}, u32[]{:S(2)}, u32[]{:S(2)}) collective-permute-start(bf16[2,16,2048]{2,1,0:T(8,128)(2,1)} %pad_maximum_fusion.107), channel_id=1, source_target_pairs={{0,1},{1,0},{2,3},{3,2},{4,5},{5,4},{6,7},{7,6},{8,9},{9,8},{10,11... | collective-permute-start | bytes 393224 | tf_op jit(solution)/shard_map/ppermute | solution.py:304
  648.3 62.0 %collective-permute-start.118 = (bf16[2,2,16,2048]{3,2,0,1:T(8,128)(2,1)}, bf16[2,2,16,2048]{3,2,0,1:T(8,128)(2,1)}, u32[]{:S(2)}, u32[]{:S(2)}) collective-permute-start(bf16[2,2,16,2048]{3,2,0,1:T(8,128)(2,1)} %get-tuple-element.329), channel_id=1, source_target_pairs={{0,4},{2,6},{4,0},{6,2},{8,12},{10,14},{12,8},{14,10},{16,20},{18,... | collective-permute-start | bytes 786440 | tf_op jit(solution)/shard_map/ppermute | solution.py:306
  650.9 59.4 %collective-permute-start.112 = (bf16[2,2,24,2048]{3,2,1,0:T(8,128)(2,1)}, bf16[2,2,24,2048]{3,2,1,0:T(8,128)(2,1)}, u32[]{:S(2)}, u32[]{:S(2)}) collective-permute-start(bf16[2,2,24,2048]{3,2,1,0:T(8,128)(2,1)} %get-tuple-element.275), channel_id=1, source_target_pairs={{0,8},{2,10},{4,12},{6,14},{8,0},{10,2},{12,4},{14,6},{16,24},{18,... | collective-permute-start | bytes 1179656 | tf_op jit(solution)/shard_map/ppermute | solution.py:306
  674.7 43.3 %all-to-all-start.5 = ((bf16[8,128,1024]{1,2,0:T(8,128)(2,1)}), bf16[8,128,1024]{1,2,0:T(8,128)(2,1)S(1)}, u32[]{:S(2)}, u32[]{:S(2)}) async-start(bf16[8,128,1024]{1,2,0:T(8,128)(2,1)} %bitcast.250), calls=%async_computation.5 | async-start | bytes 4194304 | tf_op jit(solution)/shard_map/all_to_all | solution.py:408
  680.9 25.4 %collective-permute-start.83 = (bf16[24,2048]{1,0:T(8,128)(2,1)S(1)}, bf16[24,2048]{1,0:T(8,128)(2,1)S(1)}, u32[]{:S(2)}, u32[]{:S(2)}) collective-permute-start(bf16[24,2048]{1,0:T(8,128)(2,1)S(1)} %fusion.219), channel_id=1, source_target_pairs={{0,4},{2,6},{4,0},{6,2},{8,12},{10,14},{12,8},{14,10},{16,20},{18,... | collective-permute-start | bytes 294920 | tf_op jit(solution)/shard_map/ppermute | solution.py:306
  712.8 153.1 %collective-permute-start.119 = (bf16[2,2,2,64,2048]{4,3,1,0,2:T(8,128)(2,1)}, bf16[2,2,2,64,2048]{4,3,1,0,2:T(8,128)(2,1)}, u32[]{:S(2)}, u32[]{:S(2)}) collective-permute-start(bf16[2,2,2,64,2048]{4,3,1,0,2:T(8,128)(2,1)} %maximum_maximum_fusion), channel_id=1, source_target_pairs={{0,2},{2,0},{4,6},{6,4},{8,10},{10,8},{12,14},{14,12},{16,18},{18,... | collective-permute-start | bytes 6291464 | tf_op jit(solution)/shard_map/ppermute | solution.py:306
  715.0 149.4 %collective-permute-start.98 = (bf16[512,1024]{0,1:T(8,128)(2,1)}, bf16[512,1024]{0,1:T(8,128)(2,1)}, u32[]{:S(2)}, u32[]{:S(2)}) collective-permute-start(bf16[512,1024]{0,1:T(8,128)(2,1)} %bitcast.1328), channel_id=1, source_target_pairs={{0,16},{2,18},{4,20},{6,22},{8,24},{10,26},{12,28},{14,30},{16,0},... | collective-permute-start | bytes 3145736 | tf_op jit(solution)/shard_map/ppermute | solution.py:306
  720.6 147.6 %collective-permute-start.97 = (bf16[1024,1024]{1,0:T(8,128)(2,1)}, bf16[1024,1024]{1,0:T(8,128)(2,1)S(1)}, u32[]{:S(2)}, u32[]{:S(2)}) collective-permute-start(bf16[1024,1024]{1,0:T(8,128)(2,1)} %bitcast.1306), channel_id=1, source_target_pairs={{0,16},{2,18},{4,20},{6,22},{8,24},{10,26},{12,28},{14,30},{16,0},... | collective-permute-start | bytes 6291464 | tf_op jit(solution)/shard_map/ppermute | solution.py:306
  732.5 59.1 %collective-permute-start.88 = (bf16[2,24,2048]{2,1,0:T(8,128)(2,1)S(1)}, bf16[2,24,2048]{2,1,0:T(8,128)(2,1)S(1)}, u32[]{:S(2)}, u32[]{:S(2)}) collective-permute-start(bf16[2,24,2048]{2,1,0:T(8,128)(2,1)S(1)} %get-tuple-element.385), channel_id=1, source_target_pairs={{0,4},{2,6},{4,0},{6,2},{8,12},{10,14},{12,8},{14,10},{16,20},{18,... | collective-permute-start | bytes 589832 | tf_op jit(solution)/shard_map/ppermute | solution.py:306
  733.1 57.4 %collective-permute-start.91 = (bf16[2,24,2048]{2,1,0:T(8,128)(2,1)S(1)}, bf16[2,24,2048]{2,1,0:T(8,128)(2,1)S(1)}, u32[]{:S(2)}, u32[]{:S(2)}) collective-permute-start(bf16[2,24,2048]{2,1,0:T(8,128)(2,1)S(1)} %get-tuple-element.387), channel_id=1, source_target_pairs={{0,8},{2,10},{4,12},{6,14},{8,0},{10,2},{12,4},{14,6},{16,24},{18,... | collective-permute-start | bytes 589832 | tf_op jit(solution)/shard_map/ppermute | solution.py:306
  801.4 61.5 %collective-permute-start.89 = (bf16[2,2,24,2048]{3,2,0,1:T(8,128)(2,1)S(1)}, bf16[2,2,24,2048]{3,2,0,1:T(8,128)(2,1)S(1)}, u32[]{:S(2)}, u32[]{:S(2)}) collective-permute-start(bf16[2,2,24,2048]{3,2,0,1:T(8,128)(2,1)S(1)} %get-tuple-element.277), channel_id=1, source_target_pairs={{0,8},{2,10},{4,12},{6,14},{8,0},{10,2},{12,4},{14,6},{16,24},{18,... | collective-permute-start | bytes 1179656 | tf_op jit(solution)/shard_map/ppermute | solution.py:306
  896.9 23.9 %collective-permute-start.124 = (bf16[2,2,24,2048]{3,2,1,0:T(8,128)(2,1)S(1)}, bf16[2,2,24,2048]{3,2,1,0:T(8,128)(2,1)S(1)}, u32[]{:S(2)}, u32[]{:S(2)}) collective-permute-start(bf16[2,2,24,2048]{3,2,1,0:T(8,128)(2,1)S(1)} %fusion.133), channel_id=1, source_target_pairs={{0,1},{1,0},{2,3},{3,2},{4,5},{5,4},{6,7},{7,6},{8,9},{9,8},{10,11... | collective-permute-start | bytes 1179656 | tf_op jit(solution)/shard_map/ppermute | solution.py:304
  898.0 23.0 %collective-permute-start.121 = (bf16[2,2,24,2048]{3,2,1,0:T(8,128)(2,1)S(1)}, bf16[2,2,24,2048]{3,2,1,0:T(8,128)(2,1)S(1)}, u32[]{:S(2)}, u32[]{:S(2)}) collective-permute-start(bf16[2,2,24,2048]{3,2,1,0:T(8,128)(2,1)S(1)} %slice_bitcast_fusion.32), channel_id=1, source_target_pairs={{0,8},{2,10},{4,12},{6,14},{8,0},{10,2},{12,4},{14,6},{16,24},{18,... | collective-permute-start | bytes 1179656 | tf_op jit(solution)/shard_map/ppermute | solution.py:306
  1050.1 107.0 %collective-permute-start.159 = (bf16[2,2,2,64,2048]{4,3,2,1,0:T(8,128)(2,1)}, bf16[2,2,2,64,2048]{4,3,2,1,0:T(8,128)(2,1)}, u32[]{:S(2)}, u32[]{:S(2)}) collective-permute-start(bf16[2,2,2,64,2048]{4,3,2,1,0:T(8,128)(2,1)} %maximum_maximum_fusion.2), channel_id=1, source_target_pairs={{0,2},{2,0},{4,6},{6,4},{8,10},{10,8},{12,14},{14,12},{16,18},{18,... | collective-permute-start | bytes 6291464 | tf_op jit(solution)/shard_map/ppermute | solution.py:306
  1054.4 94.7 %collective-permute-start.220 = (bf16[512,1024]{1,0:T(8,128)(2,1)}, bf16[512,1024]{1,0:T(8,128)(2,1)}, u32[]{:S(2)}, u32[]{:S(2)}) collective-permute-start(bf16[512,1024]{1,0:T(8,128)(2,1)} %fusion.46), channel_id=1, source_target_pairs={{0,16},{2,18},{4,20},{6,22},{8,24},{10,26},{12,28},{14,30},{16,0},... | collective-permute-start | bytes 3145736 | tf_op jit(solution)/shard_map/ppermute | solution.py:306
  1063.2 130.5 %collective-permute-start.219 = (bf16[1024,1024]{1,0:T(8,128)(2,1)}, bf16[1024,1024]{1,0:T(8,128)(2,1)}, u32[]{:S(2)}, u32[]{:S(2)}) collective-permute-start(bf16[1024,1024]{1,0:T(8,128)(2,1)} %fusion.36), channel_id=1, source_target_pairs={{0,16},{2,18},{4,20},{6,22},{8,24},{10,26},{12,28},{14,30},{16,0},... | collective-permute-start | bytes 6291464 | tf_op jit(solution)/shard_map/ppermute | solution.py:306
  1152.7 131.3 %all-to-all-start.15 = ((bf16[8,512,128]{2,1,0:T(8,128)(2,1)}), bf16[8,512,128]{2,1,0:T(8,128)(2,1)}, u32[]{:S(2)}, u32[]{:S(2)}) async-start(bf16[8,512,128]{2,1,0:T(8,128)(2,1)} %bitcast.1275), calls=%async_computation.15 | async-start | bytes 2097152 | tf_op jit(solution)/shard_map/all_to_all | solution.py:408
  1173.2 85.6 %collective-permute-start.160 = (bf16[2,2,2,64,2048]{4,3,2,1,0:T(8,128)(2,1)}, bf16[2,2,2,64,2048]{4,3,2,1,0:T(8,128)(2,1)}, u32[]{:S(2)}, u32[]{:S(2)}) collective-permute-start(bf16[2,2,2,64,2048]{4,3,2,1,0:T(8,128)(2,1)} %bitcast.396), channel_id=1, source_target_pairs={{0,2},{2,0},{4,6},{6,4},{8,10},{10,8},{12,14},{14,12},{16,18},{18,... | collective-permute-start | bytes 6291464 | tf_op jit(solution)/shard_map/ppermute | solution.py:306
  1200.5 31.3 %collective-permute-start.218 = (bf16[128,1024]{1,0:T(8,128)(2,1)S(1)}, bf16[128,1024]{1,0:T(8,128)(2,1)S(1)}, u32[]{:S(2)}, u32[]{:S(2)}) collective-permute-start(bf16[128,1024]{1,0:T(8,128)(2,1)S(1)} %fusion.75), channel_id=1, source_target_pairs={{0,16},{2,18},{4,20},{6,22},{8,24},{10,26},{12,28},{14,30},{16,0},... | collective-permute-start | bytes 786440 | tf_op jit(solution)/shard_map/ppermute | solution.py:306
  1201.9 46.5 %collective-permute-start.217 = (bf16[1024,384]{1,0:T(8,128)(2,1)S(1)}, bf16[1024,384]{1,0:T(8,128)(2,1)S(1)}, u32[]{:S(2)}, u32[]{:S(2)}) collective-permute-start(bf16[1024,384]{1,0:T(8,128)(2,1)S(1)} %fusion.52), channel_id=1, source_target_pairs={{0,16},{2,18},{4,20},{6,22},{8,24},{10,26},{12,28},{14,30},{16,0},... | collective-permute-start | bytes 2359304 | tf_op jit(solution)/shard_map/ppermute | solution.py:306
  1302.8 107.3 %all-to-all-start.14 = ((bf16[8,128,1024]{2,1,0:T(8,128)(2,1)}), bf16[8,128,1024]{2,1,0:T(8,128)(2,1)S(1)}, u32[]{:S(2)}, u32[]{:S(2)}) async-start(bf16[8,128,1024]{2,1,0:T(8,128)(2,1)} %bitcast.1355), calls=%async_computation.14 | async-start | bytes 4194304 | tf_op jit(solution)/shard_map/all_to_all | solution.py:408
  1309.2 40.8 %collective-permute-start.176 = (bf16[16,2048]{1,0:T(8,128)(2,1)S(1)}, bf16[16,2048]{1,0:T(8,128)(2,1)S(1)}, u32[]{:S(2)}, u32[]{:S(2)}) collective-permute-start(bf16[16,2048]{1,0:T(8,128)(2,1)S(1)} %get-tuple-element.307), channel_id=1, source_target_pairs={{0,8},{2,10},{4,12},{6,14},{8,0},{10,2},{12,4},{14,6},{16,24},{18,... | collective-permute-start | bytes 196616 | tf_op jit(solution)/shard_map/ppermute | solution.py:306
  1315.4 181.4 %collective-permute-start.216 = (bf16[512,1024]{1,0:T(8,128)(2,1)}, bf16[512,1024]{1,0:T(8,128)(2,1)}, u32[]{:S(2)}, u32[]{:S(2)}) collective-permute-start(bf16[512,1024]{1,0:T(8,128)(2,1)} %fusion.43), channel_id=1, source_target_pairs={{0,16},{2,18},{4,20},{6,22},{8,24},{10,26},{12,28},{14,30},{16,0},... | collective-permute-start | bytes 3145736 | tf_op jit(solution)/shard_map/ppermute | solution.py:306
  1317.6 188.3 %collective-permute-start.215 = (bf16[1024,1024]{1,0:T(8,128)(2,1)}, bf16[1024,1024]{1,0:T(8,128)(2,1)}, u32[]{:S(2)}, u32[]{:S(2)}) collective-permute-start(bf16[1024,1024]{1,0:T(8,128)(2,1)} %fusion.33), channel_id=1, source_target_pairs={{0,16},{2,18},{4,20},{6,22},{8,24},{10,26},{12,28},{14,30},{16,0},... | collective-permute-start | bytes 6291464 | tf_op jit(solution)/shard_map/ppermute | solution.py:306
  1318.3 32.8 %collective-permute-start.170 = (bf16[24,2048]{1,0:T(8,128)(2,1)S(1)}, bf16[24,2048]{1,0:T(8,128)(2,1)S(1)}, u32[]{:S(2)}, u32[]{:S(2)}) collective-permute-start(bf16[24,2048]{1,0:T(8,128)(2,1)S(1)} %slice.1571), channel_id=1, source_target_pairs={{0,1},{1,0},{2,3},{3,2},{4,5},{5,4},{6,7},{7,6},{8,9},{9,8},{10,11... | collective-permute-start | bytes 294920 | tf_op jit(solution)/shard_map/ppermute | solution.py:304
  1352.8 54.0 %collective-permute-start.171 = (bf16[2,24,2048]{2,1,0:T(8,128)(2,1)S(1)}, bf16[2,24,2048]{2,1,0:T(8,128)(2,1)S(1)}, u32[]{:S(2)}, u32[]{:S(2)}) collective-permute-start(bf16[2,24,2048]{2,1,0:T(8,128)(2,1)S(1)} %get-tuple-element.369), channel_id=1, source_target_pairs={{0,4},{2,6},{4,0},{6,2},{8,12},{10,14},{12,8},{14,10},{16,20},{18,... | collective-permute-start | bytes 589832 | tf_op jit(solution)/shard_map/ppermute | solution.py:306
  1357.0 46.3 %collective-permute-start.174 = (bf16[2,24,2048]{2,1,0:T(8,128)(2,1)S(1)}, bf16[2,24,2048]{2,1,0:T(8,128)(2,1)S(1)}, u32[]{:S(2)}, u32[]{:S(2)}) collective-permute-start(bf16[2,24,2048]{2,1,0:T(8,128)(2,1)S(1)} %get-tuple-element.371), channel_id=1, source_target_pairs={{0,8},{2,10},{4,12},{6,14},{8,0},{10,2},{12,4},{14,6},{16,24},{18,... | collective-permute-start | bytes 589832 | tf_op jit(solution)/shard_map/ppermute | solution.py:306
  1407.6 54.9 %collective-permute-start.172 = (bf16[2,2,24,2048]{3,2,0,1:T(8,128)(2,1)}, bf16[2,2,24,2048]{3,2,0,1:T(8,128)(2,1)}, u32[]{:S(2)}, u32[]{:S(2)}) collective-permute-start(bf16[2,2,24,2048]{3,2,0,1:T(8,128)(2,1)} %get-tuple-element.269), channel_id=1, source_target_pairs={{0,8},{2,10},{4,12},{6,14},{8,0},{10,2},{12,4},{14,6},{16,24},{18,... | collective-permute-start | bytes 1179656 | tf_op jit(solution)/shard_map/ppermute | solution.py:306
  1410.1 55.2 %all-to-all-start.13 = ((bf16[8,128,128]{2,1,0:T(8,128)(2,1)}), bf16[8,128,128]{2,1,0:T(8,128)(2,1)}, u32[]{:S(2)}, u32[]{:S(2)}) async-start(bf16[8,128,128]{2,1,0:T(8,128)(2,1)} %bitcast.1279), calls=%async_computation.13 | async-start | bytes 524288 | tf_op jit(solution)/shard_map/all_to_all | solution.py:408
  1464.9 48.8 %collective-permute-start.179 = (bf16[2,2,2,64,2048]{4,3,1,0,2:T(8,128)(2,1)}, bf16[2,2,2,64,2048]{4,3,1,0,2:T(8,128)(2,1)}, u32[]{:S(2)}, u32[]{:S(2)}) collective-permute-start(bf16[2,2,2,64,2048]{4,3,1,0,2:T(8,128)(2,1)} %pad_maximum_fusion.23), channel_id=1, source_target_pairs={{0,2},{2,0},{4,6},{6,4},{8,10},{10,8},{12,14},{14,12},{16,18},{18,... | collective-permute-start | bytes 6291464 | tf_op jit(solution)/shard_map/ppermute | solution.py:306
  1465.3 28.4 %all-to-all-start.12 = ((bf16[8,128,384]{1,2,0:T(8,128)(2,1)}), bf16[8,128,384]{1,2,0:T(8,128)(2,1)}, u32[]{:S(2)}, u32[]{:S(2)}) async-start(bf16[8,128,384]{1,2,0:T(8,128)(2,1)} %copy.676), calls=%async_computation.12 | async-start | bytes 1572864 | tf_op jit(solution)/shard_map/all_to_all | solution.py:408
  1501.4 72.2 %all-to-all-start.11 = ((bf16[8,512,128]{2,1,0:T(8,128)(2,1)}), bf16[8,512,128]{2,1,0:T(8,128)(2,1)S(1)}, u32[]{:S(2)}, u32[]{:S(2)}) async-start(bf16[8,512,128]{2,1,0:T(8,128)(2,1)} %bitcast.1277), calls=%async_computation.11 | async-start | bytes 2097152 | tf_op jit(solution)/shard_map/all_to_all | solution.py:408
  1574.5 82.0 %all-to-all-start.10 = ((bf16[8,128,1024]{2,1,0:T(8,128)(2,1)}), bf16[8,128,1024]{2,1,0:T(8,128)(2,1)S(1)}, u32[]{:S(2)}, u32[]{:S(2)}) async-start(bf16[8,128,1024]{2,1,0:T(8,128)(2,1)} %bitcast.1354), calls=%async_computation.10 | async-start | bytes 4194304 | tf_op jit(solution)/shard_map/all_to_all | solution.py:408
  1582.7 22.9 %collective-permute-start.193 = (f32[2,2,16,160]{3,2,0,1:T(8,128)S(1)}, f32[2,2,16,160]{3,2,0,1:T(8,128)S(1)}, u32[]{:S(2)}, u32[]{:S(2)}) collective-permute-start(f32[2,2,16,160]{3,2,0,1:T(8,128)S(1)} %slice_bitcast_fusion.76), channel_id=1, source_target_pairs={{0,4},{2,6},{4,0},{6,2},{8,12},{10,14},{12,8},{14,10},{16,20},{18,... | collective-permute-start | bytes 122888 | tf_op jit(solution)/shard_map/ppermute | solution.py:306
  1641.8 33.2 %collective-permute-start.214 = (bf16[128,2048]{1,0:T(8,128)(2,1)}, bf16[128,2048]{1,0:T(8,128)(2,1)}, u32[]{:S(2)}, u32[]{:S(2)}) collective-permute-start(bf16[128,2048]{1,0:T(8,128)(2,1)} %convolution_convert_fusion.9), channel_id=1, source_target_pairs={{0,16},{2,18},{4,20},{6,22},{8,24},{10,26},{12,28},{14,30},{16,0},... | collective-permute-start | bytes 1572872 | tf_op jit(solution)/shard_map/ppermute | solution.py:306
  1654.2 33.8 %collective-permute-start.200 = (bf16[2,2,2,64,2048]{4,3,1,0,2:T(8,128)(2,1)}, bf16[2,2,2,64,2048]{4,3,1,0,2:T(8,128)(2,1)}, u32[]{:S(2)}, u32[]{:S(2)}) collective-permute-start(bf16[2,2,2,64,2048]{4,3,1,0,2:T(8,128)(2,1)} %copy.664), channel_id=1, source_target_pairs={{0,2},{2,0},{4,6},{6,4},{8,10},{10,8},{12,14},{14,12},{16,18},{18,... | collective-permute-start | bytes 6291464 | tf_op jit(solution)/shard_map/ppermute | solution.py:306
  1679.8 80.6 %collective-permute-start.213 = (f32[311,128]{1,0:T(8,128)S(1)}, f32[311,128]{1,0:T(8,128)S(1)}, u32[]{:S(2)}, u32[]{:S(2)}) collective-permute-start(f32[311,128]{1,0:T(8,128)S(1)} %slice.1622), channel_id=1, source_target_pairs={{0,16},{2,18},{4,20},{6,22},{8,24},{10,26},{12,28},{14,30},{16,0},... | collective-permute-start | bytes 477704 | tf_op jit(solution)/shard_map/ppermute | solution.py:306
  1686.5 76.8 %collective-permute-start.212 = (bf16[2048,2,128]{2,0,1:T(8,128)(2,1)}, bf16[2048,2,128]{2,0,1:T(8,128)(2,1)}, u32[]{:S(2)}, u32[]{:S(2)}) collective-permute-start(bf16[2048,2,128]{2,0,1:T(8,128)(2,1)} %convolution_convert_fusion.8), channel_id=1, source_target_pairs={{0,16},{2,18},{4,20},{6,22},{8,24},{10,26},{12,28},{14,30},{16,0},... | collective-permute-start | bytes 3145736 | tf_op jit(solution)/shard_map/ppermute | solution.py:306
  1690.5 28.6 %collective-permute-start.201 = (bf16[2,2,24,2048]{3,2,1,0:T(8,128)(2,1)S(1)}, bf16[2,2,24,2048]{3,2,1,0:T(8,128)(2,1)S(1)}, u32[]{:S(2)}, u32[]{:S(2)}) collective-permute-start(bf16[2,2,24,2048]{3,2,1,0:T(8,128)(2,1)S(1)} %slice_bitcast_fusion.23), channel_id=1, source_target_pairs={{0,8},{2,10},{4,12},{6,14},{8,0},{10,2},{12,4},{14,6},{16,24},{18,... | collective-permute-start | bytes 1179656 | tf_op jit(solution)/shard_map/ppermute | solution.py:306
  1692.7 29.9 %collective-permute-start.204 = (bf16[2,2,24,2048]{3,2,1,0:T(8,128)(2,1)S(1)}, bf16[2,2,24,2048]{3,2,1,0:T(8,128)(2,1)S(1)}, u32[]{:S(2)}, u32[]{:S(2)}) collective-permute-start(bf16[2,2,24,2048]{3,2,1,0:T(8,128)(2,1)S(1)} %fusion.131), channel_id=1, source_target_pairs={{0,1},{1,0},{2,3},{3,2},{4,5},{5,4},{6,7},{7,6},{8,9},{9,8},{10,11... | collective-permute-start | bytes 1179656 | tf_op jit(solution)/shard_map/ppermute | solution.py:304
  (370 other events, 4907.8 us)

commit v2 on v1

--- a/solution.py
+++ b/solution.py
@@ -181,7 +181,8 @@
         zero = jnp.zeros((packs, LANE), jnp.float32)
         along = [zero] * parts
         rated = [zero] * parts
-        waiting = []
+        source_sums = []
+        reader_sums = []
         fresh = []
         for n in range(N):
             source = jnp.broadcast_to(mats[:, n : n + 1], (packs, LANE))
@@ -201,12 +202,12 @@
                 along[part] = along[part] + adjoint * source
                 source_sum = source_sum + adjoint * drive_now[part]
                 reader_sum = reader_sum + grad_now[part] * now
-            waiting.append(source_sum)
-            waiting.append(reader_sum)
+            source_sums.append(source_sum)
+            reader_sums.append(reader_sum)
         for part in range(parts):
             total_s[pl.ds(part * rows + t, packs, stride=span), :] = rated[part] * LN2 + mix_now[part] * along[part]
             along_s[pl.ds(part * rows + t, packs, stride=span), :] = along[part]
-        big = jnp.dot(jnp.concatenate(waiting, axis=0).astype(jnp.bfloat16), jnp.ones((LANE, LANE), jnp.bfloat16), preferred_element_type=jnp.float32)
+        big = jnp.dot(jnp.concatenate(source_sums + reader_sums, axis=0).astype(jnp.bfloat16), jnp.ones((LANE, LANE), jnp.bfloat16), preferred_element_type=jnp.float32)
         mats_grad = zero
         for q in range(2 * N):
             mats_grad = jnp.where(lane == q, big[q * packs : (q + 1) * packs], mats_grad)
@@ -302,8 +303,9 @@
 def hop(values, link):
     if link == "x":
         return lax.ppermute(values, "tensor", [(0, 1), (1, 0)])
-    bit = {"core": 1, "y": 2, "z": 4, "outer": GROUP}[link]
-    return lax.ppermute(values, "dp", [(k, k ^ bit) for k in range(lax.axis_size("dp"))])
+    dp_count = lax.axis_size("dp")
+    bit = {"core": 1, "y": 2, "outer": 4, "z": dp_count // 2}[link]
+    return lax.ppermute(values, "dp", [(k, k ^ bit) for k in range(dp_count)])
 
 
 def ordered(mine, theirs, index):
@@ -311,165 +313,232 @@
     return jnp.where(first, mine, theirs), jnp.where(first, theirs, mine)
 
 
-def cuts(rows):
-    third = rows * 3 // 8
-    return ((0, third), (third, 2 * third), (2 * third, rows))
-
-
 def gather_rows(own):
     tensor_at = lax.axis_index("tensor")
-
-    def grow(values, axis, link):
-        got = hop(values, link)
-        if link == "x":
-            return jnp.stack(ordered(values, got, tensor_at), axis=axis)
-        return jnp.stack([values, got], axis=axis)
-
-    first, second, third = [own[start:stop] for start, stop in cuts(own.shape[0])]
-    first = grow(grow(grow(first, 0, "x"), 0, "y"), 0, "z")
-    second = grow(grow(grow(second, 0, "y"), 0, "z"), 2, "x")
-    third = grow(grow(grow(third, 0, "z"), 1, "x"), 1, "y")
-    local = jnp.concatenate([first, second, third], axis=3)
-    both = jnp.stack([local, hop(local, "core")], axis=0)
-    return both.reshape((2 * GROUP * own.shape[0], own.shape[1]))
+    by_z = hop(own, "z")
+    by_x = hop(own, "x")
+    by_y = hop(own, "y")
+    by_xz = hop(by_z, "x")
+    by_yz = hop(by_z, "y")
+    by_xy = hop(by_y, "x")
+    by_xyz = hop(by_xz, "y")
+    pairs = [(own, by_x), (by_y, by_xy), (by_z, by_xz), (by_yz, by_xyz)]
+    local = jnp.concatenate(
+        [piece for near, far in pairs for piece in ordered(near, far, tensor_at)], axis=0
+    )
+    return jnp.concatenate([local, hop(local, "core")], axis=0)
 
 
 def reduce_rows(partial):
     kind = partial.dtype
     tensor_at = lax.axis_index("tensor")
-    width = partial.shape[1]
-    rows = partial.shape[0] // (2 * GROUP)
-    cube = partial.reshape((2, 2, 2, 2, rows, width))
-
-    def fold(values, axis, link):
-        low_half = lax.index_in_dim(values, 0, axis, keepdims=False)
-        high_half = lax.index_in_dim(values, 1, axis, keepdims=False)
-        if link == "x":
-            low_half, high_half = ordered(low_half, high_half, tensor_at)
-        return low_half.astype(full) + hop(high_half.astype(kind), link).astype(full)
-
-    cube = fold(cube, 0, "core")
-    first, second, third = [cube[:, :, :, start:stop] for start, stop in cuts(rows)]
-    first = fold(fold(fold(first, 0, "z"), 0, "y"), 0, "x")
-    second = fold(fold(fold(second, 2, "x"), 0, "z"), 0, "y")
-    third = fold(fold(fold(third, 1, "y"), 1, "x"), 0, "z")
-    return jnp.concatenate([first, second, third], axis=0)
+    half = partial.shape[0] // 2
+    rows = half // GROUP
+    mine = partial[:half]
+    mate = hop(partial[half:], "core")
+
+    def block(z, y, x):
+        pieces = []
+        for side in range(2):
+            at = (4 * z + 2 * y + side) * rows
+            pieces.append(mine[at : at + rows].astype(full) + mate[at : at + rows].astype(full))
+        return ordered(pieces[0], pieces[1], tensor_at)[x]
+
+    def send(values, link):
+        return hop(values.astype(kind), link).astype(full)
+
+    from_xyz = send(block(1, 1, 1), "y")
+    from_xy = send(block(0, 1, 1), "x")
+    from_yz = send(block(1, 1, 0), "y")
+    from_xz = send(block(1, 0, 1) + from_xyz, "x")
+    from_x = send(block(0, 0, 1), "x")
+    from_y = send(block(0, 1, 0) + from_xy, "y")
+    from_z = send(block(1, 0, 0) + from_yz + from_xz, "z")
+    return block(0, 0, 0) + from_x + from_y + from_z
+
+
+def total_rows(partial):
+    half = partial.shape[0] // 2
+    rows = half // GROUP
+    mine = partial[:half] + hop(partial[half:], "core")
+    cube = mine.reshape((2, 2, 2, rows, partial.shape[1]))
+    third = rows * 3 // 8
+    parts = []
+    for start, stop, order in ((0, third, "xyz"), (third, 2 * third, "yzx"), (2 * third, rows, "zxy")):
+        part = cube[:, :, :, start:stop]
+        for link in order:
+            sent = part if link == "x" else jnp.flip(part, 0 if link == "z" else 1)
+            part = part + hop(sent, link)
+        parts.append(part)
+    mine = jnp.concatenate(parts, axis=3).reshape((half, partial.shape[1]))
+    return jnp.concatenate([mine, hop(mine, "core")], axis=0)
 
 
 def outer_count():
     return lax.axis_size("dp") // GROUP
 
 
+def outer_at():
+    return lax.axis_index("dp") % (lax.axis_size("dp") // 2) // 4
+
+
+def inner_groups():
+    half = lax.axis_size("dp") // 2
+    return [
+        [half * side + 4 * outer + k for side in range(2) for k in range(4)] for outer in range(outer_count())
+    ]
+
+
 def outer_groups():
-    return [[k + GROUP * other for other in range(outer_count())] for k in range(GROUP)]
+    return [list(members) for members in zip(*inner_groups())]
+
+
+def regrouped(values, axis, back=False):
+    shape = values.shape
+    split = (outer_count(), 2) if back else (2, outer_count())
+    values = values.reshape(shape[:axis] + split + (-1,) + shape[axis + 1 :])
+    return jnp.swapaxes(values, axis, axis + 1).reshape(shape)
 
 
 def outer_gather(values, axis):
-    if outer_count() == 2:
-        pieces = ordered(values, hop(values, "outer"), lax.axis_index("dp") // GROUP)
-        return jnp.concatenate(pieces, axis=axis)
     return lax.all_gather(values, "dp", axis_index_groups=outer_groups(), axis=axis, tiled=True)
 
 
-def channel_gather(values):
-    if outer_count() == 2:
-        return jnp.concatenate([values, hop(values, "outer")], axis=-1)
-    return lax.all_gather(
-        values, "dp", axis_index_groups=outer_groups(), axis=values.ndim - 1, tiled=True
-    )
-
-
-def channel_scatter(make, width, kind):
-    if outer_count() == 2:
-        half = width // 2
-        got = hop(make(half, width).astype(kind), "outer")
-        return make(0, half) + got.astype(full)
-    values = make(0, width).astype(kind)
+def outer_scatter(values, axis):
     return lax.psum_scatter(
-        values, "dp", axis_index_groups=outer_groups(), scatter_dimension=values.ndim - 1, tiled=True
-    ).astype(full)
-
-
-def outer_sum(make):
-    if outer_count() == 2:
-        here = lax.axis_index("dp") // GROUP
-        got = hop(make(1 - here).astype(low), "outer")
-        return make(here) + got.astype(full)
-    blocks = jnp.stack([make(k).astype(low) for k in range(outer_count())], axis=0)
-    return lax.psum_scatter(
-        blocks, "dp", axis_index_groups=outer_groups(), scatter_dimension=0, tiled=True
-    )[0].astype(full)
+        values, "dp", axis_index_groups=outer_groups(), scatter_dimension=axis, tiled=True
+    )
 
 
 def inner_swap(values):
-    groups = [
-        [GROUP * outer + k for k in range(GROUP)] for outer in range(outer_count())
-    ]
     return lax.all_to_all(
-        values, "dp", split_axis=0, concat_axis=0, axis_index_groups=groups, tiled=True
-    )
-
-
-def lanes_of(values, block, count):
-    size = values.shape[1] // count
-    return lax.dynamic_slice_in_dim(values, block * size, size, axis=1)
-
-
-def take_in(weight):
-    depth, pairs, width = weight.shape
-    cut = weight.reshape((depth, pairs, GROUP, width // GROUP)).transpose((2, 0, 1, 3))
-    swapped = inner_swap(cut.reshape((GROUP, depth, pairs * width // GROUP)))
-    return outer_gather(swapped.reshape((GROUP * depth, -1)), 0)
-
-
-def give_in(make, depth, pairs, width):
-    total = outer_sum(make).astype(low).reshape((GROUP, depth, -1))
-    swapped = inner_swap(total).reshape((GROUP, depth, pairs, width // GROUP))
-    return swapped.transpose((1, 2, 0, 3)).reshape((depth, pairs, width)).astype(full)
-
-
-def take_out(weight):
-    height, depth = weight.shape
-    swapped = inner_swap(weight.reshape((GROUP, height // GROUP, depth)))
-    return outer_gather(swapped.transpose((1, 0, 2)).reshape((height // GROUP, GROUP * depth)), 1)
-
-
-def give_out(make, height, depth):
-    total = outer_sum(make).astype(low).reshape((height // GROUP, GROUP, depth))
-    return inner_swap(total.transpose((1, 0, 2))).reshape((height, depth)).astype(full)
-
-
-def feed_forward(stream, gain, gate_up, down):
-    hidden_width = down.shape[0]
-    scale, normed = normed_rows(stream, gain)
+        values, "dp", split_axis=0, concat_axis=0, axis_index_groups=inner_groups(), tiled=True
+    )
+
+
+def pack_kernel(in_ref, out_ref, packed_ref):
+    pairs, width = in_ref.shape[1:]
+    for k in range(pairs):
+        packed_ref[0, :, k * width : (k + 1) * width] = in_ref[:, k, :]
+    packed_ref[0, :, pairs * width :] = out_ref[...].T
+
+
+def pack_weights(inward, outward):
+    depth, pairs, width = inward.shape
+    width = width // GROUP
+    height = outward.shape[0] // GROUP
+    total = pairs * width + height
+    return pl.pallas_call(
+        pack_kernel,
+        grid=(GROUP,),
+        in_specs=[
+            pl.BlockSpec((depth, pairs, width), lambda k: (0, 0, k)),
+            pl.BlockSpec((height, depth), lambda k: (k, 0)),
+        ],
+        out_specs=pl.BlockSpec((1, depth, total), lambda k: (k, 0, 0)),
+        out_shape=jax.ShapeDtypeStruct((GROUP, depth, total), low),
+        compiler_params=pltpu.CompilerParams(vmem_limit_bytes=40 << 20),
+        cost_estimate=pl.CostEstimate(
+            flops=0, bytes_accessed=4 * GROUP * depth * total, transcendentals=0
+        ),
+    )(inward, outward)
+
+
+def unpack_kernel(packed_ref, in_ref, out_ref):
+    values = packed_ref[0].astype(full)
+    pairs, width = in_ref.shape[1:]
+    for k in range(pairs):
+        in_ref[:, k, :] = values[:, k * width : (k + 1) * width]
+    out_ref[...] = values[:, pairs * width :].T
+
+
+def unpack_grads(packed, pairs, height):
+    depth, total = packed.shape[1:]
+    width = (total - height) // pairs
+    return pl.pallas_call(
+        unpack_kernel,
+        grid=(GROUP,),
+        in_specs=[pl.BlockSpec((1, depth, total), lambda k: (k, 0, 0))],
+        out_specs=[
+            pl.BlockSpec((depth, pairs, width), lambda k: (0, 0, k)),
+            pl.BlockSpec((height, depth), lambda k: (k, 0)),
+        ],
+        out_shape=[
+            jax.ShapeDtypeStruct((depth, pairs, GROUP * width), full),
+            jax.ShapeDtypeStruct((GROUP * height, depth), full),
+        ],
+        compiler_params=pltpu.CompilerParams(vmem_limit_bytes=40 << 20),
+        cost_estimate=pl.CostEstimate(
+            flops=0, bytes_accessed=6 * GROUP * depth * total, transcendentals=0
+        ),
+    )(packed)
+
+
+def widen_kernel(in_ref, out_ref):
+    values = in_ref[...].astype(full)
+    pairs, width = out_ref.shape[1:]
+    for k in range(pairs):
+        out_ref[:, k, :] = values[:, k * width : (k + 1) * width]
+
+
+def widen(values, pairs):
+    depth, wide = values.shape
+    width = wide // pairs
+    rows = depth // 8
+    return pl.pallas_call(
+        widen_kernel,
+        grid=(8,),
+        in_specs=[pl.BlockSpec((rows, wide), lambda k: (k, 0))],
+        out_specs=pl.BlockSpec((rows, pairs, width), lambda k: (k, 0, 0)),
+        out_shape=jax.ShapeDtypeStruct((depth, pairs, width), full),
+        compiler_params=pltpu.CompilerParams(vmem_limit_bytes=40 << 20),
+        cost_estimate=pl.CostEstimate(flops=0, bytes_accessed=6 * depth * wide, transcendentals=0),
+    )(values)
+
+
+def tie(values, event):
+    zero = jnp.minimum(jnp.abs(event[(slice(0, 1),) * event.ndim].astype(full)), 0.0).reshape(())
+    return values + zero.astype(values.dtype)
+
+
+def queued_gather(swapped, pieces, event):
+    values = swapped.reshape((-1, swapped.shape[2]))
+    width = values.shape[1] // pieces
+    got = []
+    for k in range(pieces):
+        event = outer_gather(tie(values[:, k * width : (k + 1) * width], event), 0)
+        got.append(event)
+    return got
+
+
+def outer_total(total):
+    mine = outer_scatter(total.astype(low), 0)
+    return mine.reshape((GROUP, -1, mine.shape[1]))
+
+
+def feed_forward(stream, normed, scale, weights):
+    hidden_width = weights.shape[1] // 3
     every = gather_rows(normed)
-    pair = matmul(every, gate_up)
+    pair = matmul(every, weights[:, : 2 * hidden_width])
     gate = pair[:, :hidden_width]
     up = pair[:, hidden_width:]
     hidden = (jax.nn.silu(gate) * up).astype(low)
-    branch = reduce_rows(matmul(hidden, down).astype(low))
+    branch = reduce_rows(matmul_lanes(hidden, weights[:, 2 * hidden_width :]).astype(low))
     return stream + branch, (scale, every, gate, up, hidden)
 
 
-def feed_backward(grad, every_grad, stream, kept, gain, gate_up, down):
+def feed_backward(grad, every_grad, stream, kept, gain, weights):
     scale, every, gate, up, hidden = kept
-    count = outer_count()
-    hidden_grad = matmul_lanes(every_grad, down)
+    hidden_width = hidden.shape[1]
+    hidden_grad = matmul(every_grad, weights[:, 2 * hidden_width :])
     pair_grad = jnp.concatenate(
         [hidden_grad * up * silu_slope(gate), hidden_grad * jax.nn.silu(gate)], axis=1
     ).astype(low)
-    normed_grad = reduce_rows(matmul_lanes(pair_grad, gate_up).astype(low))
+    normed_grad = reduce_rows(matmul_lanes(pair_grad, weights[:, : 2 * hidden_width]).astype(low))
     norm_part, gain_grad = norm_backward(stream, scale, gain, normed_grad)
-    depth = gate_up.shape[0] // (count * GROUP)
-    in_grad = give_in(
-        lambda block: matmul_rows(lanes_of(every, block, count), pair_grad),
-        depth, 2, gate_up.shape[1] * GROUP // 2,
-    )
-    out_grad = give_out(
-        lambda block: matmul_rows(hidden, lanes_of(every_grad, block, count)),
-        down.shape[0] * GROUP, depth,
-    )
-    return grad + norm_part, (gain_grad, in_grad, out_grad)
+    out_grad = outer_total(matmul_rows(every_grad, hidden))
+    in_grad = outer_total(matmul_rows(every, pair_grad))
+    return grad + norm_part, gain_grad, jnp.concatenate([in_grad, out_grad], axis=2)
 
 
 def shifted(values, places):
@@ -523,14 +592,19 @@
         "dp", split_axis=0, concat_axis=0, tiled=True,
     )
     stream = matmul(own_sel, inbound[:, :, :model_width].reshape((row_count, model_width)))
+    stream = regrouped(stream, 1)
     sides = inbound[:, :, model_width:].reshape((dp_count, slot * side_width))
     gains = [
-        sides[:, k * part : (k + 1) * part].reshape((model_width,)).astype(full) for k in range(4)
+        regrouped(sides[:, k * part : (k + 1) * part].reshape((model_width,)), 0).astype(full)
+        for k in range(4)
     ]
     gain_mamba, gain_first, gain_attn, gain_second = gains
     all_lengths = sides[:, 4 * part : 4 * part + seqs].astype(full)
 
-    pack_at = dp_at ^ jnp.array([0, 2, 4, 6, 1, 3, 5, 7], jnp.int32)
+    side_bit = dp_count // 2
+    pack_at = dp_at ^ jnp.array(
+        [core + 2 * y + side_bit * z for core in range(2) for z in range(2) for y in range(2)], jnp.int32
+    )
     pack_sel = (pack_at[:, None] == jnp.arange(dp_count, dtype=jnp.int32)[None, :]).astype(full)
     pack_lengths = jnp.sum(pack_sel[:, :, None] * all_lengths[None], axis=1).astype(jnp.int32)
     seq_ends = jnp.cumsum(pack_lengths, axis=1)
@@ -545,14 +619,17 @@
     taps = [(offset >= tap).astype(full)[:, :, None] for tap in range(K)]
     keep_mask = taps[1].reshape((every_count, 1))
 
-    small = channel_gather(
-        jnp.concatenate(
-            [w_x.T, w_dt, conv_w, conv_bias[None], dt_bias[None], a_log, skip[None]], axis=0
-        )
-    )
-    in_pair = channel_gather(w_in)
-    channels = in_pair.shape[2]
-    in_flat = in_pair.reshape((model_width, 2 * channels))
+    block = w_in.shape[2]
+    channels = count * block
+    in_blocks = outer_gather(w_in[None], 0)
+    in_flat = regrouped(in_blocks.transpose((1, 0, 2, 3)), 0).reshape((model_width, 2 * channels))
+    small = jnp.concatenate(
+        [w_x.T, w_dt, conv_w, conv_bias[None], dt_bias[None], a_log, skip[None]], axis=0
+    )
+    if count == 2:
+        small = jnp.concatenate(ordered(small, hop(small, "outer"), outer_at()), axis=1)
+    else:
+        small = outer_gather(small, 1)
     select_rows = R + 2 * N
     select_proj = small[:select_rows]
     step_proj = small[select_rows : select_rows + R]
@@ -562,35 +639,40 @@
     step_bias = rest[K + 1 : K + 2]
     decay_rate = -jnp.exp(rest[K + 2 : K + 2 + N])
     skip_gain = rest[K + 2 + N : K + 3 + N]
-    if count == 2:
-        out_proj = jnp.concatenate([w_out, hop(w_out, "outer")], axis=0)
-    else:
-        out_proj = lax.all_gather(w_out, "dp", axis_index_groups=outer_groups(), axis=0, tiled=True)
-
+
+    first_swapped = inner_swap(pack_weights(mlp_one_in, mlp_one_out))
+    first_pieces = queued_gather(first_swapped, 3, in_blocks)
+    first_weights = jnp.concatenate(first_pieces, axis=1)
+    out_proj = regrouped(outer_gather(tie(w_out, first_pieces[1]), 0), 1)
     scale_mamba, normed_one = normed_rows(stream, gain_mamba)
     every_one = gather_rows(normed_one)
-    inner = matmul(every_one, in_flat)
-    conv_input = inner[:, :channels].reshape((packs, row_count, channels))
-    gate_input = inner[:, channels:]
+    inner = matmul(every_one, in_flat).reshape((every_count, count, 2, block))
+    conv_input = inner[:, :, 0].reshape((packs, row_count, channels))
+    gate_input = inner[:, :, 1].reshape((every_count, channels))
     conv_sum = conv_shift + conv_taps[0] * conv_input
     for tap in range(1, K):
         conv_sum = conv_sum + conv_taps[tap] * shifted(conv_input, tap) * taps[tap]
     mixer_low = jax.nn.silu(conv_sum).astype(low).reshape((every_count, channels))
     mixer_val = mixer_low.astype(full)
-    selected = gather_rows(reduce_rows(matmul_lanes(mixer_low, select_proj)))
+    selected = total_rows(tie(matmul_lanes(mixer_low, select_proj), first_swapped))
+    attn_swapped = inner_swap(tie(pack_weights(w_qkv, w_o), selected))
+    attn_pieces = queued_gather(attn_swapped, 1, first_pieces[-1])
+    attn_weights = jnp.concatenate(attn_pieces, axis=1)
     step_low = selected[:, :R].astype(low)
     mats = jnp.pad(selected[:, R:], ((0, 0), (0, LANE - 2 * N)))
     scan_args = (step_low, mats, keep_mask, step_proj, step_bias, decay_rate, skip_gain)
     gated_low, mixer_out, prior = scan_forward(mixer_val, gate_input, *scan_args, packs)
-    stream_mid = stream + reduce_rows(matmul(gated_low, out_proj).astype(low))
-
-    first_in = take_in(mlp_one_in)
-    first_out = take_out(mlp_one_out)
-    stream_ffn, kept_first = feed_forward(stream_mid, gain_first, first_in, first_out)
-
-    proj_flat = take_in(w_qkv)
-    attn_out = take_out(w_o)
-    inner_width = attn_out.shape[0]
+    stream_mid = stream + reduce_rows(tie(matmul(gated_low, out_proj).astype(low), attn_swapped))
+
+    second_swapped = inner_swap(tie(pack_weights(mlp_two_in, mlp_two_out), stream_mid))
+    second_pieces = queued_gather(second_swapped, 3, attn_pieces[-1])
+    second_weights = jnp.concatenate(second_pieces, axis=1)
+    scale_first, normed_first = normed_rows(stream_mid, gain_first)
+    stream_ffn, kept_first = feed_forward(stream_mid, normed_first, scale_first, first_weights)
+
+    inner_width = w_o.shape[0] // GROUP
+    proj_flat = attn_weights[:, : 3 * inner_width]
+    attn_out = attn_weights[:, 3 * inner_width :]
     head_count = inner_width // HD
     scale_attn, normed_two = normed_rows(stream_ffn, gain_attn)
     every_two = gather_rows(normed_two)
@@ -614,28 +696,23 @@
         .astype(low)
         .reshape((every_count, inner_width))
     )
-    stream_attn = stream_ffn + reduce_rows(matmul(context_low, attn_out).astype(low))
-
-    second_in = take_in(mlp_two_in)
-    second_out = take_out(mlp_two_out)
-    result, kept_second = feed_forward(stream_attn, gain_second, second_in, second_out)
+    stream_attn = stream_ffn + reduce_rows(matmul_lanes(context_low, attn_out).astype(low))
+
+    scale_second, normed_second = normed_rows(stream_attn, gain_second)
+    result, kept_second = feed_forward(stream_attn, normed_second, scale_second, second_weights)
 
     cot_in = lax.all_to_all(
         matmul(send_sel, cotangent).astype(low), "dp", split_axis=0, concat_axis=0, tiled=True
     )
-    back_grad = matmul(own_sel, cot_in)
-    grad_attn_stream, second_sums = feed_backward(
-        back_grad, gather_rows(back_grad.astype(low)), stream_attn, kept_second, gain_second, second_in, second_out
+    back_grad = regrouped(matmul(own_sel, cot_in), 1)
+    every_back = gather_rows(back_grad.astype(low))
+    grad_attn_stream, grad_gain_second, second_total = feed_backward(
+        back_grad, every_back, stream_attn, kept_second, gain_second, second_weights
     )
 
     every_branch = gather_rows(grad_attn_stream.astype(low))
-    attn_depth = part
-    grad_w_o = give_out(
-        lambda block: matmul_rows(context_low, lanes_of(every_branch, block, count)),
-        inner_width * GROUP, attn_depth,
-    )
     grad_context = (
-        matmul_lanes(every_branch, attn_out)
+        matmul(every_branch, attn_out)
         .astype(low)
         .reshape((packs, row_count, head_count, HD))
     )
@@ -652,43 +729,34 @@
         [rotated(grad_query, cosine, -sine_part), rotated(grad_key, cosine, -sine_part), grad_values], axis=2
     )
     grad_proj_low = grad_proj.astype(low).reshape((every_count, 3 * inner_width))
-    grad_w_qkv = give_in(
-        lambda block: matmul_rows(lanes_of(every_two, block, count), grad_proj_low),
-        attn_depth, 3, inner_width * GROUP,
+    attn_total = outer_total(
+        jnp.concatenate([matmul_rows(every_two, grad_proj_low), matmul_rows(every_branch, context_low)], axis=1)
     )
     grad_normed_two = reduce_rows(matmul_lanes(grad_proj_low, proj_flat).astype(low))
     norm_ffn, grad_gain_two = norm_backward(stream_ffn, scale_attn, gain_attn, grad_normed_two)
     grad_ffn_stream = grad_attn_stream + norm_ffn
 
-    grad_mid, first_sums = feed_backward(
-        grad_ffn_stream, gather_rows(grad_ffn_stream.astype(low)), stream_mid, kept_first, gain_first,
-        first_in, first_out,
+    grad_mid, grad_gain_first, first_total = feed_backward(
+        grad_ffn_stream, gather_rows(grad_ffn_stream.astype(low)), stream_mid, kept_first, gain_first, first_weights
     )
 
     every_mixed = gather_rows(grad_mid.astype(low))
     grad_gated = matmul_lanes(every_mixed, out_proj)
-    if count == 2:
-        half = channels // 2
-        got = hop(matmul_rows(gated_low[:, half:], every_mixed).astype(low), "outer")
-        grad_w_out = matmul_rows(gated_low[:, :half], every_mixed) + got.astype(full)
-    else:
-        grad_w_out = lax.psum_scatter(
-            matmul_rows(gated_low, every_mixed).astype(low), "dp", axis_index_groups=outer_groups(),
-            scatter_dimension=0, tiled=True,
-        ).astype(full)
+    grad_w_out = outer_scatter(matmul_rows(gated_low, every_mixed).astype(low), 0)
+    grad_w_out = regrouped(grad_w_out, 1, True).astype(full)
     grad_step_low, grad_mixer, grad_gate, mats_grad, grad_a_log, grad_skip = scan_backward(
         mixer_val, gate_input, mixer_out, grad_gated, *scan_args, prior, packs
     )
+    second_grads = inner_swap(tie(second_total, grad_gated))
     grad_dt_bias = jnp.sum(grad_step_low.astype(full), axis=0, keepdims=True)
     grad_w_dt = matmul_rows(step_low, grad_step_low)
-    grad_selected = gather_rows(
-        reduce_rows(
-            jnp.concatenate(
-                [matmul_lanes(grad_step_low, step_proj), mats_grad[:, 0 : 2 * N : 2], mats_grad[:, 1 : 2 * N : 2]],
-                axis=1,
-            )
-        ).astype(low)
-    )
+    grad_selected = total_rows(
+        tie(
+            jnp.concatenate([matmul_lanes(grad_step_low, step_proj), mats_grad[:, : 2 * N]], axis=1),
+            second_grads,
+        )
+    ).astype(low)
+    attn_grads = inner_swap(tie(attn_total, grad_selected))
     grad_w_x = matmul_rows(grad_selected, mixer_low)
     grad_mixer = grad_mixer + matmul(grad_selected, select_proj)
     grad_conv = grad_mixer.reshape((packs, row_count, channels)) * silu_slope(conv_sum)
@@ -700,18 +768,34 @@
         tap_grads.append(jnp.sum(masked_grad * shifted(conv_input, tap), axis=(0, 1)))
         grad_conv_input = grad_conv_input + conv_taps[tap] * shifted(masked_grad, -tap)
     grad_conv_low = grad_conv_input.astype(low).reshape((every_count, channels))
-    grad_inner = jnp.concatenate([grad_conv_low, grad_gate], axis=1)
-    grad_normed_one = reduce_rows(matmul_lanes(grad_inner, in_flat).astype(low))
-
-    def in_grads(start, stop):
-        columns = jnp.concatenate([grad_conv_low[:, start:stop], grad_gate[:, start:stop]], axis=1)
-        return matmul_rows(every_one, columns).reshape((model_width, 2, stop - start))
-
-    grad_w_in = channel_scatter(in_grads, channels, low)
+    grad_inner = jnp.stack(
+        [grad_conv_low.reshape((every_count, count, block)), grad_gate.reshape((every_count, count, block))], axis=2
+    ).reshape((every_count, 2 * channels))
+    grad_normed_one = reduce_rows(
+        tie(matmul_lanes(grad_inner, in_flat).astype(low), attn_grads)
+    )
+
+    in_total = jnp.concatenate(
+        [
+            matmul_rows(every_one, grad_inner[:, 2 * block * k : 2 * block * (k + 1)]).astype(low)
+            for k in range(count)
+        ],
+        axis=0,
+    )
+    grad_w_in = widen(regrouped(outer_scatter(in_total, 0), 0, True), 2)
     small_grads = jnp.concatenate(
         [grad_w_x, grad_w_dt, jnp.stack(tap_grads), grad_conv_bias, grad_dt_bias, grad_a_log, grad_skip], axis=0
     )
-    small_sums = channel_scatter(lambda start, stop: small_grads[:, start:stop], channels, full)
+    if count == 2:
+        here = outer_at()
+        theirs = lax.dynamic_slice_in_dim(small_grads, (1 - here) * block, block, axis=1)
+        small_sums = lax.dynamic_slice_in_dim(small_grads, here * block, block, axis=1) + hop(theirs, "outer")
+    else:
+        small_sums = outer_scatter(small_grads, 1)
+    first_grads = inner_swap(first_total)
+    grad_one_in, grad_one_out = unpack_grads(first_grads, 2, mlp_one_out.shape[0] // GROUP)
+    grad_two_in, grad_two_out = unpack_grads(second_grads, 2, mlp_two_out.shape[0] // GROUP)
+    grad_w_qkv, grad_w_o = unpack_grads(attn_grads, 3, inner_width)
     norm_in, grad_gain_one = norm_backward(stream, scale_mamba, gain_mamba, grad_normed_one)
     input_grad = grad_mid + norm_in
 
@@ -721,13 +805,13 @@
         return matmul_rows(arrive_sel, packed).astype(low).reshape((dp_count, slot, model_width))
 
     def landed(home):
-        return matmul_rows(send_sel, home.reshape((row_count, model_width)))
+        return regrouped(matmul_rows(send_sel, home.reshape((row_count, model_width))), 1, True)
 
     final_out = landed(
         lax.all_to_all(homeward(result.astype(low)), "dp", split_axis=0, concat_axis=0, tiled=True)
     )
-    gain_grads = jnp.stack([grad_gain_one, first_sums[0], grad_gain_two, second_sums[0]])
-    gain_grads = gain_grads + hop(gain_grads, "x")
+    gain_grads = jnp.stack([grad_gain_one, grad_gain_first, grad_gain_two, grad_gain_second])
+    gain_grads = regrouped(gain_grads + hop(gain_grads, "x"), 1, True)
     gain_high = gain_grads.astype(low)
     gain_parts = jnp.stack([gain_high, (gain_grads - gain_high.astype(full)).astype(low)])
     gain_parts = gain_parts.reshape((8, dp_count, part)).transpose((1, 0, 2)).reshape((dp_count, 8 * part))
@@ -749,8 +833,8 @@
     pieces = [small_sums[cut_at[k] : cut_at[k + 1]] for k in range(len(sizes))]
     return (
         final_out, final_grad, gain_sums[0], grad_w_in, pieces[2], pieces[3][0], pieces[0].T, pieces[1],
-        pieces[4][0], pieces[5], pieces[6][0], grad_w_out, gain_sums[1], first_sums[1], first_sums[2],
-        gain_sums[2], grad_w_qkv, grad_w_o, gain_sums[3], second_sums[1], second_sums[2],
+        pieces[4][0], pieces[5], pieces[6][0], grad_w_out, gain_sums[1], grad_one_in, grad_one_out,
+        gain_sums[2], grad_w_qkv, grad_w_o, gain_sums[3], grad_two_in, grad_two_out,
     )
 
 

time: 1790 us -> 1350 us (0.75)
  waiting for transfers between devices: 973 us -> 519 us
  starting transfers between devices: 333 us -> 233 us
  other arithmetic: 112 us -> 159 us
  Pallas kernels: 63.8 us -> 98.7 us
  local copies, waits for them, and re-layouts: 150 us -> 177 us
  between operations: 6.45 us -> 27.1 us
  blocking collectives: 19.9 us -> 0 us
    ppermute x158 -> x98, waiting for transfers between devices: 863 us -> 240 us  [hop(): return lax.ppermute(values, 'dp', [(k, k ^ bit) for k in range(dp_count)])]
    ppermute x158 -> x98, starting transfers between devices: 202 us -> 118 us  [hop(): return lax.ppermute(values, 'dp', [(k, k ^ bit) for k in range(dp_count)])]
    all_gather x0 -> x9, waiting for transfers between devices: none -> 76.2 us  [outer_gather(): lax.all_gather(values, 'dp', axis_index_groups=outer_groups(), axis=axis,...]
    ppermute x63 -> x57, waiting for transfers between devices: 87 us -> 154 us  [hop(): return lax.ppermute(values, 'tensor', [(0, 1), (1, 0)])]
    unnamed x1 -> x57, other arithmetic: 0.01 us -> 47.7 us
    pallas_call x0 -> x7, Pallas kernels: none -> 35 us  [the longest x3 17.1 us: unpack_grads(): pl.pallas_call(unpack_kernel, grid=(GROUP,), in_specs=[pl.BlockSpec((1, d...]
    another operation x112 -> x4, other arithmetic: 35.5 us -> 3.64 us  [the longest x1 2.27 us: shards(): jnp.stack([grad_conv_low.reshape((every_count, count, block)), grad_gate....]
    convert_element_type x55 -> x15, local copies, waits for them, and re-layouts: 38.7 us -> 9.19 us  [the longest x3 8.87 us: shards(): grad_w_out = regrouped(grad_w_out, 1, True).astype(full)]
  transfers between devices with their start and end apart: 236 -> 181, of which waited for: 133 -> 98; matrix products, arithmetic and copies ran while one was open for 17% -> 27% of each run, Pallas kernels for 2% -> 7%
where the time goes in v2:
time: 1350 us; the launch traced here: 1340 us
  waiting for transfers between devices  519 us (38%)
  starting transfers between devices  233 us (17%)
  local copies, waits for them, and re-layouts  177 us (13%)
  other arithmetic  159 us (12%)
  matrix products  130 us (10%)
  Pallas kernels  98.7 us (7%)
  between operations  27.1 us (2%)
    ppermute x98, waiting for transfers between devices, hop(): return lax.ppermute(values, 'dp', [(k, k ^ bit) for k in range(dp_count)])  240 us
    ppermute x57, waiting for transfers between devices, hop(): return lax.ppermute(values, 'tensor', [(0, 1), (1, 0)])  154 us
    ppermute x98, starting transfers between devices, hop(): return lax.ppermute(values, 'dp', [(k, k ^ bit) for k in range(dp_count)])  118 us
    all_gather x9, waiting for transfers between devices, outer_gather(): lax.all_gather(values, 'dp', axis_index_groups=outer_groups(), axis=axis,...  76.2 us
    ppermute x57, starting transfers between devices, hop(): return lax.ppermute(values, 'tensor', [(0, 1), (1, 0)])  65.3 us
    unnamed x323, local copies, waits for them, and re-layouts  56.6 us
    unnamed x57, other arithmetic  47.7 us
    dot_general x15, matrix products, matmul_rows(): lax.dot_general(left, right, (((0,), (0,)), ((), ())), preferred_element_...  47.4 us
  transfers between devices with their start and end apart: 181, of which 98 were waited for; matrix products, arithmetic and copies ran while one was open for 27% of the time, Pallas kernels for 7%

profile of v2, /device:TPU:0, one launch (start us, length us, event | category | flops | bytes accessed | tf_op | source)
XLA Modules:
  0.0 1344.4 jit_solution(5049502746321258682)
XLA Ops:
  13.3 7.4 all-to-all-start
  20.8 14.9 %all-to-all-done = bf16[16,8,2176]{2,1,0:T(8,128)(2,1)S(1)} async-done(((bf16[16,8,2176]{2,1,0:T(8,128)(2,1)}), bf16[16,8,2176]{2,1,0:T(8,128)(2,1)S(1)}, u32[]{:S(2)}, u32[]{:S(2)}) %all-to-all-start) | async-done | bytes 557088 | tf_op jit(solution)/shard_map/all_to_all | solution.py:590
  54.0 6.5 shard_map.400
  85.7 9.1 collective-permute-done.6
  94.7 10.2 collective-permute-done.7
  108.7 9.8 collective-permute-start
  118.6 6.0 collective-permute-done
  127.8 8.8 all-to-all-done.1
  139.2 10.6 copy.333
  196.3 5.8 collective-permute-done.14
  218.7 5.1 all-to-all-start.2
  232.0 20.9 %shard_map.401 = (bf16[1024,256]{1,0:T(8,128)(2,1)S(1)}, f32[1024,256]{1,0:T(8,128)S(1)}, f32[128,16,2,8,128]{4,3,2,1,0:T(8,128)}) custom-call(f32[1024,256]{1,0:T(8,128)S(1)} %bitcast_convert_fusion.1.mixer_ref, f32[1024,256]{1,0:T(8,128)S(1)} %copy.391.gate_ref, bf16[1024,128]{1,0:T(8,128)(2,1)S(1)} %fusion.21.low_ref, ...), custom_call_target="tpu_custom_call" | custom-call | flops 33554432 | bytes 16777216 | tf_op jit(solution)/shard_map/pallas_call | solution.py:106
  267.7 6.9 collective-permute-done.25
  278.7 5.8 collective-permute-done.22
  296.8 6.7 collective-permute-done.27
  306.4 13.1 collective-permute-done.31
  323.9 5.5 collective-permute-done.32
  357.3 17.0 %all-gather.17.cloned.1.call-done = bf16[2048,512]{1,0:T(8,128)(2,1)} async-done(((bf16[1024,512]{1,0:T(8,128)(2,1)}), bf16[2048,512]{1,0:T(8,128)(2,1)}) %all-gather.17.cloned.1.call-update) | async-done | bytes 2097168 | tf_op jit(solution)/shard_map/all_gather | solution.py:404
  384.7 6.9 collective-permute-done.41
  395.7 5.7 collective-permute-done.38
  417.0 7.6 collective-permute-done.43
  430.5 5.6 shard_map.403
  444.8 4.7 collective-permute-start.80
  459.0 7.7 collective-permute-done.48
  503.5 36.0 %all-gather.19.cloned.1.call-done = bf16[2048,512]{1,0:T(8,128)(2,1)} async-done(((bf16[1024,512]{1,0:T(8,128)(2,1)}), bf16[2048,512]{1,0:T(8,128)(2,1)}) %all-gather.19.cloned.1.call-update) | async-done | bytes 2097168 | tf_op jit(solution)/shard_map/all_gather | solution.py:404
  570.7 5.5 collective-permute-done.57
  583.0 4.9 collective-permute-done.54
  602.4 7.1 collective-permute-done.59
  616.1 8.2 collective-permute-done.63
  628.8 5.5 collective-permute-done.64
  665.9 6.1 fusion.98
  672.0 14.0 %all-gather.25.cloned.1.call-done = bf16[2048,512]{1,0:T(8,128)(2,1)} async-done(((bf16[1024,512]{1,0:T(8,128)(2,1)}), bf16[2048,512]{1,0:T(8,128)(2,1)}) %all-gather.25.cloned.1.call-update) | async-done | bytes 2097168 | tf_op jit(solution)/shard_map/all_gather | solution.py:404
  686.0 7.3 multiply_convert_fusion.3
  693.3 5.0 convolution_convert_fusion.7
  748.0 6.9 collective-permute-done.75
  759.3 9.4 collective-permute-done.96
  772.4 7.0 collective-permute-done.97
  808.6 7.9 collective-permute-done.106
  819.6 6.8 collective-permute-done.103
  838.8 5.5 collective-permute-done.108
  847.1 5.9 convolution_convert_fusion.9
  853.1 6.4 collective-permute-done.112
  864.5 5.6 collective-permute-done.113
  881.1 7.6 convolution_convert_fusion.5
  892.1 6.7 multiply_convert_fusion.1
  898.8 5.3 convolution_convert_fusion.6
  909.6 7.8 collective-permute-done.122
  934.3 5.0 collective-permute-done.118
  939.8 6.2 collective-permute-done.124
  953.1 7.0 collective-permute-done.128
  965.0 5.7 collective-permute-done.129
  1000.8 9.4 convolution_convert_fusion.4
  1010.2 42.8 %shard_map.404 = (bf16[1024,256]{1,0:T(8,128)(2,1)}, f32[1024,256]{1,0:T(8,128)}, bf16[1024,256]{1,0:T(8,128)(2,1)}, f32[1024,128]{1,0:T(8,128)}, f32[16,256]{1,0:T(8,128)}, /*index=5*/f32[1,256]{1,0:T(1,128)}) custom-call(f32[1024,256]{1,0:T(8,128)} %copy-done.3, f32[1024,256]{1,0:T(8,128)} %copy-done.2, f32[1024,256]{1,0:T(8,128)} %copy-done.10, ...), custom_call_target="tpu_custom_call" | custom-call | flops 83886080 | bytes 16777216 | tf_op jit(solution)/shard_map/pallas_call | solution.py:255
  1056.4 14.0 %all-to-all-done.6.packed_ref = bf16[8,128,1536]{2,1,0:T(8,128)(2,1)S(1)} async-done(((bf16[8,128,1536]{2,1,0:T(8,128)(2,1)}), bf16[8,128,1536]{2,1,0:T(8,128)(2,1)S(1)}, u32[]{:S(2)}, u32[]{:S(2)}) %all-to-all-start.6) | async-done | bytes 3145760 | tf_op jit(solution)/shard_map/all_to_all | solution.py:414
  1092.7 5.9 collective-permute-done.138
  1119.7 4.6 all-to-all-start.7
  1141.9 5.7 all-to-all-done.7.packed_ref
  1168.4 4.6 convolution_convert_fusion.11
  1192.5 19.7 %collective-permute-done.149 = bf16[64,2048]{1,0:T(8,128)(2,1)S(1)} collective-permute-done((bf16[64,2048]{1,0:T(8,128)(2,1)S(1)}, bf16[64,2048]{1,0:T(8,128)(2,1)S(1)}, u32[]{:S(2)}, u32[]{:S(2)}) %collective-permute-start.149) | collective-permute-done | bytes 262176 | tf_op jit(solution)/shard_map/ppermute | solution.py:308
  1217.9 5.4 collective-permute-done.146
  1231.7 17.1 %collective-permute-start.151 = (bf16[64,2048]{1,0:T(8,128)(2,1)}, bf16[64,2048]{1,0:T(8,128)(2,1)}, u32[]{:S(2)}, u32[]{:S(2)}) collective-permute-start(bf16[64,2048]{1,0:T(8,128)(2,1)} %get-tuple-element.237), channel_id=1, source_target_pairs={{0,16},{2,18},{4,20},{6,22},{8,24},{10,26},{12,28},{14,30},{16,0},... | collective-permute-start | bytes 786440 | tf_op jit(solution)/shard_map/ppermute | solution.py:308
  1254.4 13.3 collective-permute-done.151
  1313.3 5.8 shard_map.407
  1321.2 7.0 shard_map.406
  (1011 shorter events, 741.9 us)
Async XLA Ops:
  13.3 22.4 %all-to-all-start = ((bf16[16,8,2176]{2,1,0:T(8,128)(2,1)}), bf16[16,8,2176]{2,1,0:T(8,128)(2,1)S(1)}, u32[]{:S(2)}, u32[]{:S(2)}) async-start(bf16[16,8,2176]{2,1,0:T(8,128)(2,1)} %pad_maximum_fusion.11), calls=%async_computation | async-start | bytes 1114112 | tf_op jit(solution)/shard_map/all_to_all | solution.py:590
  50.1 15.8 %collective-permute-start.4 = (bf16[64,2048]{1,0:T(8,128)(2,1)}, bf16[64,2048]{1,0:T(8,128)(2,1)S(1)}, u32[]{:S(2)}, u32[]{:S(2)}) collective-permute-start(bf16[64,2048]{1,0:T(8,128)(2,1)} %multiply_convert_fusion.11), channel_id=1, source_target_pairs={{0,16},{2,18},{4,20},{6,22},{8,24},{10,26},{12,28},{14,30},{16,0},... | collective-permute-start | bytes 786440 | tf_op jit(solution)/shard_map/ppermute | solution.py:308
  52.5 15.9 %collective-permute-start.2 = (bf16[64,2048]{1,0:T(8,128)(2,1)}, bf16[64,2048]{1,0:T(8,128)(2,1)}, u32[]{:S(2)}, u32[]{:S(2)}) collective-permute-start(bf16[64,2048]{1,0:T(8,128)(2,1)} %multiply_convert_fusion.11), channel_id=1, source_target_pairs={{0,4},{2,6},{4,0},{6,2},{8,12},{10,14},{12,8},{14,10},{16,20},{18,... | collective-permute-start | bytes 786440 | tf_op jit(solution)/shard_map/ppermute | solution.py:308
  52.5 17.4 %collective-permute-start.1 = (bf16[64,2048]{1,0:T(8,128)(2,1)}, bf16[64,2048]{1,0:T(8,128)(2,1)}, u32[]{:S(2)}, u32[]{:S(2)}) collective-permute-start(bf16[64,2048]{1,0:T(8,128)(2,1)} %multiply_convert_fusion.11), channel_id=1, source_target_pairs={{0,1},{1,0},{2,3},{3,2},{4,5},{5,4},{6,7},{7,6},{8,9},{9,8},{10,11... | collective-permute-start | bytes 786440 | tf_op jit(solution)/shard_map/ppermute | solution.py:305
  60.4 76.1 %all-to-all-start.1 = ((bf16[8,128,1536]{2,1,0:T(8,128)(2,1)}), bf16[8,128,1536]{2,1,0:T(8,128)(2,1)}, u32[]{:S(2)}, u32[]{:S(2)}) async-start(bf16[8,128,1536]{2,1,0:T(8,128)(2,1)} %shard_map.400), calls=%async_computation.1 | async-start | bytes 6291456 | tf_op jit(solution)/shard_map/all_to_all | solution.py:414
  65.0 60.9 %all-gather.27.cloned.1.call-start = ((), (), s32[]{:S(2)}) async-start(), calls=%async_computation.32 | async-start | bytes 3145728 | tf_op jit(solution)/shard_map/all_gather | solution.py:404
  65.8 108.2 %all-gather.11.cloned.1.call-start = ((), (), s32[]{:S(2)}) async-start(), calls=%async_computation.17 | async-start | bytes 3145728 | tf_op jit(solution)/shard_map/all_gather | solution.py:404
  65.8 28.9 %collective-permute-start.6 = (bf16[64,2048]{1,0:T(8,128)(2,1)S(1)}, bf16[64,2048]{1,0:T(8,128)(2,1)S(1)}, u32[]{:S(2)}, u32[]{:S(2)}) collective-permute-start(bf16[64,2048]{1,0:T(8,128)(2,1)S(1)} %collective-permute-done.4), channel_id=1, source_target_pairs={{0,4},{2,6},{4,0},{6,2},{8,12},{10,14},{12,8},{14,10},{16,20},{18,... | collective-permute-start | bytes 786440 | tf_op jit(solution)/shard_map/ppermute | solution.py:308
  77.1 27.8 %collective-permute-start.7 = (bf16[64,2048]{1,0:T(8,128)(2,1)S(1)}, bf16[64,2048]{1,0:T(8,128)(2,1)S(1)}, u32[]{:S(2)}, u32[]{:S(2)}) collective-permute-start(bf16[64,2048]{1,0:T(8,128)(2,1)S(1)} %collective-permute-done.5), channel_id=1, source_target_pairs={{0,4},{2,6},{4,0},{6,2},{8,12},{10,14},{12,8},{14,10},{16,20},{18,... | collective-permute-start | bytes 786440 | tf_op jit(solution)/shard_map/ppermute | solution.py:308
  106.5 47.8 %collective-permute-start.8 = (bf16[512,2048]{1,0:T(8,128)(2,1)}, bf16[512,2048]{1,0:T(8,128)(2,1)}, u32[]{:S(2)}, u32[]{:S(2)}) collective-permute-start(bf16[512,2048]{1,0:T(8,128)(2,1)} %get-tuple-element.429), channel_id=1, source_target_pairs={{0,2},{2,0},{4,6},{6,4},{8,10},{10,8},{12,14},{14,12},{16,18},{18,... | collective-permute-start | bytes 6291464 | tf_op jit(solution)/shard_map/ppermute | solution.py:308
  108.7 15.9 %collective-permute-start = (bf16[311,128]{1,0:T(8,128)(2,1)S(1)}, bf16[311,128]{1,0:T(8,128)(2,1)S(1)}, u32[]{:S(2)}, u32[]{:S(2)}) collective-permute-start(bf16[311,128]{1,0:T(8,128)(2,1)S(1)} %concatenate.163), channel_id=1, source_target_pairs={{0,8},{2,10},{4,12},{6,14},{8,0},{10,2},{12,4},{14,6},{16,24},{18,... | collective-permute-start | bytes 238856 | tf_op jit(solution)/shard_map/ppermute | solution.py:308
  138.8 85.3 %all-gather.13.cloned.1.call-start = ((), (), s32[]{:S(2)}) async-start(), calls=%async_computation.18 | async-start | bytes 3145728 | tf_op jit(solution)/shard_map/all_gather | solution.py:404
  218.7 36.1 %all-to-all-start.2 = ((bf16[8,128,512]{2,1,0:T(8,128)(2,1)}), bf16[8,128,512]{2,1,0:T(8,128)(2,1)}, u32[]{:S(2)}, u32[]{:S(2)}) async-start(bf16[8,128,512]{2,1,0:T(8,128)(2,1)} %broadcast_add_fusion.3), calls=%async_computation.2 | async-start | bytes 2097152 | tf_op jit(solution)/shard_map/all_to_all | solution.py:414
  223.8 35.2 %all-gather.15.cloned.1.call-start = ((), (), s32[]{:S(2)}) async-start(), calls=%async_computation.19 | async-start | bytes 1572864 | tf_op jit(solution)/shard_map/all_gather | solution.py:404
  226.9 147.5 %all-gather.17.cloned.1.call-start = ((), (), s32[]{:S(2)}) async-start(), calls=%async_computation.20 | async-start | bytes 3145728 | tf_op jit(solution)/shard_map/all_gather | solution.py:404
  305.9 16.3 %collective-permute-start.28 = (bf16[64,2048]{1,0:T(8,128)(2,1)S(1)}, bf16[64,2048]{1,0:T(8,128)(2,1)S(1)}, u32[]{:S(2)}, u32[]{:S(2)}) collective-permute-start(bf16[64,2048]{1,0:T(8,128)(2,1)S(1)} %multiply_convert_fusion.10), channel_id=1, source_target_pairs={{0,1},{1,0},{2,3},{3,2},{4,5},{5,4},{6,7},{7,6},{8,9},{9,8},{10,11... | collective-permute-start | bytes 786440 | tf_op jit(solution)/shard_map/ppermute | solution.py:305
  319.6 17.3 %collective-permute-start.33 = (bf16[64,2048]{1,0:T(8,128)(2,1)S(1)}, bf16[64,2048]{1,0:T(8,128)(2,1)S(1)}, u32[]{:S(2)}, u32[]{:S(2)}) collective-permute-start(bf16[64,2048]{1,0:T(8,128)(2,1)S(1)} %collective-permute-done.31), channel_id=1, source_target_pairs={{0,4},{2,6},{4,0},{6,2},{8,12},{10,14},{12,8},{14,10},{16,20},{18,... | collective-permute-start | bytes 786440 | tf_op jit(solution)/shard_map/ppermute | solution.py:308
  412.6 23.6 %all-to-all-start.5 = ((bf16[16,8,2048]{2,1,0:T(8,128)(2,1)}), bf16[16,8,2048]{2,1,0:T(8,128)(2,1)}, u32[]{:S(2)}, u32[]{:S(2)}) async-start(bf16[16,8,2048]{2,1,0:T(8,128)(2,1)} %fusion.5), calls=%async_computation.5 | async-start | bytes 1048576 | tf_op jit(solution)/shard_map/all_to_all | solution.py:704
  416.8 122.6 %all-gather.19.cloned.1.call-start = ((), (), s32[]{:S(2)}) async-start(), calls=%async_computation.21 | async-start | bytes 3145728 | tf_op jit(solution)/shard_map/all_gather | solution.py:404
  427.1 24.4 %collective-permute-start.47 = (bf16[64,2048]{1,0:T(8,128)(2,1)}, bf16[64,2048]{1,0:T(8,128)(2,1)}, u32[]{:S(2)}, u32[]{:S(2)}) collective-permute-start(bf16[64,2048]{1,0:T(8,128)(2,1)} %multiply_convert_fusion.9), channel_id=1, source_target_pairs={{0,16},{2,18},{4,20},{6,22},{8,24},{10,26},{12,28},{14,30},{16,0},... | collective-permute-start | bytes 786440 | tf_op jit(solution)/shard_map/ppermute | solution.py:308
  427.1 25.9 %collective-permute-start.45 = (bf16[64,2048]{1,0:T(8,128)(2,1)}, bf16[64,2048]{1,0:T(8,128)(2,1)}, u32[]{:S(2)}, u32[]{:S(2)}) collective-permute-start(bf16[64,2048]{1,0:T(8,128)(2,1)} %multiply_convert_fusion.9), channel_id=1, source_target_pairs={{0,4},{2,6},{4,0},{6,2},{8,12},{10,14},{12,8},{14,10},{16,20},{18,... | collective-permute-start | bytes 786440 | tf_op jit(solution)/shard_map/ppermute | solution.py:308
  427.1 26.5 %collective-permute-start.44 = (bf16[64,2048]{1,0:T(8,128)(2,1)}, bf16[64,2048]{1,0:T(8,128)(2,1)}, u32[]{:S(2)}, u32[]{:S(2)}) collective-permute-start(bf16[64,2048]{1,0:T(8,128)(2,1)} %multiply_convert_fusion.9), channel_id=1, source_target_pairs={{0,1},{1,0},{2,3},{3,2},{4,5},{5,4},{6,7},{7,6},{8,9},{9,8},{10,11... | collective-permute-start | bytes 786440 | tf_op jit(solution)/shard_map/ppermute | solution.py:305
  444.8 50.7 %collective-permute-start.80 = (bf16[64,2048]{1,0:T(8,128)(2,1)}, bf16[64,2048]{1,0:T(8,128)(2,1)}, u32[]{:S(2)}, u32[]{:S(2)}) collective-permute-start(bf16[64,2048]{1,0:T(8,128)(2,1)} %convert_element_type.1490), channel_id=1, source_target_pairs={{0,16},{2,18},{4,20},{6,22},{8,24},{10,26},{12,28},{14,30},{16,0},... | collective-permute-start | bytes 786440 | tf_op jit(solution)/shard_map/ppermute | solution.py:308
  449.4 48.7 %collective-permute-start.78 = (bf16[64,2048]{1,0:T(8,128)(2,1)}, bf16[64,2048]{1,0:T(8,128)(2,1)}, u32[]{:S(2)}, u32[]{:S(2)}) collective-permute-start(bf16[64,2048]{1,0:T(8,128)(2,1)} %convert_element_type.1490), channel_id=1, source_target_pairs={{0,4},{2,6},{4,0},{6,2},{8,12},{10,14},{12,8},{14,10},{16,20},{18,... | collective-permute-start | bytes 786440 | tf_op jit(solution)/shard_map/ppermute | solution.py:308
  451.5 47.9 %collective-permute-start.77 = (bf16[64,2048]{1,0:T(8,128)(2,1)}, bf16[64,2048]{1,0:T(8,128)(2,1)S(1)}, u32[]{:S(2)}, u32[]{:S(2)}) collective-permute-start(bf16[64,2048]{1,0:T(8,128)(2,1)} %convert_element_type.1490), channel_id=1, source_target_pairs={{0,1},{1,0},{2,3},{3,2},{4,5},{5,4},{6,7},{7,6},{8,9},{9,8},{10,11... | collective-permute-start | bytes 786440 | tf_op jit(solution)/shard_map/ppermute | solution.py:305
  453.6 17.0 %collective-permute-start.46 = (bf16[64,2048]{1,0:T(8,128)(2,1)}, bf16[64,2048]{1,0:T(8,128)(2,1)S(1)}, u32[]{:S(2)}, u32[]{:S(2)}) collective-permute-start(bf16[64,2048]{1,0:T(8,128)(2,1)} %collective-permute-done.45), channel_id=1, source_target_pairs={{0,1},{1,0},{2,3},{3,2},{4,5},{5,4},{6,7},{7,6},{8,9},{9,8},{10,11... | collective-permute-start | bytes 786440 | tf_op jit(solution)/shard_map/ppermute | solution.py:305
  482.4 17.9 %collective-permute-start.51 = (bf16[512,2048]{1,0:T(8,128)(2,1)}, bf16[512,2048]{1,0:T(8,128)(2,1)}, u32[]{:S(2)}, u32[]{:S(2)}) collective-permute-start(bf16[512,2048]{1,0:T(8,128)(2,1)} %get-tuple-element.393), channel_id=1, source_target_pairs={{0,2},{2,0},{4,6},{6,4},{8,10},{10,8},{12,14},{14,12},{16,18},{18,... | collective-permute-start | bytes 6291464 | tf_op jit(solution)/shard_map/ppermute | solution.py:308
  488.4 76.2 %all-to-all-start.3 = ((bf16[8,128,1536]{2,1,0:T(8,128)(2,1)}), bf16[8,128,1536]{2,1,0:T(8,128)(2,1)}, u32[]{:S(2)}, u32[]{:S(2)}) async-start(bf16[8,128,1536]{2,1,0:T(8,128)(2,1)} %broadcast_add_fusion), calls=%async_computation.3 | async-start | bytes 6291456 | tf_op jit(solution)/shard_map/all_to_all | solution.py:414
  493.1 107.0 %all-gather.21.cloned.1.call-start = ((), (), s32[]{:S(2)}) async-start(), calls=%async_computation.22 | async-start | bytes 3145728 | tf_op jit(solution)/shard_map/all_gather | solution.py:404
  495.5 86.6 %collective-permute-start.82 = (bf16[64,2048]{1,0:T(8,128)(2,1)}, bf16[64,2048]{1,0:T(8,128)(2,1)S(1)}, u32[]{:S(2)}, u32[]{:S(2)}) collective-permute-start(bf16[64,2048]{1,0:T(8,128)(2,1)} %collective-permute-done.80), channel_id=1, source_target_pairs={{0,4},{2,6},{4,0},{6,2},{8,12},{10,14},{12,8},{14,10},{16,20},{18,... | collective-permute-start | bytes 786440 | tf_op jit(solution)/shard_map/ppermute | solution.py:308
  497.4 58.7 %collective-permute-start.81 = (bf16[64,2048]{1,0:T(8,128)(2,1)}, bf16[64,2048]{1,0:T(8,128)(2,1)S(1)}, u32[]{:S(2)}, u32[]{:S(2)}) collective-permute-start(bf16[64,2048]{1,0:T(8,128)(2,1)} %collective-permute-done.80), channel_id=1, source_target_pairs={{0,1},{1,0},{2,3},{3,2},{4,5},{5,4},{6,7},{7,6},{8,9},{9,8},{10,11... | collective-permute-start | bytes 786440 | tf_op jit(solution)/shard_map/ppermute | solution.py:305
  498.2 59.4 %collective-permute-start.79 = (bf16[64,2048]{1,0:T(8,128)(2,1)}, bf16[64,2048]{1,0:T(8,128)(2,1)S(1)}, u32[]{:S(2)}, u32[]{:S(2)}) collective-permute-start(bf16[64,2048]{1,0:T(8,128)(2,1)} %collective-permute-done.78), channel_id=1, source_target_pairs={{0,1},{1,0},{2,3},{3,2},{4,5},{5,4},{6,7},{7,6},{8,9},{9,8},{10,11... | collective-permute-start | bytes 786440 | tf_op jit(solution)/shard_map/ppermute | solution.py:305
  556.1 26.1 %collective-permute-start.83 = (bf16[64,2048]{1,0:T(8,128)(2,1)S(1)}, bf16[64,2048]{1,0:T(8,128)(2,1)S(1)}, u32[]{:S(2)}, u32[]{:S(2)}) collective-permute-start(bf16[64,2048]{1,0:T(8,128)(2,1)S(1)} %collective-permute-done.81), channel_id=1, source_target_pairs={{0,4},{2,6},{4,0},{6,2},{8,12},{10,14},{12,8},{14,10},{16,20},{18,... | collective-permute-start | bytes 786440 | tf_op jit(solution)/shard_map/ppermute | solution.py:308
  566.9 81.7 %all-gather.23.cloned.1.call-start = ((), (), s32[]{:S(2)}) async-start(), calls=%async_computation.23 | async-start | bytes 3145728 | tf_op jit(solution)/shard_map/all_gather | solution.py:404
  600.0 53.2 %collective-permute-start.84 = (bf16[512,2048]{1,0:T(8,128)(2,1)}, bf16[512,2048]{1,0:T(8,128)(2,1)}, u32[]{:S(2)}, u32[]{:S(2)}) collective-permute-start(bf16[512,2048]{1,0:T(8,128)(2,1)} %get-tuple-element.359), channel_id=1, source_target_pairs={{0,2},{2,0},{4,6},{6,4},{8,10},{10,8},{12,14},{14,12},{16,18},{18,... | collective-permute-start | bytes 6291464 | tf_op jit(solution)/shard_map/ppermute | solution.py:308
  616.1 69.9 %all-gather.25.cloned.1.call-start = ((), (), s32[]{:S(2)}) async-start(), calls=%async_computation.24 | async-start | bytes 3145728 | tf_op jit(solution)/shard_map/all_gather | solution.py:404
  624.3 16.9 %collective-permute-start.65 = (bf16[64,2048]{1,0:T(8,128)(2,1)S(1)}, bf16[64,2048]{1,0:T(8,128)(2,1)S(1)}, u32[]{:S(2)}, u32[]{:S(2)}) collective-permute-start(bf16[64,2048]{1,0:T(8,128)(2,1)S(1)} %collective-permute-done.63), channel_id=1, source_target_pairs={{0,4},{2,6},{4,0},{6,2},{8,12},{10,14},{12,8},{14,10},{16,20},{18,... | collective-permute-start | bytes 786440 | tf_op jit(solution)/shard_map/ppermute | solution.py:308
  652.7 339.9 %reduce-scatter.10.cloned.1.call-start = ((), (), s32[]{:S(2)}) async-start(), calls=%async_computation.26 | async-start | bytes 3145728 | tf_op jit(solution)/shard_map/reduce_scatter | solution.py:408
  719.8 15.8 %collective-permute-start.72 = (bf16[64,2048]{1,0:T(8,128)(2,1)S(1)}, bf16[64,2048]{1,0:T(8,128)(2,1)S(1)}, u32[]{:S(2)}, u32[]{:S(2)}) collective-permute-start(bf16[64,2048]{1,0:T(8,128)(2,1)S(1)} %get-tuple-element.267), channel_id=1, source_target_pairs={{0,4},{2,6},{4,0},{6,2},{8,12},{10,14},{12,8},{14,10},{16,20},{18,... | collective-permute-start | bytes 786440 | tf_op jit(solution)/shard_map/ppermute | solution.py:308
  722.0 16.9 %collective-permute-start.74 = (bf16[64,2048]{1,0:T(8,128)(2,1)S(1)}, bf16[64,2048]{1,0:T(8,128)(2,1)S(1)}, u32[]{:S(2)}, u32[]{:S(2)}) collective-permute-start(bf16[64,2048]{1,0:T(8,128)(2,1)S(1)} %get-tuple-element.268), channel_id=1, source_target_pairs={{0,1},{1,0},{2,3},{3,2},{4,5},{5,4},{6,7},{7,6},{8,9},{9,8},{10,11... | collective-permute-start | bytes 786440 | tf_op jit(solution)/shard_map/ppermute | solution.py:305
  728.3 16.2 %collective-permute-start.86 = (bf16[64,2048]{1,0:T(8,128)(2,1)S(1)}, bf16[64,2048]{1,0:T(8,128)(2,1)S(1)}, u32[]{:S(2)}, u32[]{:S(2)}) collective-permute-start(bf16[64,2048]{1,0:T(8,128)(2,1)S(1)} %get-tuple-element.255), channel_id=1, source_target_pairs={{0,1},{1,0},{2,3},{3,2},{4,5},{5,4},{6,7},{7,6},{8,9},{9,8},{10,11... | collective-permute-start | bytes 786440 | tf_op jit(solution)/shard_map/ppermute | solution.py:305
  729.8 17.1 %collective-permute-start.88 = (bf16[64,2048]{1,0:T(8,128)(2,1)S(1)}, bf16[64,2048]{1,0:T(8,128)(2,1)S(1)}, u32[]{:S(2)}, u32[]{:S(2)}) collective-permute-start(bf16[64,2048]{1,0:T(8,128)(2,1)S(1)} %get-tuple-element.256), channel_id=1, source_target_pairs={{0,4},{2,6},{4,0},{6,2},{8,12},{10,14},{12,8},{14,10},{16,20},{18,... | collective-permute-start | bytes 786440 | tf_op jit(solution)/shard_map/ppermute | solution.py:308
  845.0 16.5 %collective-permute-start.110 = (bf16[64,2048]{1,0:T(8,128)(2,1)S(1)}, bf16[64,2048]{1,0:T(8,128)(2,1)S(1)}, u32[]{:S(2)}, u32[]{:S(2)}) collective-permute-start(bf16[64,2048]{1,0:T(8,128)(2,1)S(1)} %get-tuple-element.221), channel_id=1, source_target_pairs={{0,4},{2,6},{4,0},{6,2},{8,12},{10,14},{12,8},{14,10},{16,20},{18,... | collective-permute-start | bytes 786440 | tf_op jit(solution)/shard_map/ppermute | solution.py:308
  846.5 16.5 %collective-permute-start.109 = (bf16[64,2048]{1,0:T(8,128)(2,1)S(1)}, bf16[64,2048]{1,0:T(8,128)(2,1)S(1)}, u32[]{:S(2)}, u32[]{:S(2)}) collective-permute-start(bf16[64,2048]{1,0:T(8,128)(2,1)S(1)} %get-tuple-element.221), channel_id=1, source_target_pairs={{0,1},{1,0},{2,3},{3,2},{4,5},{5,4},{6,7},{7,6},{8,9},{9,8},{10,11... | collective-permute-start | bytes 786440 | tf_op jit(solution)/shard_map/ppermute | solution.py:305
  853.0 139.6 %reduce-scatter.8.cloned.1.call-start = ((), (), s32[]{:S(2)}) async-start(), calls=%async_computation.25 | async-start | bytes 6291456 | tf_op jit(solution)/shard_map/reduce_scatter | solution.py:408
  859.5 18.1 %collective-permute-start.114 = (bf16[64,2048]{1,0:T(8,128)(2,1)S(1)}, bf16[64,2048]{1,0:T(8,128)(2,1)S(1)}, u32[]{:S(2)}, u32[]{:S(2)}) collective-permute-start(bf16[64,2048]{1,0:T(8,128)(2,1)S(1)} %collective-permute-done.112), channel_id=1, source_target_pairs={{0,4},{2,6},{4,0},{6,2},{8,12},{10,14},{12,8},{14,10},{16,20},{18,... | collective-permute-start | bytes 786440 | tf_op jit(solution)/shard_map/ppermute | solution.py:308
  888.7 226.4 %reduce-scatter.12.cloned.1.call-start = ((), (), s32[]{:S(2)}) async-start(), calls=%async_computation.27 | async-start | bytes 3145728 | tf_op jit(solution)/shard_map/reduce_scatter | solution.py:408
  952.9 223.3 %reduce-scatter.20.cloned.1.call-start = ((), (), s32[]{:S(2)}) async-start(), calls=%async_computation.31 | async-start | bytes 3145728 | tf_op jit(solution)/shard_map/reduce_scatter | solution.py:408
  960.1 17.5 %collective-permute-start.130 = (bf16[64,2048]{1,0:T(8,128)(2,1)S(1)}, bf16[64,2048]{1,0:T(8,128)(2,1)S(1)}, u32[]{:S(2)}, u32[]{:S(2)}) collective-permute-start(bf16[64,2048]{1,0:T(8,128)(2,1)S(1)} %collective-permute-done.128), channel_id=1, source_target_pairs={{0,4},{2,6},{4,0},{6,2},{8,12},{10,14},{12,8},{14,10},{16,20},{18,... | collective-permute-start | bytes 786440 | tf_op jit(solution)/shard_map/ppermute | solution.py:308
  996.9 73.6 %all-to-all-start.6 = ((bf16[8,128,1536]{2,1,0:T(8,128)(2,1)}), bf16[8,128,1536]{2,1,0:T(8,128)(2,1)S(1)}, u32[]{:S(2)}, u32[]{:S(2)}) async-start(bf16[8,128,1536]{2,1,0:T(8,128)(2,1)} %maximum_add_fusion), calls=%async_computation.8 | async-start | bytes 6291456 | tf_op jit(solution)/shard_map/all_to_all | solution.py:414
  1000.5 175.7 %reduce-scatter.18.cloned.1.call-start = ((), (), s32[]{:S(2)}) async-start(), calls=%async_computation.30 | async-start | bytes 6291456 | tf_op jit(solution)/shard_map/reduce_scatter | solution.py:408
  1106.8 18.0 %collective-permute-start.76 = (bf16[64,2048]{1,0:T(8,128)(2,1)}, bf16[64,2048]{1,0:T(8,128)(2,1)}, u32[]{:S(2)}, u32[]{:S(2)}) collective-permute-start(bf16[64,2048]{1,0:T(8,128)(2,1)} %get-tuple-element.358), channel_id=1, source_target_pairs={{0,1},{1,0},{2,3},{3,2},{4,5},{5,4},{6,7},{7,6},{8,9},{9,8},{10,11... | collective-permute-start | bytes 786440 | tf_op jit(solution)/shard_map/ppermute | solution.py:305
  1119.7 28.0 %all-to-all-start.7 = ((bf16[8,128,512]{2,1,0:T(8,128)(2,1)}), bf16[8,128,512]{2,1,0:T(8,128)(2,1)}, u32[]{:S(2)}, u32[]{:S(2)}) async-start(bf16[8,128,512]{2,1,0:T(8,128)(2,1)} %bitcast.311), calls=%async_computation.10 | async-start | bytes 2097152 | tf_op jit(solution)/shard_map/all_to_all | solution.py:414
  1147.6 18.7 %all-to-all-start.4 = ((bf16[16,8,2048]{2,1,0:T(8,128)(2,1)}), bf16[16,8,2048]{2,1,0:T(8,128)(2,1)}, u32[]{:S(2)}, u32[]{:S(2)}) async-start(bf16[16,8,2048]{2,1,0:T(8,128)(2,1)} %fusion.4), calls=%async_computation.4 | async-start | bytes 1048576 | tf_op jit(solution)/shard_map/all_to_all | solution.py:811
  1151.9 144.4 %reduce-scatter.16.cloned.1.call-start = ((), (), s32[]{:S(2)}) async-start(), calls=%async_computation.29 | async-start | bytes 1572864 | tf_op jit(solution)/shard_map/reduce_scatter | solution.py:408
  1161.6 23.8 %collective-permute-start.144 = (bf16[512,2048]{1,0:T(8,128)(2,1)}, bf16[512,2048]{1,0:T(8,128)(2,1)}, u32[]{:S(2)}, u32[]{:S(2)}) collective-permute-start(bf16[512,2048]{1,0:T(8,128)(2,1)} %slice.1336), channel_id=1, source_target_pairs={{0,2},{2,0},{4,6},{6,4},{8,10},{10,8},{12,14},{14,12},{16,18},{18,... | collective-permute-start | bytes 6291464 | tf_op jit(solution)/shard_map/ppermute | solution.py:308
  1180.4 101.4 %all-to-all-start.9 = ((bf16[8,128,1536]{2,1,0:T(8,128)(2,1)}), bf16[8,128,1536]{2,1,0:T(8,128)(2,1)}, u32[]{:S(2)}, u32[]{:S(2)}) async-start(bf16[8,128,1536]{2,1,0:T(8,128)(2,1)} %pad_maximum_fusion), calls=%async_computation.16 | async-start | bytes 6291456 | tf_op jit(solution)/shard_map/all_to_all | solution.py:414
  1184.8 143.3 %reduce-scatter.14.cloned.1.call-start = ((), (), s32[]{:S(2)}) async-start(), calls=%async_computation.28 | async-start | bytes 3145728 | tf_op jit(solution)/shard_map/reduce_scatter | solution.py:408
  1186.7 25.4 %collective-permute-start.149 = (bf16[64,2048]{1,0:T(8,128)(2,1)S(1)}, bf16[64,2048]{1,0:T(8,128)(2,1)S(1)}, u32[]{:S(2)}, u32[]{:S(2)}) collective-permute-start(bf16[64,2048]{1,0:T(8,128)(2,1)S(1)} %select_convert_fusion), channel_id=1, source_target_pairs={{0,4},{2,6},{4,0},{6,2},{8,12},{10,14},{12,8},{14,10},{16,20},{18,... | collective-permute-start | bytes 786440 | tf_op jit(solution)/shard_map/ppermute | solution.py:308
  1230.4 24.0 %collective-permute-start.145 = (bf16[64,2048]{1,0:T(8,128)(2,1)}, bf16[64,2048]{1,0:T(8,128)(2,1)}, u32[]{:S(2)}, u32[]{:S(2)}) collective-permute-start(bf16[64,2048]{1,0:T(8,128)(2,1)} %get-tuple-element.235), channel_id=1, source_target_pairs={{0,1},{1,0},{2,3},{3,2},{4,5},{5,4},{6,7},{7,6},{8,9},{9,8},{10,11... | collective-permute-start | bytes 786440 | tf_op jit(solution)/shard_map/ppermute | solution.py:305
  1231.1 23.3 %collective-permute-start.147 = (bf16[64,2048]{1,0:T(8,128)(2,1)}, bf16[64,2048]{1,0:T(8,128)(2,1)}, u32[]{:S(2)}, u32[]{:S(2)}) collective-permute-start(bf16[64,2048]{1,0:T(8,128)(2,1)} %get-tuple-element.236), channel_id=1, source_target_pairs={{0,4},{2,6},{4,0},{6,2},{8,12},{10,14},{12,8},{14,10},{16,20},{18,... | collective-permute-start | bytes 786440 | tf_op jit(solution)/shard_map/ppermute | solution.py:308
  1231.7 36.0 %collective-permute-start.151 = (bf16[64,2048]{1,0:T(8,128)(2,1)}, bf16[64,2048]{1,0:T(8,128)(2,1)}, u32[]{:S(2)}, u32[]{:S(2)}) collective-permute-start(bf16[64,2048]{1,0:T(8,128)(2,1)} %get-tuple-element.237), channel_id=1, source_target_pairs={{0,16},{2,18},{4,20},{6,22},{8,24},{10,26},{12,28},{14,30},{16,0},... | collective-permute-start | bytes 786440 | tf_op jit(solution)/shard_map/ppermute | solution.py:308
  1281.8 51.2 %all-to-all-start.8 = ((bf16[16,8,2176]{2,1,0:T(8,128)(2,1)}), bf16[16,8,2176]{2,1,0:T(8,128)(2,1)}, u32[]{:S(2)}, u32[]{:S(2)}) async-start(bf16[16,8,2176]{2,1,0:T(8,128)(2,1)} %pad_maximum_fusion.12), calls=%async_computation.11 | async-start | bytes 1114112 | tf_op jit(solution)/shard_map/all_to_all | solution.py:821
  1286.9 22.5 %collective-permute-start.154 = (f32[311,128]{1,0:T(8,128)}, f32[311,128]{1,0:T(8,128)}, u32[]{:S(2)}, u32[]{:S(2)}) collective-permute-start(f32[311,128]{1,0:T(8,128)} %constant_dynamic-slice_fusion), channel_id=1, source_target_pairs={{0,8},{2,10},{4,12},{6,14},{8,0},{10,2},{12,4},{14,6},{16,24},{18,... | collective-permute-start | bytes 477704 | tf_op jit(solution)/shard_map/ppermute | solution.py:308
  (270 other events, 3517.4 us)
Sparse Core Ops, SparseCore 0:
  67.4 56.2 all-gather.26
  139.0 34.9 all-gather.10
  178.1 44.0 all-gather.12
  227.0 31.9 all-gather.14
  342.8 31.4 all-gather.16
  484.8 54.5 all-gather.18
  567.0 32.3 all-gather.20
  616.2 32.3 all-gather.22
  652.8 33.1 all-gather.24
  853.2 31.3 reduce-scatter.9
  888.8 57.0 reduce-scatter.7
  953.0 30.8 reduce-scatter.11
  986.2 42.1 reduce-scatter.19
  1030.6 89.6 reduce-scatter.17
  1173.2 21.0 reduce-scatter.15
  1250.4 43.9 reduce-scatter.13
